TPU v7x, 512 devices: a whole 4x8x8 slice. The times are simulated.
512 devices in a mesh: dom: 32 (over x, y), strip: 16 (over z, core).
Axes of the slice: x: 4, y: 8, z: 8, core: 2. Of those that a mesh axis runs over, the one named last changes fastest.
Arguments:
- surface: bfloat16 [768, 512, 256], P('dom', 'strip'), may hold values from 0.5 to 2
- discharge: bfloat16 [768, 512, 256], P('dom', 'strip'), may hold values from -3 to 3
- storage: bfloat16 [768, 512, 256], P('dom', 'strip'), may hold values from 0 to 1.5
- exchange: bfloat16 [512, 256], P('strip'), may hold values from 0.049804688 to 0.29882812
- depth_perturbation: bfloat16 [2, 768, 512, 256], P(None, 'dom', 'strip'), may hold values from -1.1953125 to 1.1953125
- flow_perturbation: bfloat16 [2, 768, 512, 256], P(None, 'dom', 'strip'), may hold values from -1.1953125 to 1.1953125
- sensor_cell: int32 [512], P('strip'), may hold values from 0 to 131071, as said below
- sensor_radius: int32 [512], P('strip'), may hold values from 8 to 32
- observed: float32 [512], P('strip'), may hold values from -1 to 33
- sensor_sigma: float32 [512], P('strip'), may hold values from 0.3 to 1.5
Outputs:
- posterior_depth: float32 [512, 256], P('strip')
- posterior_flow: float32 [512, 256], P('strip')
- posterior_storage: float32 [512, 256], P('strip')
Inputs may be any that keep to these rules, and one draw needn't show every extreme that they name: `sensor_cell`: sensor k lies in strip k // 32, that is in rows (k // 32) * 32 to (k // 32 + 1) * 32 - 1.
All inputs are finite; a program needn't handle non-finite values.
Results may differ from a plain program's by a relative error of at most 0.0003.
Values may be sent and summed in bfloat16 or wider, within the bound.
No kernel may reach another device: no remote copies, remote signals or barrier semaphores. Data moves between devices by JAX's collectives and lax.ppermute only.
A program may use at most 64 MiB of HBM per device.

v0:
```python
import jax
import jax.numpy as jnp
from jax import lax
from jax.sharding import PartitionSpec as P

advection = 0.4
gravity = 0.5
diffusion = 0.15
friction = 0.3
drainage = 0.1


def from_behind(value, axis, steps):
    count = lax.axis_size(axis)
    first, last = (max(0, -steps), min(count, count - steps))
    return lax.ppermute(value, axis, [(source, source + steps) for source in range(first, last)])


def extended(cells, sides, width):
    for axis, dim in sides:
        count = lax.axis_size(axis)
        ends = count - 1
        head = lax.slice_in_dim(cells, 0, width, axis=dim)
        tail = lax.slice_in_dim(cells, cells.shape[dim] - width, cells.shape[dim], axis=dim)
        cells = jnp.concatenate(
            [
                lax.ppermute(tail, axis, [(i, (i + 1) % count) for i in range(ends)]),
                cells,
                lax.ppermute(head, axis, [((i + 1) % count, i) for i in range(ends)]),
            ],
            axis=dim,
        )
    return cells


def column_spread(field):
    left_side = jnp.concatenate([field[..., :1], field[..., :-1]], axis=-1)
    right_side = jnp.concatenate([field[..., 1:], field[..., -1:]], axis=-1)
    return left_side - 2.0 * field + right_side


def advance_depth(current_depth, current_flow, flow_below, current_storage, exchange, jitter):
    inflow = exchange * (current_depth - current_storage)
    depth_next = (
        current_depth
        - advection * (current_flow - flow_below)
        + diffusion * column_spread(current_depth)
        - inflow
        + jitter
    )
    stored_next = (1.0 - drainage) * current_storage + inflow
    return (depth_next, stored_next)


def advance_flow(current_flow, current_depth, depth_above, jitter):
    return (current_flow - gravity * (depth_above - current_depth) + jitter) / (
        1.0 + friction * jnp.abs(current_flow)
    )


def taper_table(sensor_rows, sensor_cols, sensor_reach, cell_rows, cell_cols):
    row_gap = cell_rows[None, :] - sensor_rows[:, None]
    col_gap = cell_cols[None, :] - sensor_cols[:, None]
    distance = row_gap * row_gap + col_gap * col_gap
    reach = jnp.maximum(sensor_reach * sensor_reach, 1.0)
    return jnp.maximum(1.0 - distance / reach[:, None], 0.0)


def local(
    surface,
    discharge,
    storage,
    exchange,
    depth_perturbation,
    flow_perturbation,
    sensor_cell,
    sensor_radius,
    observed,
    sensor_sigma,
):
    members = surface.shape[0]
    rows_dev = surface.shape[1]
    columns = surface.shape[2]
    horizon = depth_perturbation.shape[0]
    strip_index = lax.axis_index("strip")
    first_row = strip_index * rows_dev
    current_depth = surface.astype(jnp.float32)
    current_flow = discharge.astype(jnp.float32)
    current_storage = storage.astype(jnp.float32)
    exchange_rate = exchange.astype(jnp.float32)
    for time_step in range(horizon):
        edge_below = from_behind(current_flow[:, -1:, :], "strip", 1)
        flow_below = jnp.concatenate([edge_below, current_flow[:, :-1]], axis=1)
        current_depth, current_storage = advance_depth(
            current_depth,
            current_flow,
            flow_below,
            current_storage,
            exchange_rate,
            depth_perturbation[time_step].astype(jnp.float32),
        )
        edge_above = from_behind(current_depth[:, :1, :], "strip", -1)
        depth_above = jnp.concatenate([current_depth[:, 1:], edge_above], axis=1)
        current_flow = advance_flow(
            current_flow,
            current_depth,
            depth_above,
            flow_perturbation[time_step].astype(jnp.float32),
        )
    flat_depth = current_depth.reshape(members, rows_dev * columns)
    flat_flow = current_flow.reshape(members, rows_dev * columns)
    flat_stored = current_storage.reshape(members, rows_dev * columns)
    local_cell = sensor_cell - first_row * columns
    sampled = jnp.take(flat_depth, local_cell, axis=1)
    misfit = (sampled - observed[None, :]) / sensor_sigma[None, :]
    loglik = -0.5 * misfit * misfit
    sensor_rows = (sensor_cell // columns).astype(jnp.float32)
    sensor_cols = (sensor_cell % columns).astype(jnp.float32)
    sensor_reach = sensor_radius.astype(jnp.float32)
    packed = jnp.concatenate(
        [loglik, sensor_rows[None], sensor_cols[None], sensor_reach[None]], axis=0
    )
    beside_all = extended(packed, (("strip", 1),), packed.shape[1])
    cell_ids = jnp.arange(rows_dev * columns, dtype=jnp.int32)
    cell_rows = (cell_ids // columns + first_row).astype(jnp.float32)
    cell_cols = (cell_ids % columns).astype(jnp.float32)
    taper_rows = taper_table(
        beside_all[members], beside_all[members + 1], beside_all[members + 2], cell_rows, cell_cols
    )
    weights = jnp.dot(
        beside_all[:members],
        taper_rows,
        precision=lax.Precision.HIGHEST,
        preferred_element_type=jnp.float32,
    )
    local_peak = jnp.max(weights, axis=0)
    highest = lax.pmax(local_peak, "dom")
    highest = jnp.maximum(highest, local_peak)
    factor = jnp.exp(jnp.minimum(weights - highest[None, :], 0.0))
    total_factor, total_depth, total_flow, total_stored = lax.psum(
        (
            jnp.sum(factor, axis=0),
            jnp.sum(factor * flat_depth, axis=0),
            jnp.sum(factor * flat_flow, axis=0),
            jnp.sum(factor * flat_stored, axis=0),
        ),
        "dom",
    )
    posterior_depth = (total_depth / total_factor).reshape(rows_dev, columns)
    posterior_flow = (total_flow / total_factor).reshape(rows_dev, columns)
    posterior_storage = (total_stored / total_factor).reshape(rows_dev, columns)
    return (posterior_depth, posterior_flow, posterior_storage)


def solution(mesh):
    return jax.shard_map(
        local,
        mesh=mesh,
        in_specs=(
            P("dom", "strip", None),
            P("dom", "strip", None),
            P("dom", "strip", None),
            P("strip", None),
            P(None, "dom", "strip", None),
            P(None, "dom", "strip", None),
            P("strip"),
            P("strip"),
            P("strip"),
            P("strip"),
        ),
        out_specs=(P("strip", None), P("strip", None), P("strip", None)),
        check_vma=False,
    )
```

profile of v0, /device:TPU:8, one launch (start us, length us, event | category | flops | bytes accessed | tf_op | source)
XLA Modules:
  0.0 359.8 jit_solution(8060703788370548199)
XLA Ops:
  7.3 1.0 slice.98
  8.3 1.9 collective-permute-start
  10.1 2.4 fusion.62
  12.5 1.0 fusion.61
  13.5 0.6 compare_and_fusion
  14.1 0.6 pad_clamp_fusion
  14.7 0.1 slice.99
  14.8 0.6 convert_element_type.61
  15.4 0.1 copy.22
  15.5 0.7 copy.23
  16.2 0.7 copy.24
  16.9 0.6 copy-done.11
  17.5 2.3 multiply_add_fusion
  19.8 1.4 collective-permute-start.1
  21.2 0.3 fusion.59
  21.6 0.1 slice.104
  21.6 3.5 collective-permute-done.1
  25.2 0.3 fusion.28
  25.6 4.5 %collective-permute-start.2 = (f32[24,1,256]{2,1,0:T(1,128)S(1)}, f32[24,1,256]{2,1,0:T(1,128)S(1)}, u32[]{:S(2)}, u32[]{:S(2)}) collective-permute-start(f32[24,1,256]{2,1,0:T(1,128)S(1)} %slice.106), channel_id=1, source_target_pairs={{0,1},{1,2},{2,3},{3,4},{4,5},{5,6},{6,7},{7,8},{8,9},{9,10},{10,1... | collective-permute-start | bytes 73736 | tf_op jit(solution)/shard_map/ppermute | solution.py:16
  30.0 0.2 fusion.60
  30.2 0.7 collective-permute-done.2
  30.9 0.8 fusion.33
  31.7 0.5 copy.28
  32.2 2.6 copy.21
  34.8 2.9 gather_fusion
  37.7 0.1 multiply_multiply_fusion
  37.9 0.1 pad_maximum_fusion
  37.9 2.3 collective-permute-start.3
  40.2 1.3 collective-permute-start.4
  41.5 1.3 copy.30
  42.9 0.1 slice.113
  43.0 0.1 copy.26
  43.1 1.3 collective-permute-start.5
  44.4 0.1 copy.25
  44.4 0.5 collective-permute-done.4
  44.9 0.1 copy.27
  45.0 0.1 pad_maximum_fusion.1
  45.1 0.1 maximum_bitcast_fusion.1
  45.2 3.4 fusion.64
  48.6 138.2 %pmax.7 = f32[8192]{0:T(1024)S(1)} all-reduce(f32[8192]{0:T(1024)S(1)} %get-tuple-element.31), channel_id=1, replica_groups=mesh['dom'=32,'strip'=16] {'dom'}, use_global_device_ids=true, to_apply=%region_1.2 | all-reduce | flops 8192 | bytes 65536 | tf_op jit(solution)/shard_map/pmax | solution.py:137
  186.7 1.4 fusion.39
  188.2 0.5 copy.29
  188.7 1.1 multiply_reduce_fusion
  189.8 160.4 %all-reduce.3.cloned.1.call-done = (f32[8192]{0:T(1024)}, f32[8192]{0:T(1024)}, f32[8192]{0:T(1024)}, f32[8192]{0:T(1024)}) async-done(((f32[8192]{0:T(1024)}, f32[8192]{0:T(1024)}, f32[8192]{0:T(1024)}, f32[8192]{0:T(1024)}), (f32[8192]{0:T(1024)}, f32[8192]{0:T(1024)}, f32[8192]{0:T(1024)}, f32[8192]{0:T(1024)})) %all-reduce.3.cloned.1.call-update) | async-done | bytes 131088 | tf_op jit(solution)/shard_map/psum | solution.py:140
  350.2 0.8 fusion.63
  351.0 0.6 reshape.78
  351.7 0.6 reshape.80
  352.3 0.6 reshape.82
  (47 shorter events, 0.2 us)
Async XLA Ops:
  7.2 7.5 %copy-start.1 = (bf16[24,32,256]{2,1,0:T(8,128)(2,1)S(1)}, bf16[24,32,256]{2,1,0:T(8,128)(2,1)}, u32[]{:S(2)}) copy-start(bf16[24,32,256]{2,1,0:T(8,128)(2,1)} %param.11) | copy-start | bytes 1179652
  7.2 5.3 %copy-start = (bf16[24,32,256]{2,1,0:T(8,128)(2,1)S(1)}, bf16[24,32,256]{2,1,0:T(8,128)(2,1)}, u32[]{:S(2)}) copy-start(bf16[24,32,256]{2,1,0:T(8,128)(2,1)} %param.10) | copy-start | bytes 1179652
  7.2 6.3 %copy-start.16 = (s32[32]{0:T(128)S(1)}, s32[32]{0:T(128)}, u32[]{:S(2)}) copy-start(s32[32]{0:T(128)} %param.16) | copy-start | bytes 388
  7.2 6.9 %copy-start.17 = (s32[32]{0:T(128)S(1)}, s32[32]{0:T(128)}, u32[]{:S(2)}) copy-start(s32[32]{0:T(128)} %param.17) | copy-start | bytes 388
  7.2 343.0 %all-reduce.3.cloned.1.call-start = ((), (), s32[]{:S(2)}) async-start(), calls=%async_computation | async-start | bytes 262144 | tf_op jit(solution)/shard_map/psum | solution.py:140
  8.2 6.6 %copy-start.12 = (bf16[32,256]{1,0:T(8,128)(2,1)S(1)}, bf16[32,256]{1,0:T(8,128)(2,1)}, u32[]{:S(2)}) copy-start(bf16[32,256]{1,0:T(8,128)(2,1)} %param.13) | copy-start | bytes 49156
  8.2 9.2 %copy-start.3 = (bf16[24,32,256]{2,1,0:T(8,128)(2,1)S(1)}, bf16[24,32,256]{2,1,0:T(8,128)(2,1)}, u32[]{:S(2)}) copy-start(bf16[24,32,256]{2,1,0:T(8,128)(2,1)} %param.12) | copy-start | bytes 1179652
  8.3 8.6 %collective-permute-start = (f32[24,1,256]{2,1,0:T(1,128)S(1)}, f32[24,1,256]{2,1,0:T(1,128)S(1)}, u32[]{:S(2)}, u32[]{:S(2)}) collective-permute-start(f32[24,1,256]{2,1,0:T(1,128)S(1)} %slice.98), channel_id=1, source_target_pairs={{0,1},{1,2},{2,3},{3,4},{4,5},{5,6},{6,7},{7,8},{8,9},{9,10},{10,1... | collective-permute-start | bytes 73736 | tf_op jit(solution)/shard_map/ppermute | solution.py:16
  16.9 0.6 copy-start.11
  19.8 5.4 %copy-start.6 = (bf16[2,24,32,256]{3,2,1,0:T(8,128)(2,1)S(1)}, bf16[2,24,32,256]{3,2,1,0:T(8,128)(2,1)}, u32[]{:S(2)}) copy-start(bf16[2,24,32,256]{3,2,1,0:T(8,128)(2,1)} %param.15) | copy-start | bytes 2359300
  19.8 5.4 %collective-permute-start.1 = (f32[24,1,256]{2,1,0:T(1,128)S(1)}, f32[24,1,256]{2,1,0:T(1,128)S(1)}, u32[]{:S(2)}, u32[]{:S(2)}) collective-permute-start(f32[24,1,256]{2,1,0:T(1,128)S(1)} %slice.105), channel_id=1, source_target_pairs={{1,0},{2,1},{3,2},{4,3},{5,4},{6,5},{7,6},{8,7},{9,8},{10,9},{11,1... | collective-permute-start | bytes 73736 | tf_op jit(solution)/shard_map/ppermute | solution.py:16
  21.5 9.3 %copy-start.4 = (bf16[24,32,256]{2,1,0:T(8,128)(2,1)S(1)}, bf16[24,32,256]{2,1,0:T(8,128)(2,1)}, u32[]{:S(2)}) copy-start(bf16[24,32,256]{2,1,0:T(8,128)(2,1)} %param.12) | copy-start | bytes 1179652
  21.5 9.3 %copy-start.5 = (bf16[2,24,32,256]{3,2,1,0:T(8,128)(2,1)S(1)}, bf16[2,24,32,256]{3,2,1,0:T(8,128)(2,1)}, u32[]{:S(2)}) copy-start(bf16[2,24,32,256]{3,2,1,0:T(8,128)(2,1)} %param.14) | copy-start | bytes 2359300
  21.5 9.3 %copy-start.8 = (f32[32,256]{1,0:T(8,128)S(1)}, f32[32,256]{1,0:T(8,128)}, u32[]{:S(2)}) copy-start(f32[32,256]{1,0:T(8,128)} %convert_element_type.61) | copy-start | bytes 98308
  25.6 5.3 %collective-permute-start.2 = (f32[24,1,256]{2,1,0:T(1,128)S(1)}, f32[24,1,256]{2,1,0:T(1,128)S(1)}, u32[]{:S(2)}, u32[]{:S(2)}) collective-permute-start(f32[24,1,256]{2,1,0:T(1,128)S(1)} %slice.106), channel_id=1, source_target_pairs={{0,1},{1,2},{2,3},{3,4},{4,5},{5,6},{6,7},{7,8},{8,9},{9,10},{10,1... | collective-permute-start | bytes 73736 | tf_op jit(solution)/shard_map/ppermute | solution.py:16
  31.7 6.0 %copy-start.13 = (pred[32]{0:T(512)(128)(4,1)S(1)}, pred[32]{0:T(512)(128)(4,1)}, u32[]{:S(2)}) copy-start(pred[32]{0:T(512)(128)(4,1)} %get-tuple-element.11) | copy-start | bytes 100
  31.7 6.0 %copy-start.14 = (f32[32]{0:T(128)S(1)}, f32[32]{0:T(128)}, u32[]{:S(2)}) copy-start(f32[32]{0:T(128)} %param.19) | copy-start | bytes 388
  31.7 6.0 %copy-start.15 = (f32[32]{0:T(128)S(1)}, f32[32]{0:T(128)}, u32[]{:S(2)}) copy-start(f32[32]{0:T(128)} %param.18) | copy-start | bytes 388
  31.7 6.1 %copy-start.9 = (f32[1,32]{0,1:T(8,128)S(1)}, f32[1,32]{0,1:T(8,128)}, u32[]{:S(2)}) copy-start(f32[1,32]{0,1:T(8,128)} %copy.23) | copy-start | bytes 388
  31.7 6.1 %copy-start.10 = (f32[1,32]{0,1:T(8,128)S(1)}, f32[1,32]{0,1:T(8,128)}, u32[]{:S(2)}) copy-start(f32[1,32]{0,1:T(8,128)} %copy.24) | copy-start | bytes 388
  37.9 6.4 %collective-permute-start.3 = (f32[27,32]{0,1:T(8,128)S(1)}, f32[27,32]{0,1:T(8,128)S(1)}, u32[]{:S(2)}, u32[]{:S(2)}) collective-permute-start(f32[27,32]{0,1:T(8,128)S(1)} %pad_maximum_fusion), channel_id=1, source_target_pairs={{0,1},{1,2},{2,3},{3,4},{4,5},{5,6},{6,7},{7,8},{8,9},{9,10},{10,1... | collective-permute-start | bytes 10376 | tf_op jit(solution)/shard_map/ppermute | solution.py:27
  40.2 4.7 %collective-permute-start.4 = (f32[27,32]{0,1:T(8,128)S(1)}, f32[27,32]{0,1:T(8,128)S(1)}, u32[]{:S(2)}, u32[]{:S(2)}) collective-permute-start(f32[27,32]{0,1:T(8,128)S(1)} %pad_maximum_fusion), channel_id=1, source_target_pairs={{1,0},{2,1},{3,2},{4,3},{5,4},{6,5},{7,6},{8,7},{9,8},{10,9},{11,1... | collective-permute-start | bytes 10376 | tf_op jit(solution)/shard_map/ppermute | solution.py:29
  43.1 143.7 %collective-permute-start.5 = (f32[24,1,256]{2,1,0:T(1,128)S(1)}, f32[24,1,256]{2,1,0:T(1,128)S(1)}, u32[]{:S(2)}, u32[]{:S(2)}) collective-permute-start(f32[24,1,256]{2,1,0:T(1,128)S(1)} %slice.114), channel_id=1, source_target_pairs={{1,0},{2,1},{3,2},{4,3},{5,4},{6,5},{7,6},{8,7},{9,8},{10,9},{11,1... | collective-permute-start | bytes 73736 | tf_op jit(solution)/shard_map/ppermute | solution.py:16
  186.7 1.9 copy-start.2
  186.7 1.9 copy-start.7
Sparse Core Ops, SparseCore 0:
  190.0 160.2 all-reduce.2
where the time goes:
time: 360 us
  waiting for transfers between devices  165 us (46%)
  blocking collectives  138 us (38%)
  local copies, waits for them, and re-layouts  17.1 us (5%)
  between operations  14.4 us (4%)
  starting transfers between devices  12.6 us (4%)
  other arithmetic  9 us (2%)
    psum x1, waiting for transfers between devices, local(): lax.psum((jnp.sum(factor, axis=0), jnp.sum(factor * flat_depth, axis=0),...  160 us
    pmax x1, blocking collectives, local(): highest = lax.pmax(local_peak, 'dom')  138 us
    ppermute x4, starting transfers between devices, from_behind(): lax.ppermute(value, axis, [(source, source + steps) for source in range(f...  9.04 us
  transfers between devices with their start and end apart: 7, of which 4 were waited for; matrix products, arithmetic and copies ran while one was open for 3% of the time, Pallas kernels for 0%

commit v1 on v0

v1 whole, which is shorter than its diff:
```python
import jax
import jax.numpy as jnp
from jax import lax
from jax.experimental import pallas as pl
from jax.experimental.pallas import tpu as pltpu
from jax.sharding import PartitionSpec as P

advection = 0.4
gravity = 0.5
diffusion = 0.15
friction = 0.3
drainage = 0.1

MEMBERS = 24
ROWS = 32
COLS = 256
SENS = 32
LANES = 128
HALO = 3 * MEMBERS
MESSAGE = HALO + SENS

f32 = jnp.float32
bf16 = jnp.bfloat16


def column_spread(field):
    width = field.shape[-1]
    lane = lax.broadcasted_iota(jnp.int32, field.shape, field.ndim - 1)
    left_side = jnp.where(lane == 0, field, pltpu.roll(field, 1, field.ndim - 1))
    right_side = jnp.where(lane == width - 1, field, pltpu.roll(field, width - 1, field.ndim - 1))
    return left_side - 2.0 * field + right_side


def pack_kernel(
    cell_ref, radius_ref, surface_ref, discharge_ref, storage_ref, exchange_ref, depth_noise_ref, flow_noise_ref,
    up_ref, down_ref, first_ref, last_ref,
):
    def keep(scratch, slot, rows):
        flat = rows.reshape(MEMBERS * 8, COLS)
        scratch[slot, 0] = flat[:, :LANES]
        scratch[slot, 1] = flat[:, LANES:]

    def take(ref, lead, slot):
        head = ref[lead + (slice(None), slice(0, 16), slice(None))].astype(f32)
        tail = ref[lead + (slice(None), slice(16, 32), slice(None))].astype(f32)
        keep(first_ref, slot, head[:, :8])
        keep(last_ref, slot, tail[:, 8:])

    take(surface_ref, (), 0)
    take(discharge_ref, (), 1)
    take(storage_ref, (), 2)
    take(depth_noise_ref, (0,), 3)
    take(flow_noise_ref, (0,), 4)
    late = depth_noise_ref[1, :, 0:16, :].astype(f32)
    keep(first_ref, 5, late[:, :8])

    def row_of(ref, slot, row):
        halves = [ref[slot, half, pl.ds(row, MEMBERS, stride=8)] for half in range(2)]
        return jnp.concatenate(halves, axis=1)

    rate = exchange_ref[...].astype(f32)
    surface_0, surface_1 = row_of(first_ref, 0, 0), row_of(first_ref, 0, 1)
    flow_0, flow_1 = row_of(first_ref, 1, 0), row_of(first_ref, 1, 1)
    stored_0, stored_1 = row_of(first_ref, 2, 0), row_of(first_ref, 2, 1)
    noise_0, noise_1 = row_of(first_ref, 3, 0), row_of(first_ref, 3, 1)
    flow_noise_0, late_0 = row_of(first_ref, 4, 0), row_of(first_ref, 5, 0)
    rate_0, rate_1 = rate[0:1], rate[1:2]
    inflow_0 = rate_0 * (surface_0 - stored_0)
    partial_0 = surface_0 - advection * flow_0 + diffusion * column_spread(surface_0) - inflow_0 + noise_0
    stored_next = (1.0 - drainage) * stored_0 + inflow_0
    depth_1 = (
        surface_1 - advection * (flow_1 - flow_0) + diffusion * column_spread(surface_1)
        - rate_1 * (surface_1 - stored_1) + noise_1
    )
    inverse_0 = 1.0 / (1.0 + friction * jnp.abs(flow_0))
    flow_part = (flow_0 - gravity * depth_1 + flow_noise_0) * inverse_0
    up_ref[0:MEMBERS] = partial_0
    up_ref[MEMBERS : 2 * MEMBERS] = 1.0 - rate_0 - (advection * gravity) * inverse_0
    up_ref[2 * MEMBERS : HALO] = rate_0 * stored_next + late_0 - advection * flow_part
    surface_31, flow_30, flow_31 = row_of(last_ref, 0, 7), row_of(last_ref, 1, 6), row_of(last_ref, 1, 7)
    stored_31, noise_31, flow_noise_31 = row_of(last_ref, 2, 7), row_of(last_ref, 3, 7), row_of(last_ref, 4, 7)
    rate_31 = rate[ROWS - 1 : ROWS]
    depth_31 = (
        surface_31 - advection * (flow_31 - flow_30) + diffusion * column_spread(surface_31)
        - rate_31 * (surface_31 - stored_31) + noise_31
    )
    inverse_31 = 1.0 / (1.0 + friction * jnp.abs(flow_31))
    down_ref[0:MEMBERS] = flow_31
    down_ref[MEMBERS : 2 * MEMBERS] = (flow_31 + gravity * depth_31 + flow_noise_31) * inverse_31
    down_ref[2 * MEMBERS : HALO] = gravity * inverse_31
    lane = lax.broadcasted_iota(jnp.int32, (1, COLS), 1)
    for k in range(SENS):
        cell = cell_ref[k]
        row = ((cell >> 8) & (ROWS - 1)).astype(f32)
        column = (cell & (COLS - 1)).astype(f32)
        reach = radius_ref[k].astype(f32)
        entry = jnp.where(lane == 0, row, jnp.where(lane == 1, column, jnp.where(lane == 2, reach * reach, 1.0)))
        up_ref[HALO + k : HALO + k + 1] = entry
        down_ref[HALO + k : HALO + k + 1] = entry


def forecast_kernel(
    cell_ref, surface_ref, discharge_ref, storage_ref, exchange_ref, depth_noise_ref, flow_noise_ref,
    up_ref, down_ref, before_ref, after_ref, radius_ref, observed_ref, sigma_ref,
    depth_ref, flow_ref, stored_ref, lik_ref, edge_ref,
):
    third = lambda ref, i: ref[i * MEMBERS : (i + 1) * MEMBERS]
    has_after = after_ref[HALO : HALO + 1, 3:4]
    flow_before = third(before_ref, 0)
    depth_0 = third(up_ref, 0) + advection * flow_before
    next_before = third(before_ref, 1) - third(before_ref, 2) * depth_0
    depth_32 = (third(after_ref, 0) + advection * third(down_ref, 0)) * has_after
    flow_31 = third(down_ref, 1) - third(down_ref, 2) * depth_32
    late_32 = (
        depth_32 * third(after_ref, 1) + diffusion * column_spread(depth_32) + third(after_ref, 2) + advection * flow_31
    ) * has_after
    edge_ref[0] = flow_before
    edge_ref[1] = next_before
    edge_ref[2] = depth_32
    edge_ref[3] = late_32
    rate = exchange_ref[...].astype(f32)
    row = lax.broadcasted_iota(jnp.int32, (ROWS, COLS), 0)

    def member(p, carry):
        depth = surface_ref[p].astype(f32)
        flow = discharge_ref[p].astype(f32)
        stored = storage_ref[p].astype(f32)
        for step in range(2):
            flow_below = jnp.where(row == 0, edge_ref[step, pl.ds(p, 1)], pltpu.roll(flow, 1, 0))
            inflow = rate * (depth - stored)
            depth_next = (
                depth - advection * (flow - flow_below) + diffusion * column_spread(depth) - inflow
                + depth_noise_ref[step, p].astype(f32)
            )
            stored = (1.0 - drainage) * stored + inflow
            depth_above = jnp.where(row == ROWS - 1, edge_ref[2 + step, pl.ds(p, 1)], pltpu.roll(depth_next, ROWS - 1, 0))
            flow = (flow - gravity * (depth_above - depth_next) + flow_noise_ref[step, p].astype(f32)) / (
                1.0 + friction * jnp.abs(flow)
            )
            depth = depth_next
        at = pl.ds(pl.multiple_of(p * ROWS, ROWS), ROWS)
        for ref, value in ((depth_ref, depth), (flow_ref, flow), (stored_ref, stored)):
            ref[0, at] = value[:, :LANES]
            ref[1, at] = value[:, LANES:]
        return carry

    lax.fori_loop(0, MEMBERS, member, 0)
    lane = lax.broadcasted_iota(jnp.int32, (MEMBERS, LANES), 1)
    sampled = jnp.zeros((MEMBERS, LANES), f32)
    for k in range(SENS):
        cell = cell_ref[k]
        found = depth_ref[(cell >> 7) & 1, pl.ds((cell >> 8) & (ROWS - 1), MEMBERS, stride=ROWS)]
        found = pltpu.roll(found, (k - cell) & (LANES - 1), 1)
        sampled = jnp.where(lane == k, found, sampled)
    misfit = (sampled[:, :SENS] - observed_ref[...]) / sigma_ref[...]
    reach = radius_ref[...].astype(f32)
    lik = -0.5 * misfit * misfit / (reach * reach)
    lik_ref[...] = jnp.concatenate([lik, jnp.zeros((MEMBERS, LANES - SENS), f32)], axis=1)


def taper_kernel(down_ref, before_ref, after_ref, taper_ref):
    entries = [ref[HALO:MESSAGE, 0:LANES] for ref in (before_ref, down_ref, after_ref)]
    column_at = lax.broadcasted_iota(jnp.int32, (SENS, COLS), 1).astype(f32)
    near, rows = [], []
    for shift, entry in zip((-ROWS, 0, ROWS), entries):
        gap = column_at - entry[:, 1:2]
        near.append(entry[:, 2:3] - gap * gap)
        rows.append(jnp.broadcast_to(entry[:, 0:1] + float(shift), (SENS, COLS)))
    blank = jnp.zeros((SENS, COLS), bf16)

    def at_row(r, carry):
        here = r.astype(f32)
        for part in range(3):
            gap = here - rows[part]
            value = jnp.maximum(near[part] - gap * gap, 0.0)
            coarse = value.astype(bf16)
            taper_ref[r, part * SENS : (part + 1) * SENS] = coarse
            taper_ref[r, LANES + part * SENS : LANES + (part + 1) * SENS] = (value - coarse.astype(f32)).astype(bf16)
        taper_ref[r, 3 * SENS : LANES] = blank
        taper_ref[r, LANES + 3 * SENS : 2 * LANES] = blank
        return carry

    lax.fori_loop(0, ROWS, at_row, 0)


def weight_kernel(taper_ref, lik_ref, before_ref, after_ref, depth_ref, flow_ref, stored_ref, out_ref, weight_ref):
    lik = before_ref[...] + pltpu.roll(lik_ref[...], SENS, 1) + pltpu.roll(after_ref[...], 2 * SENS, 1)
    high = lik.astype(bf16)
    rest = lik - high.astype(f32)
    middle = rest.astype(bf16)
    low = (rest - middle.astype(f32)).astype(bf16)
    pieces = jnp.concatenate([high.astype(f32), middle.astype(f32), low.astype(f32)], axis=0).astype(bf16)
    pieces = jnp.concatenate([pieces, pieces], axis=1)

    def at_row(r, carry):
        part = jnp.dot(pieces, taper_ref[r], preferred_element_type=f32)
        weight = part[:MEMBERS] + part[MEMBERS : 2 * MEMBERS] + part[2 * MEMBERS :]
        weight_ref[0, pl.ds(pl.multiple_of(r * MEMBERS, MEMBERS), MEMBERS)] = weight[:, :LANES]
        weight_ref[1, pl.ds(pl.multiple_of(r * MEMBERS, MEMBERS), MEMBERS)] = weight[:, LANES:]
        return carry

    lax.fori_loop(0, ROWS, at_row, 0)

    def block(i, carry):
        for half in range(2):
            weights = [weight_ref[half, pl.ds(i * 8 * MEMBERS + p, 8, stride=MEMBERS)] for p in range(MEMBERS)]
            best = weights[0]
            for p in range(1, MEMBERS):
                best = jnp.maximum(best, weights[p])
            sums = [jnp.zeros((8, LANES), f32) for _ in range(4)]
            for p in range(MEMBERS):
                factor = jnp.exp(weights[p] - best)
                at = pl.ds(pl.multiple_of(p * ROWS + i * 8, 8), 8)
                sums[0] = sums[0] + factor
                sums[1] = sums[1] + factor * depth_ref[half, at]
                sums[2] = sums[2] + factor * flow_ref[half, at]
                sums[3] = sums[3] + factor * stored_ref[half, at]
            inverse = 1.0 / sums[0]
            results = (best + jnp.log(sums[0]), sums[1] * inverse, sums[2] * inverse, sums[3] * inverse)
            for slot, result in enumerate(results):
                out_ref[pl.ds(i * 64 + 2 * slot + half, 8, stride=8)] = result
        return carry

    lax.fori_loop(0, ROWS // 8, block, 0)


def combine_kernel(groups, in_ref, out_ref):
    def quantity(slot, half):
        return in_ref[pl.ds(2 * slot + half, groups, stride=8)]

    rows = []
    totals = []
    for half in range(2):
        level = quantity(0, half)
        share = jnp.exp(level - jnp.max(level, axis=0, keepdims=True))
        totals.append((share, 1.0 / jnp.sum(share, axis=0, keepdims=True)))
    for slot in range(1, 4):
        for half in range(2):
            share, inverse = totals[half]
            rows.append(jnp.sum(share * quantity(slot, half), axis=0, keepdims=True) * inverse)
    rows.append(jnp.zeros((2, LANES), f32))
    result = jnp.concatenate(rows, axis=0)
    for copy in range(groups):
        out_ref[copy * 8 : (copy + 1) * 8] = result


def spread_kernel(in_ref, depth_ref, flow_ref, stored_ref):
    for slot, ref in enumerate((depth_ref, flow_ref, stored_ref)):
        for half in range(2):
            ref[:, half * LANES : (half + 1) * LANES] = in_ref[pl.ds(2 * slot + half, ROWS, stride=8)]


VMEM = pl.BlockSpec(memory_space=pltpu.VMEM)
SMEM = pl.BlockSpec(memory_space=pltpu.SMEM)


def call(kernel, name, in_specs, outs, scratch=(), flops=0, nbytes=0):
    return pl.pallas_call(
        kernel,
        name=name,
        in_specs=in_specs,
        out_specs=[VMEM] * len(outs),
        out_shape=[jax.ShapeDtypeStruct(shape, dtype) for shape, dtype in outs],
        scratch_shapes=list(scratch),
        compiler_params=pltpu.CompilerParams(vmem_limit_bytes=40 * 1024 * 1024),
        cost_estimate=pl.CostEstimate(flops=flops, bytes_accessed=nbytes, transcendentals=0),
    )


def local(
    surface, discharge, storage, exchange, depth_perturbation, flow_perturbation,
    sensor_cell, sensor_radius, observed, sensor_sigma,
):
    strips = lax.axis_size("strip")
    groups = lax.axis_size("dom")
    downward = [(i, i + 1) for i in range(strips - 1)]
    upward = [(i + 1, i) for i in range(strips - 1)]
    fields = (surface, discharge, storage, exchange, depth_perturbation, flow_perturbation)
    up, down = call(
        pack_kernel, "pack", [SMEM] * 2 + [VMEM] * 6, [((MESSAGE, COLS), f32)] * 2,
        [pltpu.VMEM((6, 2, MEMBERS * 8, LANES), f32), pltpu.VMEM((5, 2, MEMBERS * 8, LANES), f32)],
    )(sensor_cell, sensor_radius, *fields)
    before = lax.ppermute(down, "strip", downward)
    after = lax.ppermute(up, "strip", upward)
    grid = ((2, MEMBERS * ROWS, LANES), f32)
    as_row = lambda values: values.reshape(1, SENS)
    depth, flow, stored, lik = call(
        forecast_kernel, "forecast", [SMEM] + [VMEM] * 13, [grid, grid, grid, ((MEMBERS, LANES), f32)],
        [pltpu.VMEM((4, MEMBERS, COLS), f32)],
    )(sensor_cell, *fields, up, down, before, after, as_row(sensor_radius), as_row(observed), as_row(sensor_sigma))
    lik_before = lax.ppermute(lik, "strip", downward)
    lik_after = lax.ppermute(lik, "strip", upward)
    (taper,) = call(
        taper_kernel, "taper", [VMEM] * 3, [((ROWS, 2 * LANES, COLS), bf16)], nbytes=4 << 20, flops=8 << 20,
    )(down, before, after)
    (parts,) = call(
        weight_kernel, "weights", [VMEM] * 7, [((groups * 8, LANES), f32)],
        [pltpu.VMEM((2, ROWS * MEMBERS, LANES), f32)],
    )(taper, lik, lik_before, lik_after, depth, flow, stored)
    shared = lax.all_to_all(parts.reshape(groups, 8, LANES), "dom", 0, 0, tiled=True)
    (rows,) = call(
        lambda *refs: combine_kernel(groups, *refs), "combine", [VMEM], [((groups * 8, LANES), f32)],
    )(shared.reshape(groups * 8, LANES))
    whole = lax.all_to_all(rows.reshape(groups, 8, LANES), "dom", 0, 0, tiled=True)
    return tuple(
        call(spread_kernel, "spread", [VMEM], [((ROWS, COLS), f32)] * 3)(whole.reshape(groups * 8, LANES))
    )


def solution(mesh):
    return jax.shard_map(
        local,
        mesh=mesh,
        in_specs=(
            P("dom", "strip", None),
            P("dom", "strip", None),
            P("dom", "strip", None),
            P("strip", None),
            P(None, "dom", "strip", None),
            P(None, "dom", "strip", None),
            P("strip"),
            P("strip"),
            P("strip"),
            P("strip"),
        ),
        out_specs=(P("strip", None), P("strip", None), P("strip", None)),
        check_vma=False,
    )
```

time: 360 us -> 74 us (0.21)
  the two profiles are of different devices: /device:TPU:8 before, /device:TPU:256 now
where the time goes in v1:
time: 74 us; the launch traced here: 73.4 us
  blocking collectives  33.9 us (46%)
  Pallas kernels  14 us (19%)
  starting transfers between devices  8.65 us (12%)
  local copies, waits for them, and re-layouts  8.58 us (12%)
  waiting for transfers between devices  7.55 us (10%)
    all_to_all x1, blocking collectives, local(): lax.all_to_all(parts.reshape(groups, 8, LANES), 'dom', 0, 0, tiled=True)  20.1 us
    all_to_all x1, blocking collectives, local(): lax.all_to_all(rows.reshape(groups, 8, LANES), 'dom', 0, 0, tiled=True)  13.9 us
    unnamed x20, local copies, waits for them, and re-layouts  8.58 us
    pallas_call x1, Pallas kernels, local(): call(weight_kernel, 'weights', [VMEM] * 7, [((groups * 8, LANES), f32)],...  5.76 us
    pallas_call x1, Pallas kernels, local(): call(forecast_kernel, 'forecast', [SMEM] + [VMEM] * 13, [grid, grid, grid...  5.69 us
    ppermute x1, waiting for transfers between devices, local(): before = lax.ppermute(down, 'strip', downward)  4.81 us
    ppermute x1, waiting for transfers between devices, local(): lik_before = lax.ppermute(lik, 'strip', downward)  2.74 us
    ppermute x1, starting transfers between devices, local(): before = lax.ppermute(down, 'strip', downward)  2.41 us
  transfers between devices with their start and end apart: 4, of which 2 were waited for; matrix products, arithmetic and copies ran while one was open for 0% of the time, Pallas kernels for 1%

profile of v1, /device:TPU:256, one launch (start us, length us, event | category | flops | bytes accessed | tf_op | source)
XLA Modules:
  0.0 73.4 jit_solution(6061506647286615537)
XLA Ops:
  0.6 0.0 copy-start
  0.6 1.1 %copy-done = bf16[2,24,32,256]{3,2,1,0:T(8,128)(2,1)S(1)} copy-done((bf16[2,24,32,256]{3,2,1,0:T(8,128)(2,1)S(1)}, bf16[2,24,32,256]{3,2,1,0:T(8,128)(2,1)}, u32[]{:S(2)}) %copy-start) | copy-done | bytes 786456
  1.8 0.0 copy-start.1
  1.8 1.1 %copy-done.1 = bf16[2,24,32,256]{3,2,1,0:T(8,128)(2,1)S(1)} copy-done((bf16[2,24,32,256]{3,2,1,0:T(8,128)(2,1)S(1)}, bf16[2,24,32,256]{3,2,1,0:T(8,128)(2,1)}, u32[]{:S(2)}) %copy-start.1) | copy-done | bytes 786456
  2.9 0.0 copy-start.2
  2.9 1.0 %copy-done.2 = bf16[24,32,256]{2,1,0:T(8,128)(2,1)S(1)} copy-done((bf16[24,32,256]{2,1,0:T(8,128)(2,1)S(1)}, bf16[24,32,256]{2,1,0:T(8,128)(2,1)}, u32[]{:S(2)}) %copy-start.2) | copy-done | bytes 393240
  3.9 0.0 copy-start.3
  3.9 1.0 %copy-done.3 = bf16[24,32,256]{2,1,0:T(8,128)(2,1)S(1)} copy-done((bf16[24,32,256]{2,1,0:T(8,128)(2,1)S(1)}, bf16[24,32,256]{2,1,0:T(8,128)(2,1)}, u32[]{:S(2)}) %copy-start.3) | copy-done | bytes 393240
  4.9 0.0 copy-start.4
  4.9 1.0 %copy-done.4 = bf16[24,32,256]{2,1,0:T(8,128)(2,1)S(1)} copy-done((bf16[24,32,256]{2,1,0:T(8,128)(2,1)S(1)}, bf16[24,32,256]{2,1,0:T(8,128)(2,1)}, u32[]{:S(2)}) %copy-start.4) | copy-done | bytes 393240
  5.9 0.0 copy-start.5
  5.9 0.7 copy-done.5
  6.6 0.0 copy-start.6
  6.6 0.7 copy-done.6
  7.3 0.0 copy-start.7
  7.3 0.7 copy-done.7
  7.9 0.8 %pack.1 = (f32[104,256]{1,0:T(8,128)S(1)}, f32[104,256]{1,0:T(8,128)S(1)}) custom-call(s32[32]{0:T(128)S(1)} %copy-done.6, s32[32]{0:T(128)S(1)} %copy-done.7, bf16[24,32,256]{2,1,0:T(8,128)(2,1)S(1)} %copy-done.2, bf16[24,32,256]{2,1,0:T(8,128)(2,1)S(1)} %copy-done.3, bf16[24,32,256]{2,1,0:T(8,128)(2,1)S(1)} %copy-done.4, bf16[32,256]{1,0:T(8,128)(2,1)S(1)} %copy-done.5, ...), custom_call_target="tpu_custom_call" | custom-call | tf_op jit(solution)/shard_map/pack/pallas_call | solution.py:279
  8.7 1.9 %collective-permute-start.1 = (f32[104,256]{1,0:T(8,128)S(1)}, f32[104,256]{1,0:T(8,128)S(1)}, u32[]{:S(2)}, u32[]{:S(2)}) collective-permute-start(f32[104,256]{1,0:T(8,128)S(1)} %get-tuple-element.10.up_ref), channel_id=1, source_target_pairs={{1,0},{2,1},{3,2},{4,3},{5,4},{6,5},{7,6},{8,7},{9,8},{10,9},{11,1... | collective-permute-start | bytes 319496 | tf_op jit(solution)/shard_map/ppermute | solution.py:284
  10.7 2.4 %collective-permute-start = (f32[104,256]{1,0:T(8,128)S(1)}, f32[104,256]{1,0:T(8,128)S(1)}, u32[]{:S(2)}, u32[]{:S(2)}) collective-permute-start(f32[104,256]{1,0:T(8,128)S(1)} %get-tuple-element.9.down_ref), channel_id=1, source_target_pairs={{0,1},{1,2},{2,3},{3,4},{4,5},{5,6},{6,7},{7,8},{8,9},{9,10},{10,1... | collective-permute-start | bytes 319496 | tf_op jit(solution)/shard_map/ppermute | solution.py:283
  13.1 0.0 collective-permute-done.1.after_ref
  13.1 4.8 %collective-permute-done.before_ref = f32[104,256]{1,0:T(8,128)S(1)} collective-permute-done((f32[104,256]{1,0:T(8,128)S(1)}, f32[104,256]{1,0:T(8,128)S(1)}, u32[]{:S(2)}, u32[]{:S(2)}) %collective-permute-start) | collective-permute-done | bytes 106528 | tf_op jit(solution)/shard_map/ppermute | solution.py:283
  17.9 0.0 copy-start.8
  17.9 0.7 copy-done.8
  18.5 0.0 copy-start.9
  18.5 0.7 copy-done.9
  19.2 5.7 %forecast.1 = (f32[2,768,128]{2,1,0:T(8,128)S(1)}, f32[2,768,128]{2,1,0:T(8,128)S(1)}, f32[2,768,128]{2,1,0:T(8,128)S(1)}, f32[24,128]{1,0:T(8,128)S(1)}) custom-call(s32[32]{0:T(128)S(1)} %copy-done.6, bf16[24,32,256]{2,1,0:T(8,128)(2,1)S(1)} %copy-done.2, bf16[24,32,256]{2,1,0:T(8,128)(2,1)S(1)} %copy-done.3, bf16[24,32,256]{2,1,0:T(8,128)(2,1)S(1)} %copy-done.4, ...), custom_call_target="tpu_custom_call" | custom-call | tf_op jit(solution)/shard_map/forecast/pallas_call | solution.py:287
  24.9 1.9 %collective-permute-start.3 = (f32[24,128]{1,0:T(8,128)S(1)}, f32[24,128]{1,0:T(8,128)S(1)}, u32[]{:S(2)}, u32[]{:S(2)}) collective-permute-start(f32[24,128]{1,0:T(8,128)S(1)} %get-tuple-element.11.lik_ref), channel_id=1, source_target_pairs={{1,0},{2,1},{3,2},{4,3},{5,4},{6,5},{7,6},{8,7},{9,8},{10,9},{11,1... | collective-permute-start | bytes 36872 | tf_op jit(solution)/shard_map/ppermute | solution.py:292
  26.8 2.4 %collective-permute-start.2 = (f32[24,128]{1,0:T(8,128)S(1)}, f32[24,128]{1,0:T(8,128)S(1)}, u32[]{:S(2)}, u32[]{:S(2)}) collective-permute-start(f32[24,128]{1,0:T(8,128)S(1)} %get-tuple-element.11.lik_ref), channel_id=1, source_target_pairs={{0,1},{1,2},{2,3},{3,4},{4,5},{5,6},{6,7},{7,8},{8,9},{9,10},{10,1... | collective-permute-start | bytes 36872 | tf_op jit(solution)/shard_map/ppermute | solution.py:291
  29.2 1.1 %taper.1.taper_ref = bf16[32,256,256]{2,1,0:T(8,128)(2,1)S(1)} custom-call(f32[104,256]{1,0:T(8,128)S(1)} %get-tuple-element.9.down_ref, f32[104,256]{1,0:T(8,128)S(1)} %collective-permute-done.before_ref, f32[104,256]{1,0:T(8,128)S(1)} %collective-permute-done.1.after_ref), custom_call_target="tpu_custom_call" | custom-call | flops 8388608 | bytes 4194304 | tf_op jit(solution)/shard_map/taper/pallas_call | solution.py:293
  30.3 0.0 collective-permute-done.3.after_ref
  30.3 2.7 %collective-permute-done.2.before_ref = f32[24,128]{1,0:T(8,128)S(1)} collective-permute-done((f32[24,128]{1,0:T(8,128)S(1)}, f32[24,128]{1,0:T(8,128)S(1)}, u32[]{:S(2)}, u32[]{:S(2)}) %collective-permute-start.2) | collective-permute-done | bytes 12320 | tf_op jit(solution)/shard_map/ppermute | solution.py:291
  33.0 5.8 %weights.1 = f32[256,128]{1,0:T(8,128)S(1)} custom-call(bf16[32,256,256]{2,1,0:T(8,128)(2,1)S(1)} %taper.1.taper_ref, f32[24,128]{1,0:T(8,128)S(1)} %get-tuple-element.11.lik_ref, f32[24,128]{1,0:T(8,128)S(1)} %collective-permute-done.2.before_ref, f32[24,128]{1,0:T(8,128)S(1)} %collective-permute-done.3.after_ref, ...), custom_call_target="tpu_custom_call" | custom-call | tf_op jit(solution)/shard_map/weights/pallas_call | solution.py:296
  38.8 20.1 %all_to_all.10 = f32[32,8,128]{2,1,0:T(8,128)S(1)} all-to-all(f32[32,8,128]{2,1,0:T(8,128)S(1)} %bitcast.7), channel_id=1, replica_groups=mesh['dom'=32,'strip'=16] {'dom'}, dimensions={0} | all-to-all | bytes 262144 | tf_op jit(solution)/shard_map/all_to_all | solution.py:300
  58.9 0.1 combine.1
  58.9 13.9 %all_to_all.11 = f32[32,8,128]{2,1,0:T(8,128)S(1)} all-to-all(f32[32,8,128]{2,1,0:T(8,128)S(1)} %bitcast.10), channel_id=1, replica_groups=mesh['dom'=32,'strip'=16] {'dom'}, dimensions={0} | all-to-all | bytes 262144 | tf_op jit(solution)/shard_map/all_to_all | solution.py:304
  72.8 0.7 spread.1
Async XLA Ops:
  0.6 1.1 %copy-start = (bf16[2,24,32,256]{3,2,1,0:T(8,128)(2,1)S(1)}, bf16[2,24,32,256]{3,2,1,0:T(8,128)(2,1)}, u32[]{:S(2)}) copy-start(bf16[2,24,32,256]{3,2,1,0:T(8,128)(2,1)} %depth_noise_ref.3) | copy-start | bytes 2359300
  1.8 1.1 %copy-start.1 = (bf16[2,24,32,256]{3,2,1,0:T(8,128)(2,1)S(1)}, bf16[2,24,32,256]{3,2,1,0:T(8,128)(2,1)}, u32[]{:S(2)}) copy-start(bf16[2,24,32,256]{3,2,1,0:T(8,128)(2,1)} %flow_noise_ref.3) | copy-start | bytes 2359300
  2.9 1.0 %copy-start.2 = (bf16[24,32,256]{2,1,0:T(8,128)(2,1)S(1)}, bf16[24,32,256]{2,1,0:T(8,128)(2,1)}, u32[]{:S(2)}) copy-start(bf16[24,32,256]{2,1,0:T(8,128)(2,1)} %surface_ref.3) | copy-start | bytes 1179652
  3.9 1.0 %copy-start.3 = (bf16[24,32,256]{2,1,0:T(8,128)(2,1)S(1)}, bf16[24,32,256]{2,1,0:T(8,128)(2,1)}, u32[]{:S(2)}) copy-start(bf16[24,32,256]{2,1,0:T(8,128)(2,1)} %discharge_ref.3) | copy-start | bytes 1179652
  4.9 1.0 %copy-start.4 = (bf16[24,32,256]{2,1,0:T(8,128)(2,1)S(1)}, bf16[24,32,256]{2,1,0:T(8,128)(2,1)}, u32[]{:S(2)}) copy-start(bf16[24,32,256]{2,1,0:T(8,128)(2,1)} %storage_ref.3) | copy-start | bytes 1179652
  5.9 0.7 copy-start.5
  6.6 0.7 copy-start.6
  7.3 0.7 copy-start.7
  8.7 4.3 %collective-permute-start.1 = (f32[104,256]{1,0:T(8,128)S(1)}, f32[104,256]{1,0:T(8,128)S(1)}, u32[]{:S(2)}, u32[]{:S(2)}) collective-permute-start(f32[104,256]{1,0:T(8,128)S(1)} %get-tuple-element.10.up_ref), channel_id=1, source_target_pairs={{1,0},{2,1},{3,2},{4,3},{5,4},{6,5},{7,6},{8,7},{9,8},{10,9},{11,1... | collective-permute-start | bytes 319496 | tf_op jit(solution)/shard_map/ppermute | solution.py:284
  10.7 7.2 %collective-permute-start = (f32[104,256]{1,0:T(8,128)S(1)}, f32[104,256]{1,0:T(8,128)S(1)}, u32[]{:S(2)}, u32[]{:S(2)}) collective-permute-start(f32[104,256]{1,0:T(8,128)S(1)} %get-tuple-element.9.down_ref), channel_id=1, source_target_pairs={{0,1},{1,2},{2,3},{3,4},{4,5},{5,6},{6,7},{7,8},{8,9},{9,10},{10,1... | collective-permute-start | bytes 319496 | tf_op jit(solution)/shard_map/ppermute | solution.py:283
  17.9 0.7 copy-start.8
  18.5 0.7 copy-start.9
  24.9 5.4 %collective-permute-start.3 = (f32[24,128]{1,0:T(8,128)S(1)}, f32[24,128]{1,0:T(8,128)S(1)}, u32[]{:S(2)}, u32[]{:S(2)}) collective-permute-start(f32[24,128]{1,0:T(8,128)S(1)} %get-tuple-element.11.lik_ref), channel_id=1, source_target_pairs={{1,0},{2,1},{3,2},{4,3},{5,4},{6,5},{7,6},{8,7},{9,8},{10,9},{11,1... | collective-permute-start | bytes 36872 | tf_op jit(solution)/shard_map/ppermute | solution.py:292
  26.8 6.2 %collective-permute-start.2 = (f32[24,128]{1,0:T(8,128)S(1)}, f32[24,128]{1,0:T(8,128)S(1)}, u32[]{:S(2)}, u32[]{:S(2)}) collective-permute-start(f32[24,128]{1,0:T(8,128)S(1)} %get-tuple-element.11.lik_ref), channel_id=1, source_target_pairs={{0,1},{1,2},{2,3},{3,4},{4,5},{5,6},{6,7},{7,8},{8,9},{9,10},{10,1... | collective-permute-start | bytes 36872 | tf_op jit(solution)/shard_map/ppermute | solution.py:291

commit v2 on v1

--- a/solution.py
+++ b/solution.py
@@ -31,28 +31,51 @@
     return left_side - 2.0 * field + right_side
 
 
-def pack_kernel(
-    cell_ref, radius_ref, surface_ref, discharge_ref, storage_ref, exchange_ref, depth_noise_ref, flow_noise_ref,
-    up_ref, down_ref, first_ref, last_ref,
+def sides(left_half, right_half):
+    lane = lax.broadcasted_iota(jnp.int32, left_half.shape, 1)
+    first, last = lane == 0, lane == LANES - 1
+    left_back, right_back = pltpu.roll(left_half, 1, 1), pltpu.roll(right_half, 1, 1)
+    left_on, right_on = pltpu.roll(left_half, LANES - 1, 1), pltpu.roll(right_half, LANES - 1, 1)
+    return (
+        jnp.where(first, left_half, left_back) + jnp.where(last, right_on, left_on),
+        jnp.where(first, left_back, right_back) + jnp.where(last, right_half, right_on),
+    )
+
+
+def load_kernel(
+    cell_hbm, radius_hbm, surface_hbm, discharge_hbm, storage_hbm, exchange_hbm, depth_noise_hbm, flow_noise_hbm,
+    up_ref, down_ref, surface_ref, discharge_ref, storage_ref, exchange_ref, depth_noise_ref, flow_noise_ref,
+    first_ref, last_ref, cell_ref, radius_ref, sems,
 ):
+    pairs = [
+        (surface_hbm, surface_ref), (discharge_hbm, discharge_ref), (storage_hbm, storage_ref),
+        (depth_noise_hbm.at[0], depth_noise_ref.at[0]), (flow_noise_hbm.at[0], flow_noise_ref.at[0]),
+        (depth_noise_hbm.at[1], depth_noise_ref.at[1]), (exchange_hbm, exchange_ref),
+        (cell_hbm, cell_ref), (radius_hbm, radius_ref), (flow_noise_hbm.at[1], flow_noise_ref.at[1]),
+    ]
+    copies = [pltpu.make_async_copy(source, target, sems.at[i]) for i, (source, target) in enumerate(pairs)]
+    for copy in copies:
+        copy.start()
+
     def keep(scratch, slot, rows):
         flat = rows.reshape(MEMBERS * 8, COLS)
         scratch[slot, 0] = flat[:, :LANES]
         scratch[slot, 1] = flat[:, LANES:]
 
     def take(ref, lead, slot):
-        head = ref[lead + (slice(None), slice(0, 16), slice(None))].astype(f32)
-        tail = ref[lead + (slice(None), slice(16, 32), slice(None))].astype(f32)
-        keep(first_ref, slot, head[:, :8])
-        keep(last_ref, slot, tail[:, 8:])
+        copies[slot].wait()
+        keep(first_ref, slot, ref[lead + (slice(None), slice(0, 16), slice(None))].astype(f32)[:, :8])
+        keep(last_ref, slot, ref[lead + (slice(None), slice(16, 32), slice(None))].astype(f32)[:, 8:])
 
     take(surface_ref, (), 0)
     take(discharge_ref, (), 1)
     take(storage_ref, (), 2)
     take(depth_noise_ref, (0,), 3)
     take(flow_noise_ref, (0,), 4)
-    late = depth_noise_ref[1, :, 0:16, :].astype(f32)
-    keep(first_ref, 5, late[:, :8])
+    copies[5].wait()
+    keep(first_ref, 5, depth_noise_ref[1, :, 0:16, :].astype(f32)[:, :8])
+    for copy in copies[6:9]:
+        copy.wait()
 
     def row_of(ref, slot, row):
         halves = [ref[slot, half, pl.ds(row, MEMBERS, stride=8)] for half in range(2)]
@@ -97,13 +120,20 @@
         entry = jnp.where(lane == 0, row, jnp.where(lane == 1, column, jnp.where(lane == 2, reach * reach, 1.0)))
         up_ref[HALO + k : HALO + k + 1] = entry
         down_ref[HALO + k : HALO + k + 1] = entry
+    copies[9].wait()
 
 
 def forecast_kernel(
-    cell_ref, surface_ref, discharge_ref, storage_ref, exchange_ref, depth_noise_ref, flow_noise_ref,
-    up_ref, down_ref, before_ref, after_ref, radius_ref, observed_ref, sigma_ref,
-    depth_ref, flow_ref, stored_ref, lik_ref, edge_ref,
+    cell_hbm, radius_hbm, observed_hbm, sigma_hbm,
+    surface_ref, discharge_ref, storage_ref, exchange_ref, depth_noise_ref, flow_noise_ref,
+    up_ref, down_ref, before_ref, after_ref,
+    depth_ref, flow_ref, stored_ref, lik_ref,
+    edge_ref, cell_ref, radius_ref, observed_ref, sigma_ref, sems,
 ):
+    pairs = [(cell_hbm, cell_ref), (radius_hbm, radius_ref), (observed_hbm, observed_ref), (sigma_hbm, sigma_ref)]
+    copies = [pltpu.make_async_copy(source, target, sems.at[i]) for i, (source, target) in enumerate(pairs)]
+    for copy in copies:
+        copy.start()
     third = lambda ref, i: ref[i * MEMBERS : (i + 1) * MEMBERS]
     has_after = after_ref[HALO : HALO + 1, 3:4]
     flow_before = third(before_ref, 0)
@@ -118,33 +148,41 @@
     edge_ref[1] = next_before
     edge_ref[2] = depth_32
     edge_ref[3] = late_32
-    rate = exchange_ref[...].astype(f32)
-    row = lax.broadcasted_iota(jnp.int32, (ROWS, COLS), 0)
+    row = lax.broadcasted_iota(jnp.int32, (ROWS, LANES), 0)
+
+    def halves(values):
+        return [values[:, :LANES], values[:, LANES:]]
+
+    rates = halves(exchange_ref[...].astype(f32))
 
     def member(p, carry):
-        depth = surface_ref[p].astype(f32)
-        flow = discharge_ref[p].astype(f32)
-        stored = storage_ref[p].astype(f32)
+        depth, flow, stored = [halves(ref[p].astype(f32)) for ref in (surface_ref, discharge_ref, storage_ref)]
         for step in range(2):
-            flow_below = jnp.where(row == 0, edge_ref[step, pl.ds(p, 1)], pltpu.roll(flow, 1, 0))
-            inflow = rate * (depth - stored)
-            depth_next = (
-                depth - advection * (flow - flow_below) + diffusion * column_spread(depth) - inflow
-                + depth_noise_ref[step, p].astype(f32)
-            )
-            stored = (1.0 - drainage) * stored + inflow
-            depth_above = jnp.where(row == ROWS - 1, edge_ref[2 + step, pl.ds(p, 1)], pltpu.roll(depth_next, ROWS - 1, 0))
-            flow = (flow - gravity * (depth_above - depth_next) + flow_noise_ref[step, p].astype(f32)) / (
-                1.0 + friction * jnp.abs(flow)
-            )
-            depth = depth_next
+            depth_noise, flow_noise = [halves(ref[step, p].astype(f32)) for ref in (depth_noise_ref, flow_noise_ref)]
+            row_before, row_after = [halves(edge_ref[slot, pl.ds(p, 1)]) for slot in (step, 2 + step)]
+            beside = sides(*depth)
+            for h in range(2):
+                flow_below = jnp.where(row == 0, row_before[h], pltpu.roll(flow[h], 1, 0))
+                inflow = rates[h] * (depth[h] - stored[h])
+                depth_next = (
+                    (1.0 - 2.0 * diffusion) * depth[h] + diffusion * beside[h]
+                    - advection * (flow[h] - flow_below) - inflow + depth_noise[h]
+                )
+                stored[h] = (1.0 - drainage) * stored[h] + inflow
+                depth_above = jnp.where(row == ROWS - 1, row_after[h], pltpu.roll(depth_next, ROWS - 1, 0))
+                flow[h] = (flow[h] - gravity * (depth_above - depth_next) + flow_noise[h]) * (
+                    1.0 / (1.0 + friction * jnp.abs(flow[h]))
+                )
+                depth[h] = depth_next
         at = pl.ds(pl.multiple_of(p * ROWS, ROWS), ROWS)
         for ref, value in ((depth_ref, depth), (flow_ref, flow), (stored_ref, stored)):
-            ref[0, at] = value[:, :LANES]
-            ref[1, at] = value[:, LANES:]
+            for h in range(2):
+                ref[h, at] = value[h]
         return carry
 
-    lax.fori_loop(0, MEMBERS, member, 0)
+    lax.fori_loop(0, MEMBERS, member, 0, unroll=4)
+    for copy in copies:
+        copy.wait()
     lane = lax.broadcasted_iota(jnp.int32, (MEMBERS, LANES), 1)
     sampled = jnp.zeros((MEMBERS, LANES), f32)
     for k in range(SENS):
@@ -192,25 +230,21 @@
     pieces = jnp.concatenate([high.astype(f32), middle.astype(f32), low.astype(f32)], axis=0).astype(bf16)
     pieces = jnp.concatenate([pieces, pieces], axis=1)
 
-    def at_row(r, carry):
-        part = jnp.dot(pieces, taper_ref[r], preferred_element_type=f32)
-        weight = part[:MEMBERS] + part[MEMBERS : 2 * MEMBERS] + part[2 * MEMBERS :]
-        weight_ref[0, pl.ds(pl.multiple_of(r * MEMBERS, MEMBERS), MEMBERS)] = weight[:, :LANES]
-        weight_ref[1, pl.ds(pl.multiple_of(r * MEMBERS, MEMBERS), MEMBERS)] = weight[:, LANES:]
-        return carry
-
-    lax.fori_loop(0, ROWS, at_row, 0)
-
-    def block(i, carry):
+    for i in range(ROWS // 8):
+        for r in range(8 * i, 8 * i + 8):
+            part = jnp.dot(pieces, taper_ref[r], preferred_element_type=f32)
+            weight = part[:MEMBERS] + part[MEMBERS : 2 * MEMBERS] + part[2 * MEMBERS :]
+            for half in range(2):
+                weight_ref[half, r * MEMBERS : (r + 1) * MEMBERS] = weight[:, half * LANES : (half + 1) * LANES]
         for half in range(2):
-            weights = [weight_ref[half, pl.ds(i * 8 * MEMBERS + p, 8, stride=MEMBERS)] for p in range(MEMBERS)]
+            weights = [weight_ref[half, pl.ds(8 * i * MEMBERS + p, 8, stride=MEMBERS)] for p in range(MEMBERS)]
             best = weights[0]
             for p in range(1, MEMBERS):
                 best = jnp.maximum(best, weights[p])
             sums = [jnp.zeros((8, LANES), f32) for _ in range(4)]
             for p in range(MEMBERS):
                 factor = jnp.exp(weights[p] - best)
-                at = pl.ds(pl.multiple_of(p * ROWS + i * 8, 8), 8)
+                at = pl.ds(p * ROWS + 8 * i, 8)
                 sums[0] = sums[0] + factor
                 sums[1] = sums[1] + factor * depth_ref[half, at]
                 sums[2] = sums[2] + factor * flow_ref[half, at]
@@ -218,10 +252,7 @@
             inverse = 1.0 / sums[0]
             results = (best + jnp.log(sums[0]), sums[1] * inverse, sums[2] * inverse, sums[3] * inverse)
             for slot, result in enumerate(results):
-                out_ref[pl.ds(i * 64 + 2 * slot + half, 8, stride=8)] = result
-        return carry
-
-    lax.fori_loop(0, ROWS // 8, block, 0)
+                out_ref[pl.ds(64 * i + 2 * slot + half, 8, stride=8)] = result
 
 
 def combine_kernel(groups, in_ref, out_ref):
@@ -251,7 +282,7 @@
 
 
 VMEM = pl.BlockSpec(memory_space=pltpu.VMEM)
-SMEM = pl.BlockSpec(memory_space=pltpu.SMEM)
+HBM = pl.BlockSpec(memory_space=pltpu.HBM)
 
 
 def call(kernel, name, in_specs, outs, scratch=(), flops=0, nbytes=0):
@@ -275,19 +306,27 @@
     groups = lax.axis_size("dom")
     downward = [(i, i + 1) for i in range(strips - 1)]
     upward = [(i + 1, i) for i in range(strips - 1)]
-    fields = (surface, discharge, storage, exchange, depth_perturbation, flow_perturbation)
-    up, down = call(
-        pack_kernel, "pack", [SMEM] * 2 + [VMEM] * 6, [((MESSAGE, COLS), f32)] * 2,
-        [pltpu.VMEM((6, 2, MEMBERS * 8, LANES), f32), pltpu.VMEM((5, 2, MEMBERS * 8, LANES), f32)],
-    )(sensor_cell, sensor_radius, *fields)
+    stay = lambda values: pltpu.with_memory_space_constraint(values, pltpu.HBM)
+    fields = [stay(f) for f in (surface, discharge, storage, exchange, depth_perturbation, flow_perturbation)]
+    sensor_cell = stay(sensor_cell)
+    up, down, *fields = call(
+        load_kernel, "load", [HBM] * 8, [((MESSAGE, COLS), f32)] * 2 + [(field.shape, field.dtype) for field in fields],
+        [
+            pltpu.VMEM((6, 2, MEMBERS * 8, LANES), f32), pltpu.VMEM((5, 2, MEMBERS * 8, LANES), f32),
+            pltpu.SMEM((SENS,), jnp.int32), pltpu.SMEM((SENS,), jnp.int32), pltpu.SemaphoreType.DMA((10,)),
+        ],
+    )(sensor_cell, stay(sensor_radius), *fields)
     before = lax.ppermute(down, "strip", downward)
     after = lax.ppermute(up, "strip", upward)
     grid = ((2, MEMBERS * ROWS, LANES), f32)
-    as_row = lambda values: values.reshape(1, SENS)
+    as_row = lambda values: stay(values.reshape(1, SENS))
     depth, flow, stored, lik = call(
-        forecast_kernel, "forecast", [SMEM] + [VMEM] * 13, [grid, grid, grid, ((MEMBERS, LANES), f32)],
-        [pltpu.VMEM((4, MEMBERS, COLS), f32)],
-    )(sensor_cell, *fields, up, down, before, after, as_row(sensor_radius), as_row(observed), as_row(sensor_sigma))
+        forecast_kernel, "forecast", [HBM] * 4 + [VMEM] * 10, [grid, grid, grid, ((MEMBERS, LANES), f32)],
+        [
+            pltpu.VMEM((4, MEMBERS, COLS), f32), pltpu.SMEM((SENS,), jnp.int32), pltpu.VMEM((1, SENS), jnp.int32),
+            pltpu.VMEM((1, SENS), f32), pltpu.VMEM((1, SENS), f32), pltpu.SemaphoreType.DMA((4,)),
+        ],
+    )(sensor_cell, as_row(sensor_radius), as_row(observed), as_row(sensor_sigma), *fields, up, down, before, after)
     lik_before = lax.ppermute(lik, "strip", downward)
     lik_after = lax.ppermute(lik, "strip", upward)
     (taper,) = call(

time: 74 us -> 58.5 us (0.79)
  local copies, waits for them, and re-layouts: 8.58 us -> 0 us
  Pallas kernels: 14 us -> 7.39 us
    unnamed x20 -> x0, local copies, waits for them, and re-layouts: 8.58 us -> none
    pallas_call x1, Pallas kernels: 5.76 us -> 1.13 us  [local(): call(weight_kernel, 'weights', [VMEM] * 7, [((groups * 8, LANES), f32)],...]
    pallas_call x2, Pallas kernels: 6.49 us -> 4.5 us  [the longest x1 2.64 us: local(): call(forecast_kernel, 'forecast', [HBM] * 4 + [VMEM] * 10, [grid, grid, g...]
  transfers between devices with their start and end apart: 4 -> 4, of which waited for: 2 -> 2; matrix products, arithmetic and copies ran while one was open for 0% -> 0% of each run, Pallas kernels for 1% -> 2%
where the time goes in v2:
time: 58.5 us; the launch traced here: 58.2 us
  blocking collectives  33.9 us (58%)
  starting transfers between devices  8.65 us (15%)
  waiting for transfers between devices  7.55 us (13%)
  Pallas kernels  7.39 us (13%)
  between operations  0.72 us (1%)
    all_to_all x1, blocking collectives, local(): lax.all_to_all(parts.reshape(groups, 8, LANES), 'dom', 0, 0, tiled=True)  20 us
    all_to_all x1, blocking collectives, local(): lax.all_to_all(rows.reshape(groups, 8, LANES), 'dom', 0, 0, tiled=True)  13.9 us
    ppermute x1, waiting for transfers between devices, local(): before = lax.ppermute(down, 'strip', downward)  4.81 us
    ppermute x1, waiting for transfers between devices, local(): lik_before = lax.ppermute(lik, 'strip', downward)  2.74 us
    pallas_call x1, Pallas kernels, local(): call(forecast_kernel, 'forecast', [HBM] * 4 + [VMEM] * 10, [grid, grid, g...  2.64 us
    ppermute x1, starting transfers between devices, local(): lik_before = lax.ppermute(lik, 'strip', downward)  2.41 us
    ppermute x1, starting transfers between devices, local(): before = lax.ppermute(down, 'strip', downward)  2.41 us
    ppermute x1, starting transfers between devices, local(): after = lax.ppermute(up, 'strip', upward)  1.92 us
  transfers between devices with their start and end apart: 4, of which 2 were waited for; matrix products, arithmetic and copies ran while one was open for 0% of the time, Pallas kernels for 2%

profile of v2, /device:TPU:256, one launch (start us, length us, event | category | flops | bytes accessed | tf_op | source)
XLA Modules:
  0.0 58.2 jit_solution(4085495700219790375)
XLA Ops:
  0.6 1.9 %load.1 = (f32[104,256]{1,0:T(8,128)S(1)}, f32[104,256]{1,0:T(8,128)S(1)}, bf16[24,32,256]{2,1,0:T(8,128)(2,1)S(1)}, bf16[24,32,256]{2,1,0:T(8,128)(2,1)S(1)}, b...) custom-call(s32[32]{0:T(128)} %cell_hbm.3, ...), custom_call_target="tpu_custom_call" | custom-call | tf_op jit(solution)/shard_map/load/pallas_call | solution.py:312
  2.5 1.9 %collective-permute-start.1 = (f32[104,256]{1,0:T(8,128)S(1)}, f32[104,256]{1,0:T(8,128)S(1)}, u32[]{:S(2)}, u32[]{:S(2)}) collective-permute-start(f32[104,256]{1,0:T(8,128)S(1)} %get-tuple-element.16.up_ref), channel_id=1, source_target_pairs={{1,0},{2,1},{3,2},{4,3},{5,4},{6,5},{7,6},{8,7},{9,8},{10,9},{11,1... | collective-permute-start | bytes 319496 | tf_op jit(solution)/shard_map/ppermute | solution.py:320
  4.4 2.4 %collective-permute-start = (f32[104,256]{1,0:T(8,128)S(1)}, f32[104,256]{1,0:T(8,128)S(1)}, u32[]{:S(2)}, u32[]{:S(2)}) collective-permute-start(f32[104,256]{1,0:T(8,128)S(1)} %get-tuple-element.15.down_ref), channel_id=1, source_target_pairs={{0,1},{1,2},{2,3},{3,4},{4,5},{5,6},{6,7},{7,8},{8,9},{9,10},{10,1... | collective-permute-start | bytes 319496 | tf_op jit(solution)/shard_map/ppermute | solution.py:319
  6.8 0.0 collective-permute-done.1.after_ref
  6.8 4.8 %collective-permute-done.before_ref = f32[104,256]{1,0:T(8,128)S(1)} collective-permute-done((f32[104,256]{1,0:T(8,128)S(1)}, f32[104,256]{1,0:T(8,128)S(1)}, u32[]{:S(2)}, u32[]{:S(2)}) %collective-permute-start) | collective-permute-done | bytes 106528 | tf_op jit(solution)/shard_map/ppermute | solution.py:319
  11.7 2.6 %forecast.1 = (f32[2,768,128]{2,1,0:T(8,128)S(1)}, f32[2,768,128]{2,1,0:T(8,128)S(1)}, f32[2,768,128]{2,1,0:T(8,128)S(1)}, f32[24,128]{1,0:T(8,128)S(1)}) custom-call(s32[32]{0:T(128)} %cell_hbm.3, s32[1,32]{1,0:T(1,128)} %bitcast.11, f32[1,32]{1,0:T(1,128)} %bitcast.12, f32[1,32]{1,0:T(1,128)} %bitcast.13, ...), custom_call_target="tpu_custom_call" | custom-call | tf_op jit(solution)/shard_map/forecast/pallas_call | solution.py:323
  14.3 1.9 %collective-permute-start.3 = (f32[24,128]{1,0:T(8,128)S(1)}, f32[24,128]{1,0:T(8,128)S(1)}, u32[]{:S(2)}, u32[]{:S(2)}) collective-permute-start(f32[24,128]{1,0:T(8,128)S(1)} %get-tuple-element.23.lik_ref), channel_id=1, source_target_pairs={{1,0},{2,1},{3,2},{4,3},{5,4},{6,5},{7,6},{8,7},{9,8},{10,9},{11,1... | collective-permute-start | bytes 36872 | tf_op jit(solution)/shard_map/ppermute | solution.py:331
  16.2 2.4 %collective-permute-start.2 = (f32[24,128]{1,0:T(8,128)S(1)}, f32[24,128]{1,0:T(8,128)S(1)}, u32[]{:S(2)}, u32[]{:S(2)}) collective-permute-start(f32[24,128]{1,0:T(8,128)S(1)} %get-tuple-element.23.lik_ref), channel_id=1, source_target_pairs={{0,1},{1,2},{2,3},{3,4},{4,5},{5,6},{6,7},{7,8},{8,9},{9,10},{10,1... | collective-permute-start | bytes 36872 | tf_op jit(solution)/shard_map/ppermute | solution.py:330
  18.7 1.1 %taper.1.taper_ref = bf16[32,256,256]{2,1,0:T(8,128)(2,1)S(1)} custom-call(f32[104,256]{1,0:T(8,128)S(1)} %get-tuple-element.15.down_ref, f32[104,256]{1,0:T(8,128)S(1)} %collective-permute-done.before_ref, f32[104,256]{1,0:T(8,128)S(1)} %collective-permute-done.1.after_ref), custom_call_target="tpu_custom_call" | custom-call | flops 8388608 | bytes 4194304 | tf_op jit(solution)/shard_map/taper/pallas_call | solution.py:332
  19.7 0.0 collective-permute-done.3.after_ref
  19.7 2.7 %collective-permute-done.2.before_ref = f32[24,128]{1,0:T(8,128)S(1)} collective-permute-done((f32[24,128]{1,0:T(8,128)S(1)}, f32[24,128]{1,0:T(8,128)S(1)}, u32[]{:S(2)}, u32[]{:S(2)}) %collective-permute-start.2) | collective-permute-done | bytes 12320 | tf_op jit(solution)/shard_map/ppermute | solution.py:330
  22.5 1.1 %weights.1 = f32[256,128]{1,0:T(8,128)S(1)} custom-call(bf16[32,256,256]{2,1,0:T(8,128)(2,1)S(1)} %taper.1.taper_ref, f32[24,128]{1,0:T(8,128)S(1)} %get-tuple-element.23.lik_ref, f32[24,128]{1,0:T(8,128)S(1)} %collective-permute-done.2.before_ref, f32[24,128]{1,0:T(8,128)S(1)} %collective-permute-done.3.after_ref, ...), custom_call_target="tpu_custom_call" | custom-call | tf_op jit(solution)/shard_map/weights/pallas_call | solution.py:335
  23.6 20.0 %all_to_all.10 = f32[32,8,128]{2,1,0:T(8,128)S(1)} all-to-all(f32[32,8,128]{2,1,0:T(8,128)S(1)} %bitcast.7), channel_id=1, replica_groups=mesh['dom'=32,'strip'=16] {'dom'}, dimensions={0} | all-to-all | bytes 262144 | tf_op jit(solution)/shard_map/all_to_all | solution.py:339
  43.6 0.1 combine.1
  43.7 13.9 %all_to_all.11 = f32[32,8,128]{2,1,0:T(8,128)S(1)} all-to-all(f32[32,8,128]{2,1,0:T(8,128)S(1)} %bitcast.10), channel_id=1, replica_groups=mesh['dom'=32,'strip'=16] {'dom'}, dimensions={0} | all-to-all | bytes 262144 | tf_op jit(solution)/shard_map/all_to_all | solution.py:343
  57.6 0.7 %spread.1 = (f32[32,256]{1,0:T(8,128)}, f32[32,256]{1,0:T(8,128)}, f32[32,256]{1,0:T(8,128)}) custom-call(f32[256,128]{1,0:T(8,128)S(1)} %bitcast.8), custom_call_target="tpu_custom_call" | custom-call | tf_op jit(solution)/shard_map/spread/pallas_call | solution.py:345
Async XLA Ops:
  2.5 4.3 %collective-permute-start.1 = (f32[104,256]{1,0:T(8,128)S(1)}, f32[104,256]{1,0:T(8,128)S(1)}, u32[]{:S(2)}, u32[]{:S(2)}) collective-permute-start(f32[104,256]{1,0:T(8,128)S(1)} %get-tuple-element.16.up_ref), channel_id=1, source_target_pairs={{1,0},{2,1},{3,2},{4,3},{5,4},{6,5},{7,6},{8,7},{9,8},{10,9},{11,1... | collective-permute-start | bytes 319496 | tf_op jit(solution)/shard_map/ppermute | solution.py:320
  4.4 7.2 %collective-permute-start = (f32[104,256]{1,0:T(8,128)S(1)}, f32[104,256]{1,0:T(8,128)S(1)}, u32[]{:S(2)}, u32[]{:S(2)}) collective-permute-start(f32[104,256]{1,0:T(8,128)S(1)} %get-tuple-element.15.down_ref), channel_id=1, source_target_pairs={{0,1},{1,2},{2,3},{3,4},{4,5},{5,6},{6,7},{7,8},{8,9},{9,10},{10,1... | collective-permute-start | bytes 319496 | tf_op jit(solution)/shard_map/ppermute | solution.py:319
  14.3 5.4 %collective-permute-start.3 = (f32[24,128]{1,0:T(8,128)S(1)}, f32[24,128]{1,0:T(8,128)S(1)}, u32[]{:S(2)}, u32[]{:S(2)}) collective-permute-start(f32[24,128]{1,0:T(8,128)S(1)} %get-tuple-element.23.lik_ref), channel_id=1, source_target_pairs={{1,0},{2,1},{3,2},{4,3},{5,4},{6,5},{7,6},{8,7},{9,8},{10,9},{11,1... | collective-permute-start | bytes 36872 | tf_op jit(solution)/shard_map/ppermute | solution.py:331
  16.2 6.2 %collective-permute-start.2 = (f32[24,128]{1,0:T(8,128)S(1)}, f32[24,128]{1,0:T(8,128)S(1)}, u32[]{:S(2)}, u32[]{:S(2)}) collective-permute-start(f32[24,128]{1,0:T(8,128)S(1)} %get-tuple-element.23.lik_ref), channel_id=1, source_target_pairs={{0,1},{1,2},{2,3},{3,4},{4,5},{5,6},{6,7},{7,8},{8,9},{9,10},{10,1... | collective-permute-start | bytes 36872 | tf_op jit(solution)/shard_map/ppermute | solution.py:330

commit v3 on v2

--- a/solution.py
+++ b/solution.py
@@ -117,7 +117,8 @@
         row = ((cell >> 8) & (ROWS - 1)).astype(f32)
         column = (cell & (COLS - 1)).astype(f32)
         reach = radius_ref[k].astype(f32)
-        entry = jnp.where(lane == 0, row, jnp.where(lane == 1, column, jnp.where(lane == 2, reach * reach, 1.0)))
+        strip = (cell >> 13).astype(f32)
+        entry = jnp.where(lane == 0, row, jnp.where(lane == 1, column, jnp.where(lane == 2, reach * reach, strip)))
         up_ref[HALO + k : HALO + k + 1] = entry
         down_ref[HALO + k : HALO + k + 1] = entry
     copies[9].wait()
@@ -135,15 +136,19 @@
     for copy in copies:
         copy.start()
     third = lambda ref, i: ref[i * MEMBERS : (i + 1) * MEMBERS]
-    has_after = after_ref[HALO : HALO + 1, 3:4]
-    flow_before = third(before_ref, 0)
+    strip_of = lambda ref: ref[HALO : HALO + 1, 3:4]
+    has_before = strip_of(before_ref) == strip_of(down_ref) - 1.0
+    has_after = strip_of(after_ref) == strip_of(down_ref) + 1.0
+    flow_before = jnp.where(has_before, third(before_ref, 0), 0.0)
     depth_0 = third(up_ref, 0) + advection * flow_before
-    next_before = third(before_ref, 1) - third(before_ref, 2) * depth_0
-    depth_32 = (third(after_ref, 0) + advection * third(down_ref, 0)) * has_after
+    next_before = jnp.where(has_before, third(before_ref, 1) - third(before_ref, 2) * depth_0, 0.0)
+    depth_32 = jnp.where(has_after, third(after_ref, 0) + advection * third(down_ref, 0), 0.0)
     flow_31 = third(down_ref, 1) - third(down_ref, 2) * depth_32
-    late_32 = (
-        depth_32 * third(after_ref, 1) + diffusion * column_spread(depth_32) + third(after_ref, 2) + advection * flow_31
-    ) * has_after
+    late_32 = jnp.where(
+        has_after,
+        depth_32 * third(after_ref, 1) + diffusion * column_spread(depth_32) + third(after_ref, 2) + advection * flow_31,
+        0.0,
+    )
     edge_ref[0] = flow_before
     edge_ref[1] = next_before
     edge_ref[2] = depth_32
@@ -202,7 +207,8 @@
     near, rows = [], []
     for shift, entry in zip((-ROWS, 0, ROWS), entries):
         gap = column_at - entry[:, 1:2]
-        near.append(entry[:, 2:3] - gap * gap)
+        beside = entry[:, 3:4] == entries[1][:, 3:4] + float(shift // ROWS)
+        near.append(jnp.where(beside, entry[:, 2:3], 0.0) - gap * gap)
         rows.append(jnp.broadcast_to(entry[:, 0:1] + float(shift), (SENS, COLS)))
     blank = jnp.zeros((SENS, COLS), bf16)
 
@@ -304,8 +310,8 @@
 ):
     strips = lax.axis_size("strip")
     groups = lax.axis_size("dom")
-    downward = [(i, i + 1) for i in range(strips - 1)]
-    upward = [(i + 1, i) for i in range(strips - 1)]
+    downward = [(i, (i + 1) % strips) for i in range(strips)]
+    upward = [((i + 1) % strips, i) for i in range(strips)]
     stay = lambda values: pltpu.with_memory_space_constraint(values, pltpu.HBM)
     fields = [stay(f) for f in (surface, discharge, storage, exchange, depth_perturbation, flow_perturbation)]
     sensor_cell = stay(sensor_cell)

time: 58.5 us -> 58.9 us (level)
  the two profiles are of different devices: /device:TPU:256 before, /device:TPU:8 now
where the time goes in v3:
time: 58.9 us; the launch traced here: 58.7 us
  blocking collectives  33.5 us (57%)
  starting transfers between devices  9.01 us (15%)
  waiting for transfers between devices  8.07 us (14%)
  Pallas kernels  7.45 us (13%)
  between operations  0.69 us (1%)
    all_to_all x1, blocking collectives, local(): lax.all_to_all(parts.reshape(groups, 8, LANES), 'dom', 0, 0, tiled=True)  19.6 us
    all_to_all x1, blocking collectives, local(): lax.all_to_all(rows.reshape(groups, 8, LANES), 'dom', 0, 0, tiled=True)  13.9 us
    ppermute x1, starting transfers between devices, local(): after = lax.ppermute(up, 'strip', upward)  8.49 us
    ppermute x1, waiting for transfers between devices, local(): before = lax.ppermute(down, 'strip', downward)  3.05 us
    ppermute x1, waiting for transfers between devices, local(): lik_before = lax.ppermute(lik, 'strip', downward)  2.73 us
    pallas_call x1, Pallas kernels, local(): call(forecast_kernel, 'forecast', [HBM] * 4 + [VMEM] * 10, [grid, grid, g...  2.65 us
    ppermute x1, waiting for transfers between devices, local(): after = lax.ppermute(up, 'strip', upward)  2.29 us
    pallas_call x1, Pallas kernels, local(): call(load_kernel, 'load', [HBM] * 8, [((MESSAGE, COLS), f32)] * 2 + [(fie...  1.86 us
  transfers between devices with their start and end apart: 4, of which 3 were waited for; matrix products, arithmetic and copies ran while one was open for 0% of the time, Pallas kernels for 2%

profile of v3, /device:TPU:8, one launch (start us, length us, event | category | flops | bytes accessed | tf_op | source)
XLA Modules:
  0.0 58.7 jit_solution(17557469526043098240)
XLA Ops:
  0.6 1.9 %load.1 = (f32[104,256]{1,0:T(8,128)S(1)}, f32[104,256]{1,0:T(8,128)S(1)}, bf16[24,32,256]{2,1,0:T(8,128)(2,1)S(1)}, bf16[24,32,256]{2,1,0:T(8,128)(2,1)S(1)}, b...) custom-call(s32[32]{0:T(128)} %cell_hbm.3, ...), custom_call_target="tpu_custom_call" | custom-call | tf_op jit(solution)/shard_map/load/pallas_call | solution.py:318
  2.5 8.5 %collective-permute-start.1 = (f32[104,256]{1,0:T(8,128)S(1)}, f32[104,256]{1,0:T(8,128)S(1)}, u32[]{:S(2)}, u32[]{:S(2)}) collective-permute-start(f32[104,256]{1,0:T(8,128)S(1)} %get-tuple-element.16.up_ref), channel_id=1, source_target_pairs={{1,0},{2,1},{3,2},{4,3},{5,4},{6,5},{7,6},{8,7},{9,8},{10,9},{11,1... | collective-permute-start | bytes 319496 | tf_op jit(solution)/shard_map/ppermute | solution.py:326
  11.0 0.0 collective-permute-start
  11.0 2.3 %collective-permute-done.1.after_ref = f32[104,256]{1,0:T(8,128)S(1)} collective-permute-done((f32[104,256]{1,0:T(8,128)S(1)}, f32[104,256]{1,0:T(8,128)S(1)}, u32[]{:S(2)}, u32[]{:S(2)}) %collective-permute-start.1) | collective-permute-done | bytes 106528 | tf_op jit(solution)/shard_map/ppermute | solution.py:326
  13.3 3.0 %collective-permute-done.before_ref = f32[104,256]{1,0:T(8,128)S(1)} collective-permute-done((f32[104,256]{1,0:T(8,128)S(1)}, f32[104,256]{1,0:T(8,128)S(1)}, u32[]{:S(2)}, u32[]{:S(2)}) %collective-permute-start) | collective-permute-done | bytes 106528 | tf_op jit(solution)/shard_map/ppermute | solution.py:325
  16.3 2.7 %forecast.1 = (f32[2,768,128]{2,1,0:T(8,128)S(1)}, f32[2,768,128]{2,1,0:T(8,128)S(1)}, f32[2,768,128]{2,1,0:T(8,128)S(1)}, f32[24,128]{1,0:T(8,128)S(1)}) custom-call(s32[32]{0:T(128)} %cell_hbm.3, s32[1,32]{1,0:T(1,128)} %bitcast.11, f32[1,32]{1,0:T(1,128)} %bitcast.12, f32[1,32]{1,0:T(1,128)} %bitcast.13, ...), custom_call_target="tpu_custom_call" | custom-call | tf_op jit(solution)/shard_map/forecast/pallas_call | solution.py:329
  19.0 0.0 collective-permute-start.3
  19.0 0.5 collective-permute-start.2
  19.5 1.1 %taper.1.taper_ref = bf16[32,256,256]{2,1,0:T(8,128)(2,1)S(1)} custom-call(f32[104,256]{1,0:T(8,128)S(1)} %get-tuple-element.15.down_ref, f32[104,256]{1,0:T(8,128)S(1)} %collective-permute-done.before_ref, f32[104,256]{1,0:T(8,128)S(1)} %collective-permute-done.1.after_ref), custom_call_target="tpu_custom_call" | custom-call | flops 8388608 | bytes 4194304 | tf_op jit(solution)/shard_map/taper/pallas_call | solution.py:338
  20.6 0.0 collective-permute-done.3.after_ref
  20.6 2.7 %collective-permute-done.2.before_ref = f32[24,128]{1,0:T(8,128)S(1)} collective-permute-done((f32[24,128]{1,0:T(8,128)S(1)}, f32[24,128]{1,0:T(8,128)S(1)}, u32[]{:S(2)}, u32[]{:S(2)}) %collective-permute-start.2) | collective-permute-done | bytes 12320 | tf_op jit(solution)/shard_map/ppermute | solution.py:336
  23.4 1.1 %weights.1 = f32[256,128]{1,0:T(8,128)S(1)} custom-call(bf16[32,256,256]{2,1,0:T(8,128)(2,1)S(1)} %taper.1.taper_ref, f32[24,128]{1,0:T(8,128)S(1)} %get-tuple-element.23.lik_ref, f32[24,128]{1,0:T(8,128)S(1)} %collective-permute-done.2.before_ref, f32[24,128]{1,0:T(8,128)S(1)} %collective-permute-done.3.after_ref, ...), custom_call_target="tpu_custom_call" | custom-call | tf_op jit(solution)/shard_map/weights/pallas_call | solution.py:341
  24.5 19.6 %all_to_all.10 = f32[32,8,128]{2,1,0:T(8,128)S(1)} all-to-all(f32[32,8,128]{2,1,0:T(8,128)S(1)} %bitcast.7), channel_id=1, replica_groups=mesh['dom'=32,'strip'=16] {'dom'}, dimensions={0} | all-to-all | bytes 262144 | tf_op jit(solution)/shard_map/all_to_all | solution.py:345
  44.1 0.1 combine.1
  44.2 13.9 %all_to_all.11 = f32[32,8,128]{2,1,0:T(8,128)S(1)} all-to-all(f32[32,8,128]{2,1,0:T(8,128)S(1)} %bitcast.10), channel_id=1, replica_groups=mesh['dom'=32,'strip'=16] {'dom'}, dimensions={0} | all-to-all | bytes 262144 | tf_op jit(solution)/shard_map/all_to_all | solution.py:349
  58.0 0.7 %spread.1 = (f32[32,256]{1,0:T(8,128)}, f32[32,256]{1,0:T(8,128)}, f32[32,256]{1,0:T(8,128)}) custom-call(f32[256,128]{1,0:T(8,128)S(1)} %bitcast.8), custom_call_target="tpu_custom_call" | custom-call | tf_op jit(solution)/shard_map/spread/pallas_call | solution.py:351
Async XLA Ops:
  2.5 10.8 %collective-permute-start.1 = (f32[104,256]{1,0:T(8,128)S(1)}, f32[104,256]{1,0:T(8,128)S(1)}, u32[]{:S(2)}, u32[]{:S(2)}) collective-permute-start(f32[104,256]{1,0:T(8,128)S(1)} %get-tuple-element.16.up_ref), channel_id=1, source_target_pairs={{1,0},{2,1},{3,2},{4,3},{5,4},{6,5},{7,6},{8,7},{9,8},{10,9},{11,1... | collective-permute-start | bytes 319496 | tf_op jit(solution)/shard_map/ppermute | solution.py:326
  11.0 5.3 %collective-permute-start = (f32[104,256]{1,0:T(8,128)S(1)}, f32[104,256]{1,0:T(8,128)S(1)}, u32[]{:S(2)}, u32[]{:S(2)}) collective-permute-start(f32[104,256]{1,0:T(8,128)S(1)} %get-tuple-element.15.down_ref), channel_id=1, source_target_pairs={{0,1},{1,2},{2,3},{3,4},{4,5},{5,6},{6,7},{7,8},{8,9},{9,10},{10,1... | collective-permute-start | bytes 319496 | tf_op jit(solution)/shard_map/ppermute | solution.py:325
  19.0 1.6 %collective-permute-start.3 = (f32[24,128]{1,0:T(8,128)S(1)}, f32[24,128]{1,0:T(8,128)S(1)}, u32[]{:S(2)}, u32[]{:S(2)}) collective-permute-start(f32[24,128]{1,0:T(8,128)S(1)} %get-tuple-element.23.lik_ref), channel_id=1, source_target_pairs={{1,0},{2,1},{3,2},{4,3},{5,4},{6,5},{7,6},{8,7},{9,8},{10,9},{11,1... | collective-permute-start | bytes 36872 | tf_op jit(solution)/shard_map/ppermute | solution.py:337
  19.0 4.3 %collective-permute-start.2 = (f32[24,128]{1,0:T(8,128)S(1)}, f32[24,128]{1,0:T(8,128)S(1)}, u32[]{:S(2)}, u32[]{:S(2)}) collective-permute-start(f32[24,128]{1,0:T(8,128)S(1)} %get-tuple-element.23.lik_ref), channel_id=1, source_target_pairs={{0,1},{1,2},{2,3},{3,4},{4,5},{5,6},{6,7},{7,8},{8,9},{9,10},{10,1... | collective-permute-start | bytes 36872 | tf_op jit(solution)/shard_map/ppermute | solution.py:336

commit v4 on v2

v4 whole, which is shorter than its diff:
```python
import jax
import jax.numpy as jnp
from jax import lax
from jax.experimental import pallas as pl
from jax.experimental.pallas import tpu as pltpu
from jax.sharding import PartitionSpec as P

advection = 0.4
gravity = 0.5
diffusion = 0.15
friction = 0.3
drainage = 0.1

MEMBERS = 24
ROWS = 32
COLS = 256
SENS = 32
LANES = 128
SAMPLED = 6 * MEMBERS
SLOPE = SAMPLED + MEMBERS
ENTRY = SLOPE + MEMBERS
ACROSS = ENTRY + SENS
MESSAGE = ACROSS + 8

f32 = jnp.float32
bf16 = jnp.bfloat16


def sides(left_half, right_half):
    lane = lax.broadcasted_iota(jnp.int32, left_half.shape, 1)
    first, last = lane == 0, lane == LANES - 1
    left_back, right_back = pltpu.roll(left_half, 1, 1), pltpu.roll(right_half, 1, 1)
    left_on, right_on = pltpu.roll(left_half, LANES - 1, 1), pltpu.roll(right_half, LANES - 1, 1)
    return (
        jnp.where(first, left_half, left_back) + jnp.where(last, right_on, left_on),
        jnp.where(first, left_back, right_back) + jnp.where(last, right_half, right_on),
    )


def spread(field):
    return [diffusion * (around - 2.0 * here) for around, here in zip(sides(*field), field)]


def halves(values):
    return [values[:, :LANES], values[:, LANES:]]


def each(function, *rows):
    return [function(*parts) for parts in zip(*rows)]


def put(ref, slot, row):
    for h in range(2):
        ref[(2 * slot + h) * MEMBERS : (2 * slot + h + 1) * MEMBERS] = row[h]


def get(ref, slot):
    return [ref[(2 * slot + h) * MEMBERS : (2 * slot + h + 1) * MEMBERS] for h in range(2)]


def forecast_kernel(
    cell_hbm, radii_hbm, cells_hbm, radius_hbm, observed_hbm, sigma_hbm,
    surface_hbm, discharge_hbm, storage_hbm, exchange_hbm, depth_noise_hbm, flow_noise_hbm,
    own_ref, along_ref, across_ref, far_ref, extra_ref, depth_ref, flow_ref, stored_ref,
    surface_ref, discharge_ref, storage_ref, exchange_ref, depth_noise_ref, flow_noise_ref,
    first_ref, last_ref, slope_ref, cell_ref, radii_ref, cells_ref, radius_ref, observed_ref, sigma_ref, sems,
):
    pairs = [
        (surface_hbm, surface_ref), (discharge_hbm, discharge_ref), (storage_hbm, storage_ref),
        (depth_noise_hbm.at[0], depth_noise_ref.at[0]), (flow_noise_hbm.at[0], flow_noise_ref.at[0]),
        (depth_noise_hbm.at[1], depth_noise_ref.at[1]), (flow_noise_hbm.at[1], flow_noise_ref.at[1]),
        (exchange_hbm, exchange_ref), (cell_hbm, cell_ref), (radii_hbm, radii_ref), (cells_hbm, cells_ref), (radius_hbm, radius_ref),
        (observed_hbm, observed_ref), (sigma_hbm, sigma_ref),
    ]
    copies = [pltpu.make_async_copy(source, target, sems.at[i]) for i, (source, target) in enumerate(pairs)]
    for copy in copies:
        copy.start()

    def keep(scratch, slot, rows):
        flat = rows.reshape(MEMBERS * 8, COLS)
        scratch[slot, 0] = flat[:, :LANES]
        scratch[slot, 1] = flat[:, LANES:]

    def take(ref, lead, slot):
        copies[slot].wait()
        keep(first_ref, slot, ref[lead + (slice(None), slice(0, 16), slice(None))].astype(f32)[:, :8])
        if slot != 5:
            keep(last_ref, slot, ref[lead + (slice(None), slice(16, 32), slice(None))].astype(f32)[:, 8:])

    take(surface_ref, (), 0)
    take(discharge_ref, (), 1)
    take(storage_ref, (), 2)
    take(depth_noise_ref, (0,), 3)
    take(flow_noise_ref, (0,), 4)
    take(depth_noise_ref, (1,), 5)
    take(flow_noise_ref, (1,), 6)
    for copy in copies[7:]:
        copy.wait()

    def row_of(ref, slot, row):
        return [ref[slot, h, pl.ds(row, MEMBERS, stride=8)] for h in range(2)]

    def step_one(surface, flow, flow_below, stored, rate, noise):
        return each(
            lambda s, q, b, t, e, n, d: s - advection * (q - b) + d - e * (s - t) + n,
            surface, flow, flow_below, stored, rate, noise, spread(surface),
        )

    nothing = [jnp.zeros((MEMBERS, LANES), f32)] * 2
    rate = halves(exchange_ref[...].astype(f32))
    rate_0, rate_1, rate_31 = [[r[i : i + 1] for r in rate] for i in (0, 1, ROWS - 1)]
    surface_0, surface_1 = row_of(first_ref, 0, 0), row_of(first_ref, 0, 1)
    flow_0, flow_1 = row_of(first_ref, 1, 0), row_of(first_ref, 1, 1)
    stored_0, stored_1 = row_of(first_ref, 2, 0), row_of(first_ref, 2, 1)
    depth_0 = step_one(surface_0, flow_0, nothing, stored_0, rate_0, row_of(first_ref, 3, 0))
    depth_1 = step_one(surface_1, flow_1, flow_0, stored_1, rate_1, row_of(first_ref, 3, 1))
    stored_next = each(lambda s, t, e: (1.0 - drainage) * t + e * (s - t), surface_0, stored_0, rate_0)
    inverse_0 = each(lambda q: 1.0 / (1.0 + friction * jnp.abs(q)), flow_0)
    flow_part = each(
        lambda q, d, n, i: (q - gravity * d + n) * i, flow_0, depth_1, row_of(first_ref, 4, 0), inverse_0
    )
    up_ref, down_ref = own_ref.at[0], own_ref.at[1]
    put(up_ref, 0, depth_0)
    put(up_ref, 1, each(lambda e, i: 1.0 - e - (advection * gravity) * i, rate_0, inverse_0))
    put(up_ref, 2, each(lambda e, t, n, q: e * t + n - advection * q, rate_0, stored_next, row_of(first_ref, 5, 0), flow_part))
    flow_31 = row_of(last_ref, 1, 7)
    depth_31 = step_one(
        row_of(last_ref, 0, 7), flow_31, row_of(last_ref, 1, 6), row_of(last_ref, 2, 7), rate_31, row_of(last_ref, 3, 7)
    )
    inverse_31 = each(lambda q: 1.0 / (1.0 + friction * jnp.abs(q)), flow_31)
    put(down_ref, 0, flow_31)
    put(down_ref, 1, each(lambda q, d, n, i: (q + gravity * d + n) * i, flow_31, depth_31, row_of(last_ref, 4, 7), inverse_31))
    put(down_ref, 2, each(lambda i: gravity * i, inverse_31))
    put(far_ref, 0, flow_31)
    put(extra_ref, 0, each(lambda i: gravity * i, inverse_0))
    put(extra_ref, 1, each(lambda q, i, d: q + gravity * i * d, flow_part, inverse_0, depth_0))
    put(extra_ref, 2, row_of(first_ref, 6, 0))
    put(extra_ref, 3, row_of(last_ref, 6, 7))
    put(extra_ref, 6, each(lambda e, z: e + z, rate_0, nothing))
    for h in range(2):
        slope_ref[h] = (advection * advection * gravity) * inverse_0[h]

    row = lax.broadcasted_iota(jnp.int32, (ROWS, LANES), 0)

    def member(p, carry):
        depth, flow, stored = [halves(ref[p].astype(f32)) for ref in (surface_ref, discharge_ref, storage_ref)]
        for step in range(2):
            depth_noise, flow_noise = [halves(ref[step, p].astype(f32)) for ref in (depth_noise_ref, flow_noise_ref)]
            beside = sides(*depth)
            for h in range(2):
                flow_below = jnp.where(row == 0, 0.0, pltpu.roll(flow[h], 1, 0))
                inflow = rate[h] * (depth[h] - stored[h])
                depth_next = (
                    (1.0 - 2.0 * diffusion) * depth[h] + diffusion * beside[h]
                    - advection * (flow[h] - flow_below) - inflow + depth_noise[h]
                )
                stored[h] = (1.0 - drainage) * stored[h] + inflow
                depth_above = jnp.where(row == ROWS - 1, 0.0, pltpu.roll(depth_next, ROWS - 1, 0))
                flow[h] = (flow[h] - gravity * (depth_above - depth_next) + flow_noise[h]) * (
                    1.0 / (1.0 + friction * jnp.abs(flow[h]))
                )
                depth[h] = depth_next
                if step == 0:
                    edge = pl.ds(pl.multiple_of(p * 8, 8), 8)
                    first_ref[7, h, edge] = flow[h][:8]
                    last_ref[7, h, edge] = flow[h][ROWS - 8 :]
        at = pl.ds(pl.multiple_of(p * ROWS, ROWS), ROWS)
        for ref, value in ((depth_ref, depth), (flow_ref, flow), (stored_ref, stored)):
            for h in range(2):
                ref[h, at] = value[h]
        return carry

    lax.fori_loop(0, MEMBERS, member, 0, unroll=4)
    put(extra_ref, 4, each(lambda q: 1.0 / (1.0 + friction * jnp.abs(q)), row_of(first_ref, 7, 1)))
    put(extra_ref, 5, each(lambda q: 1.0 / (1.0 + friction * jnp.abs(q)), row_of(last_ref, 7, 6)))

    lane = lax.broadcasted_iota(jnp.int32, (MEMBERS, LANES), 1)
    one_lane = lax.broadcasted_iota(jnp.int32, (1, LANES), 1)
    sampled, slope = jnp.zeros((MEMBERS, LANES), f32), jnp.zeros((MEMBERS, LANES), f32)
    for k in range(SENS):
        cell = cell_ref[k]
        half, line, turn = (cell >> 7) & 1, (cell >> 8) & (ROWS - 1), (k - cell) & (LANES - 1)
        found = pltpu.roll(depth_ref[half, pl.ds(line, MEMBERS, stride=ROWS)], turn, 1)
        sampled = jnp.where(lane == k, found, sampled)
        slope = jnp.where(lane == k, pltpu.roll(slope_ref[half], turn, 1), slope)
        place, column = line.astype(f32), (cell & (COLS - 1)).astype(f32)
        strip = (cell >> 13).astype(f32)
        reach = radii_ref[k].astype(f32)
        entry = jnp.where(
            one_lane == 0, place, jnp.where(one_lane == 1, column, jnp.where(one_lane == 2, reach * reach, strip))
        )
        for i in range(2):
            own_ref[i, ENTRY + k : ENTRY + k + 1] = entry
    cells = cells_ref[...]
    place = ((cells >> 8) & (ROWS - 1)).astype(f32)
    reach = radius_ref[...].astype(f32)
    facts = [
        place, (cells & (COLS - 1)).astype(f32), reach * reach, (cells >> 13).astype(f32),
        observed_ref[...], sigma_ref[...], jnp.zeros((2, SENS), f32),
    ]
    facts = jnp.concatenate([jnp.concatenate(facts, axis=0), jnp.ones((8, LANES - SENS), f32)], axis=1)
    slope = jnp.where(facts[0:1] == 1.0, slope, 0.0)
    for i in range(2):
        own_ref[i, SAMPLED:SLOPE] = sampled
        own_ref[i, SLOPE:ENTRY] = slope
        own_ref[i, ACROSS:MESSAGE] = facts
    odd = (cell_ref[0] >> 13) & 1
    along_ref[...] = own_ref[odd]
    across_ref[0] = own_ref[1 - odd]


def join_kernel(across_ref, arrived_ref, joined_ref):
    del across_ref
    joined_ref[1] = arrived_ref[...]


def finish_kernel(
    own_ref, extra_ref, arrived_ref, far_ref, joined_ref, depth_in, flow_in, stored_in,
    out_ref, depth_ref, flow_ref, stored_ref,
    before_ref, after_ref, near_ref, taper_ref, weight_ref,
):
    del depth_in, flow_in, stored_in
    up_ref, down_ref = own_ref.at[0], own_ref.at[1]
    strip = own_ref[0, ACROSS + 3 : ACROSS + 4, 0:1]
    odd = strip - 2.0 * jnp.floor(0.5 * strip) > 0.5
    before_ref[...] = jnp.where(odd, joined_ref[0], joined_ref[1])
    after_ref[...] = jnp.where(odd, joined_ref[1], joined_ref[0])
    has_before = before_ref[ACROSS + 3 : ACROSS + 4, 0:1] == strip - 1.0
    has_after = after_ref[ACROSS + 3 : ACROSS + 4, 0:1] == strip + 1.0
    keep = lambda condition, row: each(lambda v: jnp.where(condition, v, 0.0), row)

    def line(ref, row):
        return [ref[h, pl.ds(row, MEMBERS, stride=ROWS)] for h in range(2)]

    def set_line(ref, row, values):
        for h in range(2):
            ref[h, pl.ds(row, MEMBERS, stride=ROWS)] = values[h]

    back = keep(has_before, get(before_ref, 0))
    start = each(lambda d, q: d + advection * q, get(up_ref, 0), back)
    back_next = keep(has_before, each(lambda f, i, d: f - i * d, get(before_ref, 1), get(before_ref, 2), start))
    depth_0 = each(
        lambda d, c, s, k, q: d * c + s + k + advection * q,
        start, get(up_ref, 1), spread(start), get(up_ref, 2), back_next,
    )
    turn_0 = get(extra_ref, 0)
    more_1 = each(lambda i, q: (advection * advection) * i * q, turn_0, back)
    depth_1 = each(lambda d, m: d + m, line(depth_ref, 1), more_1)
    flow_0 = each(lambda f, i, q: f + advection * i * q, get(extra_ref, 1), turn_0, back)
    set_line(depth_ref, 0, depth_0)
    set_line(depth_ref, 1, depth_1)
    set_line(flow_ref, 0, each(
        lambda f, a, d, n: (f - gravity * (a - d) + n) * (1.0 / (1.0 + friction * jnp.abs(f))),
        flow_0, depth_1, depth_0, get(extra_ref, 2),
    ))
    set_line(flow_ref, 1, each(lambda f, i, m: f + gravity * i * m, line(flow_ref, 1), get(extra_ref, 4), more_1))
    set_line(stored_ref, 0, each(lambda t, e, q: t + advection * e * q, line(stored_ref, 0), get(extra_ref, 6), back))
    last = get(down_ref, 0)
    end = keep(has_after, each(lambda d, q: d + advection * q, get(after_ref, 0), last))
    flow_31 = each(lambda f, i, d: f - i * d, get(down_ref, 1), get(down_ref, 2), end)
    depth_32 = keep(has_after, each(
        lambda d, c, s, k, q: d * c + s + k + advection * q,
        end, get(after_ref, 1), spread(end), get(after_ref, 2), flow_31,
    ))
    more_31 = each(lambda i, d: advection * i * d, get(down_ref, 2), end)
    depth_31 = each(lambda d, m: d + m, line(depth_ref, ROWS - 1), more_31)
    set_line(depth_ref, ROWS - 1, depth_31)
    set_line(flow_ref, ROWS - 1, each(
        lambda f, a, d, n: (f - gravity * (a - d) + n) * (1.0 / (1.0 + friction * jnp.abs(f))),
        flow_31, depth_32, depth_31, get(extra_ref, 3),
    ))
    set_line(flow_ref, ROWS - 2, each(
        lambda f, i, m: f - gravity * i * m, line(flow_ref, ROWS - 2), get(extra_ref, 5), more_31
    ))

    lane = lax.broadcasted_iota(jnp.int32, (1, LANES), 1)
    group = lane // SENS

    def beside(ref, first, count):
        parts = (before_ref[first : first + count], ref[0, first : first + count], after_ref[first : first + count])
        parts = [parts[0], pltpu.roll(parts[1], SENS, 1), pltpu.roll(parts[2], 2 * SENS, 1)]
        return jnp.where(group == 0, parts[0], jnp.where(group == 1, parts[1], parts[2]))

    facts = beside(own_ref, ACROSS, 8)
    place, column = facts[0:1], facts[1:2]
    hit = (lax.broadcasted_iota(jnp.int32, (COLS, LANES), 0).astype(f32) == column).astype(f32)

    def sample(rows):
        left, right = [], []
        for values, wanted, in_group, pieces in rows:
            values = jnp.concatenate(values, axis=1)
            stack = []
            for _ in range(pieces):
                piece = values.astype(bf16).astype(f32)
                stack.append(piece)
                values = values - piece
            left.append(jnp.concatenate(stack, axis=0).astype(bf16))
            right.append(jnp.where((place == wanted) & (group == in_group), hit, 0.0).astype(bf16))
        total = jnp.dot(jnp.concatenate(left, axis=1), jnp.concatenate(right, axis=0), preferred_element_type=f32)
        return sum(total[i * MEMBERS : (i + 1) * MEMBERS] for i in range(1, pieces)) + total[:MEMBERS] if pieces > 1 else total

    far = each(lambda a, b: jnp.where(strip > 1.5, jnp.where(odd, a, b), 0.0), get(arrived_ref, 0), get(far_ref, 0))
    added = sample([
        (each(lambda i, d: advection * i * d, keep(has_before, get(before_ref, 2)), start), ROWS - 1.0, 0, 3),
        (depth_0, 0.0, 1, 3), (more_1, 1.0, 1, 3), (more_31, ROWS - 1.0, 1, 3),
        (depth_32, 0.0, 2, 3),
    ])
    beyond = sample([(far, 1.0, 0, 1), (last, 1.0, 2, 1)])
    known = jnp.where((place == 0.0) & (group > 0), 0.0, beside(own_ref, SAMPLED, MEMBERS))
    found = known + added + beside(own_ref, SLOPE, MEMBERS) * beyond
    real = group < 3
    misfit = (found - facts[4:5]) / jnp.where(real, facts[5:6], 1.0)
    lik = jnp.where(real, -0.5 * misfit * misfit / jnp.where(real, facts[2:3], 1.0), 0.0)
    stack = []
    rest = lik
    for _ in range(3):
        piece = rest.astype(bf16).astype(f32)
        stack.append(piece)
        rest = rest - piece
    pieces = jnp.concatenate(stack, axis=0)
    turned = pltpu.roll(pieces, 3 * SENS, 1)
    pieces = jnp.concatenate(
        [jnp.where(lane < 3 * SENS, pieces, turned), jnp.where(lane < 3 * SENS, turned, 0.0)], axis=1
    )[:, : 6 * SENS].astype(bf16)

    entries = [ref[ENTRY:ACROSS] for ref in (before_ref, down_ref, after_ref)]
    column_at = lax.broadcasted_iota(jnp.int32, (SENS, COLS), 1).astype(f32)
    lines = []
    for part, (entry, offset) in enumerate(zip(entries, (-1.0, 0.0, 1.0))):
        gap = column_at - entry[:, 1:2]
        squared = jnp.where(entry[:, 3:4] == strip + offset, entry[:, 2:3], 0.0)
        near_ref[part] = squared - gap * gap
        lines.append(jnp.broadcast_to(entry[:, 0:1] + offset * ROWS, (SENS, LANES)))

    def at_row(r, carry):
        here = r.astype(f32)
        for part in range(3):
            gap = here - lines[part]
            gap = gap * gap
            value = jnp.maximum(near_ref[part] - jnp.concatenate([gap, gap], axis=1), 0.0)
            coarse = value.astype(bf16)
            taper_ref[r, part * SENS : (part + 1) * SENS] = coarse
            taper_ref[r, (3 + part) * SENS : (4 + part) * SENS] = (value - coarse.astype(f32)).astype(bf16)
        return carry

    lax.fori_loop(0, ROWS, at_row, 0, unroll=2)

    for i in range(ROWS // 8):
        for r in range(8 * i, 8 * i + 8):
            part = jnp.dot(pieces, taper_ref[r], preferred_element_type=f32)
            weight = part[:MEMBERS] + part[MEMBERS : 2 * MEMBERS] + part[2 * MEMBERS :]
            for half in range(2):
                weight_ref[half, r * MEMBERS : (r + 1) * MEMBERS] = weight[:, half * LANES : (half + 1) * LANES]
        for half in range(2):
            weights = [weight_ref[half, pl.ds(8 * i * MEMBERS + p, 8, stride=MEMBERS)] for p in range(MEMBERS)]
            best = weights[0]
            for p in range(1, MEMBERS):
                best = jnp.maximum(best, weights[p])
            sums = [jnp.zeros((8, LANES), f32) for _ in range(4)]
            for p in range(MEMBERS):
                factor = jnp.exp(weights[p] - best)
                at = pl.ds(p * ROWS + 8 * i, 8)
                sums[0] = sums[0] + factor
                sums[1] = sums[1] + factor * depth_ref[half, at]
                sums[2] = sums[2] + factor * flow_ref[half, at]
                sums[3] = sums[3] + factor * stored_ref[half, at]
            inverse = 1.0 / sums[0]
            results = (best + jnp.log(sums[0]), sums[1] * inverse, sums[2] * inverse, sums[3] * inverse)
            for slot, result in enumerate(results):
                out_ref[pl.ds(64 * i + 2 * slot + half, 8, stride=8)] = result


def combine_kernel(groups, in_ref, out_ref):
    def quantity(slot, half):
        return in_ref[pl.ds(2 * slot + half, groups, stride=8)]

    rows = []
    totals = []
    for half in range(2):
        level = quantity(0, half)
        share = jnp.exp(level - jnp.max(level, axis=0, keepdims=True))
        totals.append((share, 1.0 / jnp.sum(share, axis=0, keepdims=True)))
    for slot in range(1, 4):
        for half in range(2):
            share, inverse = totals[half]
            rows.append(jnp.sum(share * quantity(slot, half), axis=0, keepdims=True) * inverse)
    rows.append(jnp.zeros((2, LANES), f32))
    result = jnp.concatenate(rows, axis=0)
    for copy in range(groups):
        out_ref[copy * 8 : (copy + 1) * 8] = result


def spread_kernel(in_ref, depth_ref, flow_ref, stored_ref):
    for slot, ref in enumerate((depth_ref, flow_ref, stored_ref)):
        for half in range(2):
            ref[:, half * LANES : (half + 1) * LANES] = in_ref[pl.ds(2 * slot + half, ROWS, stride=8)]


VMEM = pl.BlockSpec(memory_space=pltpu.VMEM)
HBM = pl.BlockSpec(memory_space=pltpu.HBM)


def call(kernel, name, in_specs, outs, scratch=(), aliases=None):
    return pl.pallas_call(
        kernel,
        name=name,
        in_specs=in_specs,
        out_specs=[VMEM] * len(outs),
        out_shape=[jax.ShapeDtypeStruct(shape, dtype) for shape, dtype in outs],
        scratch_shapes=list(scratch),
        input_output_aliases=aliases or {},
        compiler_params=pltpu.CompilerParams(vmem_limit_bytes=40 * 1024 * 1024),
    )


def local(
    surface, discharge, storage, exchange, depth_perturbation, flow_perturbation,
    sensor_cell, sensor_radius, observed, sensor_sigma,
):
    strips = lax.axis_size("strip")
    groups = lax.axis_size("dom")
    order = list(range(0, strips, 2)) + list(range(strips - 1, 0, -2))
    onward = [(order[i], order[(i + 1) % strips]) for i in range(strips)]
    backward = [(b, a) for a, b in onward]
    swapped = [(i, i ^ 1) for i in range(strips)]
    stay = lambda values: pltpu.with_memory_space_constraint(values, pltpu.HBM)
    as_row = lambda values: stay(values.reshape(1, SENS))
    fields = [stay(f) for f in (surface, discharge, storage, exchange, depth_perturbation, flow_perturbation)]
    grid = ((2, MEMBERS * ROWS, LANES), f32)
    message = (MESSAGE, LANES)
    edges = lambda count: ((2 * count * MEMBERS, LANES), f32)
    row_of = lambda dtype: pltpu.VMEM((1, SENS), dtype)
    own, along, across, far, extra, depth, flow, stored = call(
        forecast_kernel, "forecast", [HBM] * 12,
        [((2,) + message, f32), (message, f32), ((2,) + message, f32), edges(1), edges(7), grid, grid, grid],
        [pltpu.VMEM(field.shape, field.dtype) for field in fields]
        + [
            pltpu.VMEM((8, 2, MEMBERS * 8, LANES), f32), pltpu.VMEM((8, 2, MEMBERS * 8, LANES), f32),
            pltpu.VMEM((2, MEMBERS, LANES), f32), pltpu.SMEM((SENS,), jnp.int32), pltpu.SMEM((SENS,), jnp.int32),
            row_of(jnp.int32), row_of(jnp.int32),
            row_of(f32), row_of(f32), pltpu.SemaphoreType.DMA((14,)),
        ],
    )(
        stay(sensor_cell), stay(sensor_radius), as_row(sensor_cell), as_row(sensor_radius), as_row(observed),
        as_row(sensor_sigma), *fields,
    )
    arrived = lax.ppermute(along, "strip", backward)
    far = lax.ppermute(far, "strip", onward)
    (joined,) = call(join_kernel, "join", [VMEM] * 2, [((2,) + message, f32)], aliases={0: 0})(across, arrived)
    joined = lax.ppermute(joined, "strip", swapped)
    parts, depth, flow, stored = call(
        finish_kernel, "finish", [VMEM] * 8, [((groups * 8, LANES), f32), grid, grid, grid],
        [
            pltpu.VMEM(message, f32), pltpu.VMEM(message, f32), pltpu.VMEM((3, SENS, COLS), f32),
            pltpu.VMEM((ROWS, 6 * SENS, COLS), bf16), pltpu.VMEM((2, ROWS * MEMBERS, LANES), f32),
        ],
        aliases={5: 1, 6: 2, 7: 3},
    )(own, extra, arrived, far, joined, depth, flow, stored)
    shared = lax.all_to_all(parts.reshape(groups, 8, LANES), "dom", 0, 0, tiled=True)
    (rows,) = call(
        lambda *refs: combine_kernel(groups, *refs), "combine", [VMEM], [((groups * 8, LANES), f32)],
    )(shared.reshape(groups * 8, LANES))
    whole = lax.all_to_all(rows.reshape(groups, 8, LANES), "dom", 0, 0, tiled=True)
    return tuple(
        call(spread_kernel, "spread", [VMEM], [((ROWS, COLS), f32)] * 3)(whole.reshape(groups * 8, LANES))
    )


def solution(mesh):
    return jax.shard_map(
        local,
        mesh=mesh,
        in_specs=(
            P("dom", "strip", None),
            P("dom", "strip", None),
            P("dom", "strip", None),
            P("strip", None),
            P(None, "dom", "strip", None),
            P(None, "dom", "strip", None),
            P("strip"),
            P("strip"),
            P("strip"),
            P("strip"),
        ),
        out_specs=(P("strip", None), P("strip", None), P("strip", None)),
        check_vma=False,
    )
```

time: 58.5 us -> 55.2 us (0.944)
  the two profiles are of different devices: /device:TPU:256 before, /device:TPU:192 now
where the time goes in v4:
time: 55.2 us; the launch traced here: 55 us
  blocking collectives  34.7 us (63%)
  waiting for transfers between devices  8.19 us (15%)
  Pallas kernels  7.43 us (13%)
  starting transfers between devices  3.98 us (7%)
  between operations  0.68 us (1%)
    all_to_all x1, blocking collectives, local(): lax.all_to_all(parts.reshape(groups, 8, LANES), 'dom', 0, 0, tiled=True)  20.9 us
    all_to_all x1, blocking collectives, local(): lax.all_to_all(rows.reshape(groups, 8, LANES), 'dom', 0, 0, tiled=True)  13.8 us
    ppermute x1, waiting for transfers between devices, local(): arrived = lax.ppermute(along, 'strip', backward)  6.38 us
    pallas_call x1, Pallas kernels, local(): call(forecast_kernel, 'forecast', [HBM] * 12, [((2,) + message, f32), (me...  4.41 us
    pallas_call x1, Pallas kernels, local(): call(finish_kernel, 'finish', [VMEM] * 8, [((groups * 8, LANES), f32), gr...  2.3 us
    ppermute x1, starting transfers between devices, local(): far = lax.ppermute(far, 'strip', onward)  2.04 us
    ppermute x1, starting transfers between devices, local(): joined = lax.ppermute(joined, 'strip', swapped)  1.92 us
    ppermute x1, waiting for transfers between devices, local(): far = lax.ppermute(far, 'strip', onward)  1.81 us
  transfers between devices with their start and end apart: 3, of which 2 were waited for; matrix products, arithmetic and copies ran while one was open for 0% of the time, Pallas kernels for 0%

profile of v4, /device:TPU:192, one launch (start us, length us, event | category | flops | bytes accessed | tf_op | source)
XLA Modules:
  0.0 55.0 jit_solution(13784858262624567911)
XLA Ops:
  0.6 4.4 %forecast.1 = (f32[2,232,128]{2,1,0:T(8,128)S(1)}, f32[232,128]{1,0:T(8,128)S(1)}, f32[2,232,128]{2,1,0:T(8,128)S(1)}, f32[48,128]{1,0:T(8,128)S(1)}, f32[336,12...) custom-call(s32[32]{0:T(128)} %cell_hbm.1, s32[32]{0:T(128)} %radii_hbm.1, ...), custom_call_target="tpu_custom_call" | custom-call | tf_op jit(solution)/shard_map/forecast/pallas_call | solution.py:433
  5.1 0.0 collective-permute-start
  5.1 6.4 %collective-permute-done.arrived_ref = f32[232,128]{1,0:T(8,128)S(1)} collective-permute-done((f32[232,128]{1,0:T(8,128)S(1)}, f32[232,128]{1,0:T(8,128)S(1)}, u32[]{:S(2)}, u32[]{:S(2)}) %collective-permute-start) | collective-permute-done | bytes 118816 | tf_op jit(solution)/shard_map/ppermute | solution.py:447
  11.5 1.9 %collective-permute-start.2 = (f32[2,232,128]{2,1,0:T(8,128)S(1)}, f32[2,232,128]{2,1,0:T(8,128)S(1)}, u32[]{:S(2)}, u32[]{:S(2)}) collective-permute-start(f32[2,232,128]{2,1,0:T(8,128)S(1)} %join.1), channel_id=1, source_target_pairs={{0,1},{1,0},{2,3},{3,2},{4,5},{5,4},{6,7},{7,6},{8,9},{9,8},{10,11... | collective-permute-start | bytes 712712 | tf_op jit(solution)/shard_map/ppermute | solution.py:450
  13.4 2.0 %collective-permute-start.1 = (f32[48,128]{1,0:T(8,128)S(1)}, f32[48,128]{1,0:T(8,128)S(1)}, u32[]{:S(2)}, u32[]{:S(2)}) collective-permute-start(f32[48,128]{1,0:T(8,128)S(1)} %get-tuple-element.15), channel_id=1, source_target_pairs={{0,2},{2,4},{4,6},{6,8},{8,10},{10,12},{12,14},{14,15},{15,13},{13... | collective-permute-start | bytes 73736 | tf_op jit(solution)/shard_map/ppermute | solution.py:448
  15.4 1.8 %collective-permute-done.1.far_ref = f32[48,128]{1,0:T(8,128)S(1)} collective-permute-done((f32[48,128]{1,0:T(8,128)S(1)}, f32[48,128]{1,0:T(8,128)S(1)}, u32[]{:S(2)}, u32[]{:S(2)}) %collective-permute-start.1) | collective-permute-done | bytes 24608 | tf_op jit(solution)/shard_map/ppermute | solution.py:448
  17.3 0.0 collective-permute-done.2.joined_ref
  17.3 2.3 %finish.1 = (f32[256,128]{1,0:T(8,128)S(1)}, f32[2,768,128]{2,1,0:T(8,128)S(1)}, f32[2,768,128]{2,1,0:T(8,128)S(1)}, f32[2,768,128]{2,1,0:T(8,128)S(1)}) custom-call(f32[2,232,128]{2,1,0:T(8,128)S(1)} %get-tuple-element.12.own_ref, f32[336,128]{1,0:T(8,128)S(1)} %get-tuple-element.13.extra_ref, ...), custom_call_target="tpu_custom_call", output_to_operand_aliasing={{1}: (5, {}), {2}: (6, {}), {3}: (7, {})} | custom-call | tf_op jit(solution)/shard_map/finish/pallas_call | solution.py:451
  19.6 20.9 %all_to_all.10 = f32[32,8,128]{2,1,0:T(8,128)S(1)} all-to-all(f32[32,8,128]{2,1,0:T(8,128)S(1)} %bitcast.11), channel_id=1, replica_groups=mesh['dom'=32,'strip'=16] {'dom'}, dimensions={0} | all-to-all | bytes 262144 | tf_op jit(solution)/shard_map/all_to_all | solution.py:459
  40.5 0.1 combine.1
  40.5 13.8 %all_to_all.11 = f32[32,8,128]{2,1,0:T(8,128)S(1)} all-to-all(f32[32,8,128]{2,1,0:T(8,128)S(1)} %bitcast.10), channel_id=1, replica_groups=mesh['dom'=32,'strip'=16] {'dom'}, dimensions={0} | all-to-all | bytes 262144 | tf_op jit(solution)/shard_map/all_to_all | solution.py:463
  54.3 0.7 %spread.1 = (f32[32,256]{1,0:T(8,128)}, f32[32,256]{1,0:T(8,128)}, f32[32,256]{1,0:T(8,128)}) custom-call(f32[256,128]{1,0:T(8,128)S(1)} %bitcast.8), custom_call_target="tpu_custom_call" | custom-call | tf_op jit(solution)/shard_map/spread/pallas_call | solution.py:465
  (1 shorter events, 0.0 us)
Async XLA Ops:
  5.1 6.4 %collective-permute-start = (f32[232,128]{1,0:T(8,128)S(1)}, f32[232,128]{1,0:T(8,128)S(1)}, u32[]{:S(2)}, u32[]{:S(2)}) collective-permute-start(f32[232,128]{1,0:T(8,128)S(1)} %get-tuple-element.14), channel_id=1, source_target_pairs={{2,0},{4,2},{6,4},{8,6},{10,8},{12,10},{14,12},{15,14},{13,15},{11... | collective-permute-start | bytes 356360 | tf_op jit(solution)/shard_map/ppermute | solution.py:447
  11.5 5.8 %collective-permute-start.2 = (f32[2,232,128]{2,1,0:T(8,128)S(1)}, f32[2,232,128]{2,1,0:T(8,128)S(1)}, u32[]{:S(2)}, u32[]{:S(2)}) collective-permute-start(f32[2,232,128]{2,1,0:T(8,128)S(1)} %join.1), channel_id=1, source_target_pairs={{0,1},{1,0},{2,3},{3,2},{4,5},{5,4},{6,7},{7,6},{8,9},{9,8},{10,11... | collective-permute-start | bytes 712712 | tf_op jit(solution)/shard_map/ppermute | solution.py:450
  13.4 3.8 %collective-permute-start.1 = (f32[48,128]{1,0:T(8,128)S(1)}, f32[48,128]{1,0:T(8,128)S(1)}, u32[]{:S(2)}, u32[]{:S(2)}) collective-permute-start(f32[48,128]{1,0:T(8,128)S(1)} %get-tuple-element.15), channel_id=1, source_target_pairs={{0,2},{2,4},{4,6},{6,8},{8,10},{10,12},{12,14},{14,15},{15,13},{13... | collective-permute-start | bytes 73736 | tf_op jit(solution)/shard_map/ppermute | solution.py:448

commit v5 on v4

--- a/solution.py
+++ b/solution.py
@@ -209,13 +209,42 @@
     across_ref[0] = own_ref[1 - odd]
 
 
-def join_kernel(across_ref, arrived_ref, joined_ref):
-    del across_ref
+def join_kernel(across_ref, arrived_ref, far_ref, joined_ref):
+    del across_ref, far_ref
     joined_ref[1] = arrived_ref[...]
 
 
+def taper_rows(messages, offsets, strip, near_ref, taper_ref):
+    count = len(messages)
+    column_at = lax.broadcasted_iota(jnp.int32, (SENS, COLS), 1).astype(f32)
+    lines = []
+    for part, (message, offset) in enumerate(zip(messages, offsets)):
+        entry = message[ENTRY:ACROSS]
+        gap = column_at - entry[:, 1:2]
+        squared = jnp.where(entry[:, 3:4] == strip + offset, entry[:, 2:3], 0.0)
+        near_ref[part] = squared - gap * gap
+        lines.append(jnp.broadcast_to(entry[:, 0:1] + offset * ROWS, (SENS, LANES)))
+
+    def at_row(r, carry):
+        here = r.astype(f32)
+        for part in range(count):
+            gap = here - lines[part]
+            gap = gap * gap
+            value = jnp.maximum(near_ref[part] - jnp.concatenate([gap, gap], axis=1), 0.0)
+            coarse = value.astype(bf16)
+            taper_ref[r, part * SENS : (part + 1) * SENS] = coarse
+            taper_ref[r, (count + part) * SENS : (count + part + 1) * SENS] = (value - coarse.astype(f32)).astype(bf16)
+        return carry
+
+    lax.fori_loop(0, ROWS, at_row, 0, unroll=4 // count)
+
+
+def taper_kernel(own_ref, tapers_ref, near_ref):
+    taper_rows([own_ref.at[0]], [0.0], own_ref[0, ACROSS + 3 : ACROSS + 4, 0:1], near_ref, tapers_ref)
+
+
 def finish_kernel(
-    own_ref, extra_ref, arrived_ref, far_ref, joined_ref, depth_in, flow_in, stored_in,
+    own_ref, tapers_ref, extra_ref, arrived_ref, far_ref, joined_ref, depth_in, flow_in, stored_in,
     out_ref, depth_ref, flow_ref, stored_ref,
     before_ref, after_ref, near_ref, taper_ref, weight_ref,
 ):
@@ -277,7 +306,7 @@
     group = lane // SENS
 
     def beside(ref, first, count):
-        parts = (before_ref[first : first + count], ref[0, first : first + count], after_ref[first : first + count])
+        parts = (ref[0, first : first + count], before_ref[first : first + count], after_ref[first : first + count])
         parts = [parts[0], pltpu.roll(parts[1], SENS, 1), pltpu.roll(parts[2], 2 * SENS, 1)]
         return jnp.where(group == 0, parts[0], jnp.where(group == 1, parts[1], parts[2]))
 
@@ -301,12 +330,12 @@
 
     far = each(lambda a, b: jnp.where(strip > 1.5, jnp.where(odd, a, b), 0.0), get(arrived_ref, 0), get(far_ref, 0))
     added = sample([
-        (each(lambda i, d: advection * i * d, keep(has_before, get(before_ref, 2)), start), ROWS - 1.0, 0, 3),
-        (depth_0, 0.0, 1, 3), (more_1, 1.0, 1, 3), (more_31, ROWS - 1.0, 1, 3),
+        (each(lambda i, d: advection * i * d, keep(has_before, get(before_ref, 2)), start), ROWS - 1.0, 1, 3),
+        (depth_0, 0.0, 0, 3), (more_1, 1.0, 0, 3), (more_31, ROWS - 1.0, 0, 3),
         (depth_32, 0.0, 2, 3),
     ])
-    beyond = sample([(far, 1.0, 0, 1), (last, 1.0, 2, 1)])
-    known = jnp.where((place == 0.0) & (group > 0), 0.0, beside(own_ref, SAMPLED, MEMBERS))
+    beyond = sample([(far, 1.0, 1, 1), (last, 1.0, 2, 1)])
+    known = jnp.where((place == 0.0) & (group != 1), 0.0, beside(own_ref, SAMPLED, MEMBERS))
     found = known + added + beside(own_ref, SLOPE, MEMBERS) * beyond
     real = group < 3
     misfit = (found - facts[4:5]) / jnp.where(real, facts[5:6], 1.0)
@@ -318,36 +347,15 @@
         stack.append(piece)
         rest = rest - piece
     pieces = jnp.concatenate(stack, axis=0)
-    turned = pltpu.roll(pieces, 3 * SENS, 1)
     pieces = jnp.concatenate(
-        [jnp.where(lane < 3 * SENS, pieces, turned), jnp.where(lane < 3 * SENS, turned, 0.0)], axis=1
+        [jnp.where(group == 0, pieces, pltpu.roll(pieces, SENS, 1)), pltpu.roll(pieces, LANES - SENS, 1)], axis=1
     )[:, : 6 * SENS].astype(bf16)
 
-    entries = [ref[ENTRY:ACROSS] for ref in (before_ref, down_ref, after_ref)]
-    column_at = lax.broadcasted_iota(jnp.int32, (SENS, COLS), 1).astype(f32)
-    lines = []
-    for part, (entry, offset) in enumerate(zip(entries, (-1.0, 0.0, 1.0))):
-        gap = column_at - entry[:, 1:2]
-        squared = jnp.where(entry[:, 3:4] == strip + offset, entry[:, 2:3], 0.0)
-        near_ref[part] = squared - gap * gap
-        lines.append(jnp.broadcast_to(entry[:, 0:1] + offset * ROWS, (SENS, LANES)))
-
-    def at_row(r, carry):
-        here = r.astype(f32)
-        for part in range(3):
-            gap = here - lines[part]
-            gap = gap * gap
-            value = jnp.maximum(near_ref[part] - jnp.concatenate([gap, gap], axis=1), 0.0)
-            coarse = value.astype(bf16)
-            taper_ref[r, part * SENS : (part + 1) * SENS] = coarse
-            taper_ref[r, (3 + part) * SENS : (4 + part) * SENS] = (value - coarse.astype(f32)).astype(bf16)
-        return carry
-
-    lax.fori_loop(0, ROWS, at_row, 0, unroll=2)
-
+    taper_rows([before_ref, after_ref], [-1.0, 1.0], strip, near_ref, taper_ref)
     for i in range(ROWS // 8):
         for r in range(8 * i, 8 * i + 8):
-            part = jnp.dot(pieces, taper_ref[r], preferred_element_type=f32)
+            tapers = jnp.concatenate([tapers_ref[r], taper_ref[r]], axis=0)
+            part = jnp.dot(pieces, tapers, preferred_element_type=f32)
             weight = part[:MEMBERS] + part[MEMBERS : 2 * MEMBERS] + part[2 * MEMBERS :]
             for half in range(2):
                 weight_ref[half, r * MEMBERS : (r + 1) * MEMBERS] = weight[:, half * LANES : (half + 1) * LANES]
@@ -446,16 +454,19 @@
     )
     arrived = lax.ppermute(along, "strip", backward)
     far = lax.ppermute(far, "strip", onward)
-    (joined,) = call(join_kernel, "join", [VMEM] * 2, [((2,) + message, f32)], aliases={0: 0})(across, arrived)
+    (joined,) = call(join_kernel, "join", [VMEM] * 3, [((2,) + message, f32)], aliases={0: 0})(across, arrived, far)
     joined = lax.ppermute(joined, "strip", swapped)
+    (tapers,) = call(
+        taper_kernel, "taper", [VMEM], [((ROWS, 2 * SENS, COLS), bf16)], [pltpu.VMEM((1, SENS, COLS), f32)],
+    )(own)
     parts, depth, flow, stored = call(
-        finish_kernel, "finish", [VMEM] * 8, [((groups * 8, LANES), f32), grid, grid, grid],
+        finish_kernel, "finish", [VMEM] * 9, [((groups * 8, LANES), f32), grid, grid, grid],
         [
-            pltpu.VMEM(message, f32), pltpu.VMEM(message, f32), pltpu.VMEM((3, SENS, COLS), f32),
-            pltpu.VMEM((ROWS, 6 * SENS, COLS), bf16), pltpu.VMEM((2, ROWS * MEMBERS, LANES), f32),
+            pltpu.VMEM(message, f32), pltpu.VMEM(message, f32), pltpu.VMEM((2, SENS, COLS), f32),
+            pltpu.VMEM((ROWS, 4 * SENS, COLS), bf16), pltpu.VMEM((2, ROWS * MEMBERS, LANES), f32),
         ],
-        aliases={5: 1, 6: 2, 7: 3},
-    )(own, extra, arrived, far, joined, depth, flow, stored)
+        aliases={6: 1, 7: 2, 8: 3},
+    )(own, tapers, extra, arrived, far, joined, depth, flow, stored)
     shared = lax.all_to_all(parts.reshape(groups, 8, LANES), "dom", 0, 0, tiled=True)
     (rows,) = call(
         lambda *refs: combine_kernel(groups, *refs), "combine", [VMEM], [((groups * 8, LANES), f32)],

time: 55.2 us -> 52.6 us (0.953)
  waiting for transfers between devices: 8.19 us -> 3.47 us
  starting transfers between devices: 3.98 us -> 6.17 us
    ppermute x1, waiting for transfers between devices: 6.38 us -> 1.26 us  [local(): arrived = lax.ppermute(along, 'strip', backward)]
    ppermute x1, starting transfers between devices: 2.04 us -> 3.6 us  [local(): far = lax.ppermute(far, 'strip', onward)]
    ppermute x1, waiting for transfers between devices: 0.01 us -> 0.68 us  [local(): joined = lax.ppermute(joined, 'strip', swapped)]
    ppermute x1, starting transfers between devices: 1.92 us -> 2.55 us  [local(): joined = lax.ppermute(joined, 'strip', swapped)]
    pallas_call x2 -> x3, Pallas kernels: 2.31 us -> 2.5 us  [the longest x1 2.08 us: local(): call(finish_kernel, 'finish', [VMEM] * 9, [((groups * 8, LANES), f32), gr...]
  transfers between devices with their start and end apart: 3 -> 3, of which waited for: 2 -> 3; matrix products, arithmetic and copies ran while one was open for 0% -> 0% of each run, Pallas kernels for 0% -> 1%
where the time goes in v5:
time: 52.6 us; the launch traced here: 52.4 us
  blocking collectives  34.5 us (66%)
  Pallas kernels  7.62 us (14%)
  starting transfers between devices  6.17 us (12%)
  waiting for transfers between devices  3.47 us (7%)
  between operations  0.69 us (1%)
    all_to_all x1, blocking collectives, local(): lax.all_to_all(parts.reshape(groups, 8, LANES), 'dom', 0, 0, tiled=True)  20.5 us
    all_to_all x1, blocking collectives, local(): lax.all_to_all(rows.reshape(groups, 8, LANES), 'dom', 0, 0, tiled=True)  13.9 us
    pallas_call x1, Pallas kernels, local(): call(forecast_kernel, 'forecast', [HBM] * 12, [((2,) + message, f32), (me...  4.41 us
    ppermute x1, starting transfers between devices, local(): far = lax.ppermute(far, 'strip', onward)  3.6 us
    ppermute x1, starting transfers between devices, local(): joined = lax.ppermute(joined, 'strip', swapped)  2.55 us
    pallas_call x1, Pallas kernels, local(): call(finish_kernel, 'finish', [VMEM] * 9, [((groups * 8, LANES), f32), gr...  2.08 us
    ppermute x1, waiting for transfers between devices, local(): far = lax.ppermute(far, 'strip', onward)  1.52 us
    ppermute x1, waiting for transfers between devices, local(): arrived = lax.ppermute(along, 'strip', backward)  1.26 us
  transfers between devices with their start and end apart: 3, of which 3 were waited for; matrix products, arithmetic and copies ran while one was open for 0% of the time, Pallas kernels for 1%

profile of v5, /device:TPU:192, one launch (start us, length us, event | category | flops | bytes accessed | tf_op | source)
XLA Modules:
  0.0 52.4 jit_solution(13297793982403247471)
XLA Ops:
  0.6 4.4 %forecast.1 = (f32[2,232,128]{2,1,0:T(8,128)S(1)}, f32[232,128]{1,0:T(8,128)S(1)}, f32[2,232,128]{2,1,0:T(8,128)S(1)}, f32[48,128]{1,0:T(8,128)S(1)}, f32[336,12...) custom-call(s32[32]{0:T(128)} %cell_hbm.1, s32[32]{0:T(128)} %radii_hbm.1, ...), custom_call_target="tpu_custom_call" | custom-call | tf_op jit(solution)/shard_map/forecast/pallas_call | solution.py:441
  5.1 0.0 collective-permute-start
  5.1 3.6 %collective-permute-start.1 = (f32[48,128]{1,0:T(8,128)S(1)}, f32[48,128]{1,0:T(8,128)S(1)}, u32[]{:S(2)}, u32[]{:S(2)}) collective-permute-start(f32[48,128]{1,0:T(8,128)S(1)} %get-tuple-element.15), channel_id=1, source_target_pairs={{0,2},{2,4},{4,6},{6,8},{8,10},{10,12},{12,14},{14,15},{15,13},{13... | collective-permute-start | bytes 73736 | tf_op jit(solution)/shard_map/ppermute | solution.py:456
  8.7 1.5 %collective-permute-done.1.far_ref = f32[48,128]{1,0:T(8,128)S(1)} collective-permute-done((f32[48,128]{1,0:T(8,128)S(1)}, f32[48,128]{1,0:T(8,128)S(1)}, u32[]{:S(2)}, u32[]{:S(2)}) %collective-permute-start.1) | collective-permute-done | bytes 24608 | tf_op jit(solution)/shard_map/ppermute | solution.py:456
  10.2 1.3 %collective-permute-done.arrived_ref = f32[232,128]{1,0:T(8,128)S(1)} collective-permute-done((f32[232,128]{1,0:T(8,128)S(1)}, f32[232,128]{1,0:T(8,128)S(1)}, u32[]{:S(2)}, u32[]{:S(2)}) %collective-permute-start) | collective-permute-done | bytes 118816 | tf_op jit(solution)/shard_map/ppermute | solution.py:455
  11.5 2.5 %collective-permute-start.2 = (f32[2,232,128]{2,1,0:T(8,128)S(1)}, f32[2,232,128]{2,1,0:T(8,128)S(1)}, u32[]{:S(2)}, u32[]{:S(2)}) collective-permute-start(f32[2,232,128]{2,1,0:T(8,128)S(1)} %join.1), channel_id=1, source_target_pairs={{0,1},{1,0},{2,3},{3,2},{4,5},{5,4},{6,7},{7,6},{8,9},{9,8},{10,11... | collective-permute-start | bytes 712712 | tf_op jit(solution)/shard_map/ppermute | solution.py:458
  14.0 0.4 taper.1.tapers_ref
  14.5 0.7 %collective-permute-done.2.joined_ref = f32[2,232,128]{2,1,0:T(8,128)S(1)} collective-permute-done((f32[2,232,128]{2,1,0:T(8,128)S(1)}, f32[2,232,128]{2,1,0:T(8,128)S(1)}, u32[]{:S(2)}, u32[]{:S(2)}) %collective-permute-start.2) | collective-permute-done | bytes 237600 | tf_op jit(solution)/shard_map/ppermute | solution.py:458
  15.1 2.1 %finish.1 = (f32[256,128]{1,0:T(8,128)S(1)}, f32[2,768,128]{2,1,0:T(8,128)S(1)}, f32[2,768,128]{2,1,0:T(8,128)S(1)}, f32[2,768,128]{2,1,0:T(8,128)S(1)}) custom-call(f32[2,232,128]{2,1,0:T(8,128)S(1)} %get-tuple-element.12.own_ref, bf16[32,64,256]{2,1,0:T(8,128)(2,1)S(1)} %taper.1.tapers_ref, ...), custom_call_target="tpu_custom_call", output_to_operand_aliasing={{1}: (6, {}), {2}: (7, {}), {3}: (8, {})} | custom-call | tf_op jit(solution)/shard_map/finish/pallas_call | solution.py:462
  17.2 20.5 %all_to_all.10 = f32[32,8,128]{2,1,0:T(8,128)S(1)} all-to-all(f32[32,8,128]{2,1,0:T(8,128)S(1)} %bitcast.11), channel_id=1, replica_groups=mesh['dom'=32,'strip'=16] {'dom'}, dimensions={0} | all-to-all | bytes 262144 | tf_op jit(solution)/shard_map/all_to_all | solution.py:470
  37.8 0.1 combine.1
  37.8 13.9 %all_to_all.11 = f32[32,8,128]{2,1,0:T(8,128)S(1)} all-to-all(f32[32,8,128]{2,1,0:T(8,128)S(1)} %bitcast.10), channel_id=1, replica_groups=mesh['dom'=32,'strip'=16] {'dom'}, dimensions={0} | all-to-all | bytes 262144 | tf_op jit(solution)/shard_map/all_to_all | solution.py:474
  51.7 0.7 %spread.1 = (f32[32,256]{1,0:T(8,128)}, f32[32,256]{1,0:T(8,128)}, f32[32,256]{1,0:T(8,128)}) custom-call(f32[256,128]{1,0:T(8,128)S(1)} %bitcast.8), custom_call_target="tpu_custom_call" | custom-call | tf_op jit(solution)/shard_map/spread/pallas_call | solution.py:476
  (1 shorter events, 0.0 us)
Async XLA Ops:
  5.1 6.4 %collective-permute-start = (f32[232,128]{1,0:T(8,128)S(1)}, f32[232,128]{1,0:T(8,128)S(1)}, u32[]{:S(2)}, u32[]{:S(2)}) collective-permute-start(f32[232,128]{1,0:T(8,128)S(1)} %get-tuple-element.14), channel_id=1, source_target_pairs={{2,0},{4,2},{6,4},{8,6},{10,8},{12,10},{14,12},{15,14},{13,15},{11... | collective-permute-start | bytes 356360 | tf_op jit(solution)/shard_map/ppermute | solution.py:455
  5.1 5.1 %collective-permute-start.1 = (f32[48,128]{1,0:T(8,128)S(1)}, f32[48,128]{1,0:T(8,128)S(1)}, u32[]{:S(2)}, u32[]{:S(2)}) collective-permute-start(f32[48,128]{1,0:T(8,128)S(1)} %get-tuple-element.15), channel_id=1, source_target_pairs={{0,2},{2,4},{4,6},{6,8},{8,10},{10,12},{12,14},{14,15},{15,13},{13... | collective-permute-start | bytes 73736 | tf_op jit(solution)/shard_map/ppermute | solution.py:456
  11.5 3.7 %collective-permute-start.2 = (f32[2,232,128]{2,1,0:T(8,128)S(1)}, f32[2,232,128]{2,1,0:T(8,128)S(1)}, u32[]{:S(2)}, u32[]{:S(2)}) collective-permute-start(f32[2,232,128]{2,1,0:T(8,128)S(1)} %join.1), channel_id=1, source_target_pairs={{0,1},{1,0},{2,3},{3,2},{4,5},{5,4},{6,7},{7,6},{8,9},{9,8},{10,11... | collective-permute-start | bytes 712712 | tf_op jit(solution)/shard_map/ppermute | solution.py:458

commit v6 on v5

--- a/solution.py
+++ b/solution.py
@@ -16,10 +16,9 @@
 COLS = 256
 SENS = 32
 LANES = 128
+CHUNK = 8
 SAMPLED = 6 * MEMBERS
-SLOPE = SAMPLED + MEMBERS
-ENTRY = SLOPE + MEMBERS
-ACROSS = ENTRY + SENS
+ACROSS = SAMPLED + MEMBERS
 MESSAGE = ACROSS + 8
 
 f32 = jnp.float32
@@ -58,94 +57,74 @@
     return [ref[(2 * slot + h) * MEMBERS : (2 * slot + h + 1) * MEMBERS] for h in range(2)]
 
 
+def split(values, pieces):
+    stack = []
+    for _ in range(pieces):
+        piece = values.astype(bf16).astype(f32)
+        stack.append(piece)
+        values = values - piece
+    return jnp.concatenate(stack, axis=0)
+
+
+def exact_product(rows, marks, pieces):
+    left = jnp.concatenate([split(values, pieces) for values in rows], axis=1).astype(bf16)
+    right = jnp.concatenate(marks, axis=0).astype(bf16)
+    total = jnp.dot(left, right, preferred_element_type=f32)
+    parts = [total[i * MEMBERS : (i + 1) * MEMBERS] for i in range(pieces)]
+    return sum(parts[1:], parts[0])
+
+
 def forecast_kernel(
-    cell_hbm, radii_hbm, cells_hbm, radius_hbm, observed_hbm, sigma_hbm,
+    cell_hbm, cells_hbm, radius_hbm, observed_hbm, sigma_hbm,
     surface_hbm, discharge_hbm, storage_hbm, exchange_hbm, depth_noise_hbm, flow_noise_hbm,
     own_ref, along_ref, across_ref, far_ref, extra_ref, depth_ref, flow_ref, stored_ref,
     surface_ref, discharge_ref, storage_ref, exchange_ref, depth_noise_ref, flow_noise_ref,
-    first_ref, last_ref, slope_ref, cell_ref, radii_ref, cells_ref, radius_ref, observed_ref, sigma_ref, sems,
+    first_ref, last_ref, cell_ref, cells_ref, radius_ref, observed_ref, sigma_ref, sems,
 ):
-    pairs = [
-        (surface_hbm, surface_ref), (discharge_hbm, discharge_ref), (storage_hbm, storage_ref),
-        (depth_noise_hbm.at[0], depth_noise_ref.at[0]), (flow_noise_hbm.at[0], flow_noise_ref.at[0]),
-        (depth_noise_hbm.at[1], depth_noise_ref.at[1]), (flow_noise_hbm.at[1], flow_noise_ref.at[1]),
-        (exchange_hbm, exchange_ref), (cell_hbm, cell_ref), (radii_hbm, radii_ref), (cells_hbm, cells_ref), (radius_hbm, radius_ref),
-        (observed_hbm, observed_ref), (sigma_hbm, sigma_ref),
-    ]
-    copies = [pltpu.make_async_copy(source, target, sems.at[i]) for i, (source, target) in enumerate(pairs)]
-    for copy in copies:
-        copy.start()
-
-    def keep(scratch, slot, rows):
-        flat = rows.reshape(MEMBERS * 8, COLS)
-        scratch[slot, 0] = flat[:, :LANES]
-        scratch[slot, 1] = flat[:, LANES:]
-
-    def take(ref, lead, slot):
-        copies[slot].wait()
-        keep(first_ref, slot, ref[lead + (slice(None), slice(0, 16), slice(None))].astype(f32)[:, :8])
-        if slot != 5:
-            keep(last_ref, slot, ref[lead + (slice(None), slice(16, 32), slice(None))].astype(f32)[:, 8:])
-
-    take(surface_ref, (), 0)
-    take(discharge_ref, (), 1)
-    take(storage_ref, (), 2)
-    take(depth_noise_ref, (0,), 3)
-    take(flow_noise_ref, (0,), 4)
-    take(depth_noise_ref, (1,), 5)
-    take(flow_noise_ref, (1,), 6)
-    for copy in copies[7:]:
-        copy.wait()
-
-    def row_of(ref, slot, row):
-        return [ref[slot, h, pl.ds(row, MEMBERS, stride=8)] for h in range(2)]
-
-    def step_one(surface, flow, flow_below, stored, rate, noise):
-        return each(
-            lambda s, q, b, t, e, n, d: s - advection * (q - b) + d - e * (s - t) + n,
-            surface, flow, flow_below, stored, rate, noise, spread(surface),
-        )
-
-    nothing = [jnp.zeros((MEMBERS, LANES), f32)] * 2
-    rate = halves(exchange_ref[...].astype(f32))
-    rate_0, rate_1, rate_31 = [[r[i : i + 1] for r in rate] for i in (0, 1, ROWS - 1)]
-    surface_0, surface_1 = row_of(first_ref, 0, 0), row_of(first_ref, 0, 1)
-    flow_0, flow_1 = row_of(first_ref, 1, 0), row_of(first_ref, 1, 1)
-    stored_0, stored_1 = row_of(first_ref, 2, 0), row_of(first_ref, 2, 1)
-    depth_0 = step_one(surface_0, flow_0, nothing, stored_0, rate_0, row_of(first_ref, 3, 0))
-    depth_1 = step_one(surface_1, flow_1, flow_0, stored_1, rate_1, row_of(first_ref, 3, 1))
-    stored_next = each(lambda s, t, e: (1.0 - drainage) * t + e * (s - t), surface_0, stored_0, rate_0)
-    inverse_0 = each(lambda q: 1.0 / (1.0 + friction * jnp.abs(q)), flow_0)
-    flow_part = each(
-        lambda q, d, n, i: (q - gravity * d + n) * i, flow_0, depth_1, row_of(first_ref, 4, 0), inverse_0
-    )
-    up_ref, down_ref = own_ref.at[0], own_ref.at[1]
-    put(up_ref, 0, depth_0)
-    put(up_ref, 1, each(lambda e, i: 1.0 - e - (advection * gravity) * i, rate_0, inverse_0))
-    put(up_ref, 2, each(lambda e, t, n, q: e * t + n - advection * q, rate_0, stored_next, row_of(first_ref, 5, 0), flow_part))
-    flow_31 = row_of(last_ref, 1, 7)
-    depth_31 = step_one(
-        row_of(last_ref, 0, 7), flow_31, row_of(last_ref, 1, 6), row_of(last_ref, 2, 7), rate_31, row_of(last_ref, 3, 7)
-    )
-    inverse_31 = each(lambda q: 1.0 / (1.0 + friction * jnp.abs(q)), flow_31)
-    put(down_ref, 0, flow_31)
-    put(down_ref, 1, each(lambda q, d, n, i: (q + gravity * d + n) * i, flow_31, depth_31, row_of(last_ref, 4, 7), inverse_31))
-    put(down_ref, 2, each(lambda i: gravity * i, inverse_31))
-    put(far_ref, 0, flow_31)
-    put(extra_ref, 0, each(lambda i: gravity * i, inverse_0))
-    put(extra_ref, 1, each(lambda q, i, d: q + gravity * i * d, flow_part, inverse_0, depth_0))
-    put(extra_ref, 2, row_of(first_ref, 6, 0))
-    put(extra_ref, 3, row_of(last_ref, 6, 7))
-    put(extra_ref, 6, each(lambda e, z: e + z, rate_0, nothing))
-    for h in range(2):
-        slope_ref[h] = (advection * advection * gravity) * inverse_0[h]
+    chunks = []
+    for c in range(MEMBERS // CHUNK):
+        some = pl.ds(c * CHUNK, CHUNK)
+        pairs = [
+            (ref.at[some], to.at[some])
+            for ref, to in ((surface_hbm, surface_ref), (discharge_hbm, discharge_ref), (storage_hbm, storage_ref))
+        ] + [
+            (ref.at[:, some], to.at[:, some])
+            for ref, to in ((depth_noise_hbm, depth_noise_ref), (flow_noise_hbm, flow_noise_ref))
+        ]
+        if c == 0:
+            pairs.append((exchange_hbm, exchange_ref))
+        chunks.append(pairs)
+    chunks.append([
+        (cell_hbm, cell_ref), (cells_hbm, cells_ref), (radius_hbm, radius_ref), (observed_hbm, observed_ref),
+        (sigma_hbm, sigma_ref),
+    ])
+    copies, used = [], 0
+    for pairs in chunks:
+        copies.append([])
+        for source, target in pairs:
+            copies[-1].append(pltpu.make_async_copy(source, target, sems.at[used]))
+            copies[-1][-1].start()
+            used += 1
 
     row = lax.broadcasted_iota(jnp.int32, (ROWS, LANES), 0)
 
     def member(p, carry):
+        edge = pl.ds(pl.multiple_of(p * 8, 8), 8)
+
+        def keep(slot, value):
+            for h in range(2):
+                first_ref[slot, h, edge] = value[h][:8]
+                if slot != 5:
+                    last_ref[slot, h, edge] = value[h][ROWS - 8 :]
+
         depth, flow, stored = [halves(ref[p].astype(f32)) for ref in (surface_ref, discharge_ref, storage_ref)]
+        keep(0, depth)
+        keep(1, flow)
+        keep(2, stored)
         for step in range(2):
             depth_noise, flow_noise = [halves(ref[step, p].astype(f32)) for ref in (depth_noise_ref, flow_noise_ref)]
+            keep(3 + 2 * step, depth_noise)
+            keep(4 + 2 * step, flow_noise)
             beside = sides(*depth)
             for h in range(2):
                 flow_below = jnp.where(row == 0, 0.0, pltpu.roll(flow[h], 1, 0))
@@ -160,49 +139,85 @@
                     1.0 / (1.0 + friction * jnp.abs(flow[h]))
                 )
                 depth[h] = depth_next
-                if step == 0:
-                    edge = pl.ds(pl.multiple_of(p * 8, 8), 8)
-                    first_ref[7, h, edge] = flow[h][:8]
-                    last_ref[7, h, edge] = flow[h][ROWS - 8 :]
+            if step == 0:
+                keep(7, flow)
         at = pl.ds(pl.multiple_of(p * ROWS, ROWS), ROWS)
         for ref, value in ((depth_ref, depth), (flow_ref, flow), (stored_ref, stored)):
             for h in range(2):
                 ref[h, at] = value[h]
         return carry
 
-    lax.fori_loop(0, MEMBERS, member, 0, unroll=4)
+    for c in range(MEMBERS // CHUNK):
+        for copy in copies[c]:
+            copy.wait()
+        if c == 0:
+            rate = halves(exchange_ref[...].astype(f32))
+        lax.fori_loop(c * CHUNK, (c + 1) * CHUNK, member, 0, unroll=4)
+
+    def row_of(ref, slot, row):
+        return [ref[slot, h, pl.ds(row, MEMBERS, stride=8)] for h in range(2)]
+
+    def step_one(surface, flow, flow_below, stored, rate, noise):
+        return each(
+            lambda s, q, b, t, e, n, d: s - advection * (q - b) + d - e * (s - t) + n,
+            surface, flow, flow_below, stored, rate, noise, spread(surface),
+        )
+
+    nothing = [jnp.zeros((MEMBERS, LANES), f32)] * 2
+    rate_0, rate_1, rate_31 = [[r[i : i + 1] for r in rate] for i in (0, 1, ROWS - 1)]
+    surface_0, surface_1 = row_of(first_ref, 0, 0), row_of(first_ref, 0, 1)
+    flow_0, flow_1 = row_of(first_ref, 1, 0), row_of(first_ref, 1, 1)
+    stored_0, stored_1 = row_of(first_ref, 2, 0), row_of(first_ref, 2, 1)
+    depth_0 = step_one(surface_0, flow_0, nothing, stored_0, rate_0, row_of(first_ref, 3, 0))
+    depth_1 = step_one(surface_1, flow_1, flow_0, stored_1, rate_1, row_of(first_ref, 3, 1))
+    stored_next = each(lambda s, t, e: (1.0 - drainage) * t + e * (s - t), surface_0, stored_0, rate_0)
+    inverse_0 = each(lambda q: 1.0 / (1.0 + friction * jnp.abs(q)), flow_0)
+    flow_part = each(
+        lambda q, d, n, i: (q - gravity * d + n) * i, flow_0, depth_1, row_of(first_ref, 4, 0), inverse_0
+    )
+    up_ref, down_ref = own_ref.at[0], own_ref.at[1]
+    put(up_ref, 0, depth_0)
+    put(up_ref, 1, each(lambda e, i: 1.0 - e - (advection * gravity) * i, rate_0, inverse_0))
+    put(up_ref, 2, each(lambda e, t, n, q: e * t + n - advection * q, rate_0, stored_next, row_of(first_ref, 5, 0), flow_part))
+    flow_31 = row_of(last_ref, 1, 7)
+    depth_31 = step_one(
+        row_of(last_ref, 0, 7), flow_31, row_of(last_ref, 1, 6), row_of(last_ref, 2, 7), rate_31, row_of(last_ref, 3, 7)
+    )
+    inverse_31 = each(lambda q: 1.0 / (1.0 + friction * jnp.abs(q)), flow_31)
+    put(down_ref, 0, flow_31)
+    put(down_ref, 1, each(lambda q, d, n, i: (q + gravity * d + n) * i, flow_31, depth_31, row_of(last_ref, 4, 7), inverse_31))
+    put(down_ref, 2, each(lambda i: gravity * i, inverse_31))
+    put(far_ref, 0, flow_31)
+    put(extra_ref, 0, each(lambda i: gravity * i, inverse_0))
+    put(extra_ref, 1, each(lambda q, i, d: q + gravity * i * d, flow_part, inverse_0, depth_0))
+    put(extra_ref, 2, row_of(first_ref, 6, 0))
+    put(extra_ref, 3, row_of(last_ref, 6, 7))
+    put(extra_ref, 6, each(lambda e, z: e + z, rate_0, nothing))
     put(extra_ref, 4, each(lambda q: 1.0 / (1.0 + friction * jnp.abs(q)), row_of(first_ref, 7, 1)))
     put(extra_ref, 5, each(lambda q: 1.0 / (1.0 + friction * jnp.abs(q)), row_of(last_ref, 7, 6)))
 
+    for copy in copies[-1]:
+        copy.wait()
+    cells = cells_ref[...]
+    reach = radius_ref[...].astype(f32)
+    facts = [
+        ((cells >> 8) & (ROWS - 1)).astype(f32), (cells & (COLS - 1)).astype(f32), reach * reach,
+        (cells >> 13).astype(f32), observed_ref[...], sigma_ref[...], jnp.zeros((2, SENS), f32),
+    ]
+    facts = jnp.concatenate([jnp.concatenate(facts, axis=0), jnp.ones((8, LANES - SENS), f32)], axis=1)
     lane = lax.broadcasted_iota(jnp.int32, (MEMBERS, LANES), 1)
-    one_lane = lax.broadcasted_iota(jnp.int32, (1, LANES), 1)
-    sampled, slope = jnp.zeros((MEMBERS, LANES), f32), jnp.zeros((MEMBERS, LANES), f32)
+    hit = lax.broadcasted_iota(jnp.int32, (COLS, LANES), 0).astype(f32) == facts[1:2]
+    slope = exact_product(
+        [jnp.concatenate(each(lambda i: (advection * advection * gravity) * i, inverse_0), axis=1)],
+        [jnp.where((facts[0:1] == 1.0) & (lane[0:1] < SENS), hit.astype(f32), 0.0)], 3,
+    )
+    sampled = pltpu.roll(slope, SENS, 1)
     for k in range(SENS):
         cell = cell_ref[k]
-        half, line, turn = (cell >> 7) & 1, (cell >> 8) & (ROWS - 1), (k - cell) & (LANES - 1)
-        found = pltpu.roll(depth_ref[half, pl.ds(line, MEMBERS, stride=ROWS)], turn, 1)
-        sampled = jnp.where(lane == k, found, sampled)
-        slope = jnp.where(lane == k, pltpu.roll(slope_ref[half], turn, 1), slope)
-        place, column = line.astype(f32), (cell & (COLS - 1)).astype(f32)
-        strip = (cell >> 13).astype(f32)
-        reach = radii_ref[k].astype(f32)
-        entry = jnp.where(
-            one_lane == 0, place, jnp.where(one_lane == 1, column, jnp.where(one_lane == 2, reach * reach, strip))
-        )
-        for i in range(2):
-            own_ref[i, ENTRY + k : ENTRY + k + 1] = entry
-    cells = cells_ref[...]
-    place = ((cells >> 8) & (ROWS - 1)).astype(f32)
-    reach = radius_ref[...].astype(f32)
-    facts = [
-        place, (cells & (COLS - 1)).astype(f32), reach * reach, (cells >> 13).astype(f32),
-        observed_ref[...], sigma_ref[...], jnp.zeros((2, SENS), f32),
-    ]
-    facts = jnp.concatenate([jnp.concatenate(facts, axis=0), jnp.ones((8, LANES - SENS), f32)], axis=1)
-    slope = jnp.where(facts[0:1] == 1.0, slope, 0.0)
+        found = depth_ref[(cell >> 7) & 1, pl.ds((cell >> 8) & (ROWS - 1), MEMBERS, stride=ROWS)]
+        sampled = jnp.where(lane == k, pltpu.roll(found, (k - cell) & (LANES - 1), 1), sampled)
     for i in range(2):
-        own_ref[i, SAMPLED:SLOPE] = sampled
-        own_ref[i, SLOPE:ENTRY] = slope
+        own_ref[i, SAMPLED:ACROSS] = sampled
         own_ref[i, ACROSS:MESSAGE] = facts
     odd = (cell_ref[0] >> 13) & 1
     along_ref[...] = own_ref[odd]
@@ -214,12 +229,13 @@
     joined_ref[1] = arrived_ref[...]
 
 
-def taper_rows(messages, offsets, strip, near_ref, taper_ref):
-    count = len(messages)
+def taper_rows(facts, at, offsets, strip, near_ref, taper_ref):
+    count = len(offsets)
+    entries = jnp.transpose(facts)
     column_at = lax.broadcasted_iota(jnp.int32, (SENS, COLS), 1).astype(f32)
     lines = []
-    for part, (message, offset) in enumerate(zip(messages, offsets)):
-        entry = message[ENTRY:ACROSS]
+    for part, offset in enumerate(offsets):
+        entry = entries[at + part * SENS : at + (part + 1) * SENS]
         gap = column_at - entry[:, 1:2]
         squared = jnp.where(entry[:, 3:4] == strip + offset, entry[:, 2:3], 0.0)
         near_ref[part] = squared - gap * gap
@@ -240,7 +256,8 @@
 
 
 def taper_kernel(own_ref, tapers_ref, near_ref):
-    taper_rows([own_ref.at[0]], [0.0], own_ref[0, ACROSS + 3 : ACROSS + 4, 0:1], near_ref, tapers_ref)
+    facts = own_ref[0, ACROSS:MESSAGE]
+    taper_rows(facts, 0, [0.0], facts[3:4, 0:1], near_ref, tapers_ref)
 
 
 def finish_kernel(
@@ -305,53 +322,37 @@
     lane = lax.broadcasted_iota(jnp.int32, (1, LANES), 1)
     group = lane // SENS
 
-    def beside(ref, first, count):
-        parts = (ref[0, first : first + count], before_ref[first : first + count], after_ref[first : first + count])
-        parts = [parts[0], pltpu.roll(parts[1], SENS, 1), pltpu.roll(parts[2], 2 * SENS, 1)]
+    def beside(first, end, shift=0):
+        parts = (own_ref[0, first:end], before_ref[first:end], after_ref[first:end])
+        parts = [pltpu.roll(part, (i * SENS - shift) % LANES, 1) for i, part in enumerate(parts)]
         return jnp.where(group == 0, parts[0], jnp.where(group == 1, parts[1], parts[2]))
 
-    facts = beside(own_ref, ACROSS, 8)
-    place, column = facts[0:1], facts[1:2]
-    hit = (lax.broadcasted_iota(jnp.int32, (COLS, LANES), 0).astype(f32) == column).astype(f32)
-
-    def sample(rows):
-        left, right = [], []
-        for values, wanted, in_group, pieces in rows:
-            values = jnp.concatenate(values, axis=1)
-            stack = []
-            for _ in range(pieces):
-                piece = values.astype(bf16).astype(f32)
-                stack.append(piece)
-                values = values - piece
-            left.append(jnp.concatenate(stack, axis=0).astype(bf16))
-            right.append(jnp.where((place == wanted) & (group == in_group), hit, 0.0).astype(bf16))
-        total = jnp.dot(jnp.concatenate(left, axis=1), jnp.concatenate(right, axis=0), preferred_element_type=f32)
-        return sum(total[i * MEMBERS : (i + 1) * MEMBERS] for i in range(1, pieces)) + total[:MEMBERS] if pieces > 1 else total
+    facts = beside(ACROSS, MESSAGE)
+    place = facts[0:1]
+    hit = (lax.broadcasted_iota(jnp.int32, (COLS, LANES), 0).astype(f32) == facts[1:2]).astype(f32)
+
+    def sample(rows, pieces):
+        marks = [jnp.where((place == wanted) & (group == of), hit, 0.0) for _, wanted, of in rows]
+        return exact_product([jnp.concatenate(values, axis=1) for values, _, _ in rows], marks, pieces)
 
     far = each(lambda a, b: jnp.where(strip > 1.5, jnp.where(odd, a, b), 0.0), get(arrived_ref, 0), get(far_ref, 0))
     added = sample([
-        (each(lambda i, d: advection * i * d, keep(has_before, get(before_ref, 2)), start), ROWS - 1.0, 1, 3),
-        (depth_0, 0.0, 0, 3), (more_1, 1.0, 0, 3), (more_31, ROWS - 1.0, 0, 3),
-        (depth_32, 0.0, 2, 3),
-    ])
-    beyond = sample([(far, 1.0, 1, 1), (last, 1.0, 2, 1)])
-    known = jnp.where((place == 0.0) & (group != 1), 0.0, beside(own_ref, SAMPLED, MEMBERS))
-    found = known + added + beside(own_ref, SLOPE, MEMBERS) * beyond
+        (each(lambda i, d: advection * i * d, keep(has_before, get(before_ref, 2)), start), ROWS - 1.0, 1),
+        (depth_0, 0.0, 0), (more_1, 1.0, 0), (more_31, ROWS - 1.0, 0),
+        (depth_32, 0.0, 2),
+    ], 3)
+    beyond = sample([(far, 1.0, 1), (last, 1.0, 2)], 1)
+    known = jnp.where((place == 0.0) & (group != 1), 0.0, beside(SAMPLED, ACROSS))
+    found = known + added + beside(SAMPLED, ACROSS, SENS) * beyond
     real = group < 3
     misfit = (found - facts[4:5]) / jnp.where(real, facts[5:6], 1.0)
     lik = jnp.where(real, -0.5 * misfit * misfit / jnp.where(real, facts[2:3], 1.0), 0.0)
-    stack = []
-    rest = lik
-    for _ in range(3):
-        piece = rest.astype(bf16).astype(f32)
-        stack.append(piece)
-        rest = rest - piece
-    pieces = jnp.concatenate(stack, axis=0)
+    pieces = split(lik, 3)
     pieces = jnp.concatenate(
         [jnp.where(group == 0, pieces, pltpu.roll(pieces, SENS, 1)), pltpu.roll(pieces, LANES - SENS, 1)], axis=1
     )[:, : 6 * SENS].astype(bf16)
 
-    taper_rows([before_ref, after_ref], [-1.0, 1.0], strip, near_ref, taper_ref)
+    taper_rows(facts, SENS, [-1.0, 1.0], strip, near_ref, taper_ref)
     for i in range(ROWS // 8):
         for r in range(8 * i, 8 * i + 8):
             tapers = jnp.concatenate([tapers_ref[r], taper_ref[r]], axis=0)
@@ -439,19 +440,15 @@
     edges = lambda count: ((2 * count * MEMBERS, LANES), f32)
     row_of = lambda dtype: pltpu.VMEM((1, SENS), dtype)
     own, along, across, far, extra, depth, flow, stored = call(
-        forecast_kernel, "forecast", [HBM] * 12,
+        forecast_kernel, "forecast", [HBM] * 11,
         [((2,) + message, f32), (message, f32), ((2,) + message, f32), edges(1), edges(7), grid, grid, grid],
         [pltpu.VMEM(field.shape, field.dtype) for field in fields]
         + [
             pltpu.VMEM((8, 2, MEMBERS * 8, LANES), f32), pltpu.VMEM((8, 2, MEMBERS * 8, LANES), f32),
-            pltpu.VMEM((2, MEMBERS, LANES), f32), pltpu.SMEM((SENS,), jnp.int32), pltpu.SMEM((SENS,), jnp.int32),
-            row_of(jnp.int32), row_of(jnp.int32),
-            row_of(f32), row_of(f32), pltpu.SemaphoreType.DMA((14,)),
+            pltpu.SMEM((SENS,), jnp.int32), row_of(jnp.int32), row_of(jnp.int32), row_of(f32), row_of(f32),
+            pltpu.SemaphoreType.DMA((21,)),
         ],
-    )(
-        stay(sensor_cell), stay(sensor_radius), as_row(sensor_cell), as_row(sensor_radius), as_row(observed),
-        as_row(sensor_sigma), *fields,
-    )
+    )(stay(sensor_cell), as_row(sensor_cell), as_row(sensor_radius), as_row(observed), as_row(sensor_sigma), *fields)
     arrived = lax.ppermute(along, "strip", backward)
     far = lax.ppermute(far, "strip", onward)
     (joined,) = call(join_kernel, "join", [VMEM] * 3, [((2,) + message, f32)], aliases={0: 0})(across, arrived, far)

time: 52.6 us -> 52.2 us (level)
  no operation moved by 1% of the time
where the time goes in v6:
time: 52.2 us; the launch traced here: 52 us
  blocking collectives  34.5 us (66%)
  Pallas kernels  7.34 us (14%)
  starting transfers between devices  6.47 us (12%)
  waiting for transfers between devices  3.02 us (6%)
  between operations  0.68 us (1%)
    all_to_all x1, blocking collectives, local(): lax.all_to_all(parts.reshape(groups, 8, LANES), 'dom', 0, 0, tiled=True)  20.6 us
    all_to_all x1, blocking collectives, local(): lax.all_to_all(rows.reshape(groups, 8, LANES), 'dom', 0, 0, tiled=True)  13.9 us
    pallas_call x1, Pallas kernels, local(): call(forecast_kernel, 'forecast', [HBM] * 11, [((2,) + message, f32), (me...  4.06 us
    ppermute x1, starting transfers between devices, local(): far = lax.ppermute(far, 'strip', onward)  3.6 us
    ppermute x1, starting transfers between devices, local(): joined = lax.ppermute(joined, 'strip', swapped)  2.85 us
    pallas_call x1, Pallas kernels, local(): call(finish_kernel, 'finish', [VMEM] * 9, [((groups * 8, LANES), f32), gr...  2.09 us
    ppermute x1, waiting for transfers between devices, local(): far = lax.ppermute(far, 'strip', onward)  1.52 us
  transfers between devices with their start and end apart: 3, of which 3 were waited for; matrix products, arithmetic and copies ran while one was open for 0% of the time, Pallas kernels for 1%

profile of v6, /device:TPU:192, one launch (start us, length us, event | category | flops | bytes accessed | tf_op | source)
XLA Modules:
  0.0 52.0 jit_solution(7356338107799143032)
XLA Ops:
  0.6 4.1 %forecast.1 = (f32[2,176,128]{2,1,0:T(8,128)S(1)}, f32[176,128]{1,0:T(8,128)S(1)}, f32[2,176,128]{2,1,0:T(8,128)S(1)}, f32[48,128]{1,0:T(8,128)S(1)}, f32[336,12...) custom-call(s32[32]{0:T(128)} %cell_hbm.1, ...), custom_call_target="tpu_custom_call" | custom-call | tf_op jit(solution)/shard_map/forecast/pallas_call | solution.py:442
  4.7 0.0 collective-permute-start
  4.7 3.6 %collective-permute-start.1 = (f32[48,128]{1,0:T(8,128)S(1)}, f32[48,128]{1,0:T(8,128)S(1)}, u32[]{:S(2)}, u32[]{:S(2)}) collective-permute-start(f32[48,128]{1,0:T(8,128)S(1)} %get-tuple-element.15), channel_id=1, source_target_pairs={{0,2},{2,4},{4,6},{6,8},{8,10},{10,12},{12,14},{14,15},{15,13},{13... | collective-permute-start | bytes 73736 | tf_op jit(solution)/shard_map/ppermute | solution.py:453
  8.3 1.5 %collective-permute-done.1.far_ref = f32[48,128]{1,0:T(8,128)S(1)} collective-permute-done((f32[48,128]{1,0:T(8,128)S(1)}, f32[48,128]{1,0:T(8,128)S(1)}, u32[]{:S(2)}, u32[]{:S(2)}) %collective-permute-start.1) | collective-permute-done | bytes 24608 | tf_op jit(solution)/shard_map/ppermute | solution.py:453
  9.9 1.0 %collective-permute-done.arrived_ref = f32[176,128]{1,0:T(8,128)S(1)} collective-permute-done((f32[176,128]{1,0:T(8,128)S(1)}, f32[176,128]{1,0:T(8,128)S(1)}, u32[]{:S(2)}, u32[]{:S(2)}) %collective-permute-start) | collective-permute-done | bytes 90144 | tf_op jit(solution)/shard_map/ppermute | solution.py:452
  10.8 2.8 %collective-permute-start.2 = (f32[2,176,128]{2,1,0:T(8,128)S(1)}, f32[2,176,128]{2,1,0:T(8,128)S(1)}, u32[]{:S(2)}, u32[]{:S(2)}) collective-permute-start(f32[2,176,128]{2,1,0:T(8,128)S(1)} %join.1), channel_id=1, source_target_pairs={{0,1},{1,0},{2,3},{3,2},{4,5},{5,4},{6,7},{7,6},{8,9},{9,8},{10,11... | collective-permute-start | bytes 540680 | tf_op jit(solution)/shard_map/ppermute | solution.py:455
  13.7 0.5 taper.1.tapers_ref
  14.2 0.5 %collective-permute-done.2.joined_ref = f32[2,176,128]{2,1,0:T(8,128)S(1)} collective-permute-done((f32[2,176,128]{2,1,0:T(8,128)S(1)}, f32[2,176,128]{2,1,0:T(8,128)S(1)}, u32[]{:S(2)}, u32[]{:S(2)}) %collective-permute-start.2) | collective-permute-done | bytes 180256 | tf_op jit(solution)/shard_map/ppermute | solution.py:455
  14.7 2.1 %finish.1 = (f32[256,128]{1,0:T(8,128)S(1)}, f32[2,768,128]{2,1,0:T(8,128)S(1)}, f32[2,768,128]{2,1,0:T(8,128)S(1)}, f32[2,768,128]{2,1,0:T(8,128)S(1)}) custom-call(f32[2,176,128]{2,1,0:T(8,128)S(1)} %get-tuple-element.12.own_ref, bf16[32,64,256]{2,1,0:T(8,128)(2,1)S(1)} %taper.1.tapers_ref, ...), custom_call_target="tpu_custom_call", output_to_operand_aliasing={{1}: (6, {}), {2}: (7, {}), {3}: (8, {})} | custom-call | tf_op jit(solution)/shard_map/finish/pallas_call | solution.py:459
  16.8 20.6 %all_to_all.10 = f32[32,8,128]{2,1,0:T(8,128)S(1)} all-to-all(f32[32,8,128]{2,1,0:T(8,128)S(1)} %bitcast.11), channel_id=1, replica_groups=mesh['dom'=32,'strip'=16] {'dom'}, dimensions={0} | all-to-all | bytes 262144 | tf_op jit(solution)/shard_map/all_to_all | solution.py:467
  37.4 0.1 combine.1
  37.4 13.9 %all_to_all.11 = f32[32,8,128]{2,1,0:T(8,128)S(1)} all-to-all(f32[32,8,128]{2,1,0:T(8,128)S(1)} %bitcast.10), channel_id=1, replica_groups=mesh['dom'=32,'strip'=16] {'dom'}, dimensions={0} | all-to-all | bytes 262144 | tf_op jit(solution)/shard_map/all_to_all | solution.py:471
  51.3 0.7 %spread.1 = (f32[32,256]{1,0:T(8,128)}, f32[32,256]{1,0:T(8,128)}, f32[32,256]{1,0:T(8,128)}) custom-call(f32[256,128]{1,0:T(8,128)S(1)} %bitcast.8), custom_call_target="tpu_custom_call" | custom-call | tf_op jit(solution)/shard_map/spread/pallas_call | solution.py:473
  (1 shorter events, 0.0 us)
Async XLA Ops:
  4.7 6.1 %collective-permute-start = (f32[176,128]{1,0:T(8,128)S(1)}, f32[176,128]{1,0:T(8,128)S(1)}, u32[]{:S(2)}, u32[]{:S(2)}) collective-permute-start(f32[176,128]{1,0:T(8,128)S(1)} %get-tuple-element.14), channel_id=1, source_target_pairs={{2,0},{4,2},{6,4},{8,6},{10,8},{12,10},{14,12},{15,14},{13,15},{11... | collective-permute-start | bytes 270344 | tf_op jit(solution)/shard_map/ppermute | solution.py:452
  4.7 5.1 %collective-permute-start.1 = (f32[48,128]{1,0:T(8,128)S(1)}, f32[48,128]{1,0:T(8,128)S(1)}, u32[]{:S(2)}, u32[]{:S(2)}) collective-permute-start(f32[48,128]{1,0:T(8,128)S(1)} %get-tuple-element.15), channel_id=1, source_target_pairs={{0,2},{2,4},{4,6},{6,8},{8,10},{10,12},{12,14},{14,15},{15,13},{13... | collective-permute-start | bytes 73736 | tf_op jit(solution)/shard_map/ppermute | solution.py:453
  10.8 3.9 %collective-permute-start.2 = (f32[2,176,128]{2,1,0:T(8,128)S(1)}, f32[2,176,128]{2,1,0:T(8,128)S(1)}, u32[]{:S(2)}, u32[]{:S(2)}) collective-permute-start(f32[2,176,128]{2,1,0:T(8,128)S(1)} %join.1), channel_id=1, source_target_pairs={{0,1},{1,0},{2,3},{3,2},{4,5},{5,4},{6,7},{7,6},{8,9},{9,8},{10,11... | collective-permute-start | bytes 540680 | tf_op jit(solution)/shard_map/ppermute | solution.py:455

commit v7 on v6

--- a/solution.py
+++ b/solution.py
@@ -17,6 +17,7 @@
 SENS = 32
 LANES = 128
 CHUNK = 8
+PITCH = 40
 SAMPLED = 6 * MEMBERS
 ACROSS = SAMPLED + MEMBERS
 MESSAGE = ACROSS + 8
@@ -66,12 +67,15 @@
     return jnp.concatenate(stack, axis=0)
 
 
-def exact_product(rows, marks, pieces):
-    left = jnp.concatenate([split(values, pieces) for values in rows], axis=1).astype(bf16)
-    right = jnp.concatenate(marks, axis=0).astype(bf16)
-    total = jnp.dot(left, right, preferred_element_type=f32)
-    parts = [total[i * MEMBERS : (i + 1) * MEMBERS] for i in range(pieces)]
-    return sum(parts[1:], parts[0])
+def pick(rows, hit):
+    left = jnp.concatenate([split(jnp.concatenate(values, axis=1), pieces) for values, pieces in rows], axis=0)
+    total = jnp.dot(left.astype(bf16), hit, preferred_element_type=f32)
+    found, at = [], 0
+    for _, pieces in rows:
+        parts = [total[at + i * MEMBERS : at + (i + 1) * MEMBERS] for i in range(pieces)]
+        found.append(sum(parts[1:], parts[0]))
+        at += pieces * MEMBERS
+    return found
 
 
 def forecast_kernel(
@@ -141,7 +145,7 @@
                 depth[h] = depth_next
             if step == 0:
                 keep(7, flow)
-        at = pl.ds(pl.multiple_of(p * ROWS, ROWS), ROWS)
+        at = pl.ds(pl.multiple_of(p * PITCH, 8), ROWS)
         for ref, value in ((depth_ref, depth), (flow_ref, flow), (stored_ref, stored)):
             for h in range(2):
                 ref[h, at] = value[h]
@@ -206,15 +210,12 @@
     ]
     facts = jnp.concatenate([jnp.concatenate(facts, axis=0), jnp.ones((8, LANES - SENS), f32)], axis=1)
     lane = lax.broadcasted_iota(jnp.int32, (MEMBERS, LANES), 1)
-    hit = lax.broadcasted_iota(jnp.int32, (COLS, LANES), 0).astype(f32) == facts[1:2]
-    slope = exact_product(
-        [jnp.concatenate(each(lambda i: (advection * advection * gravity) * i, inverse_0), axis=1)],
-        [jnp.where((facts[0:1] == 1.0) & (lane[0:1] < SENS), hit.astype(f32), 0.0)], 3,
-    )
-    sampled = pltpu.roll(slope, SENS, 1)
+    hit = (lax.broadcasted_iota(jnp.int32, (COLS, LANES), 0).astype(f32) == facts[1:2]).astype(f32).astype(bf16)
+    (slope,) = pick([(each(lambda i: (advection * advection * gravity) * i, inverse_0), 3)], hit)
+    sampled = pltpu.roll(jnp.where((facts[0:1] == 1.0) & (lane < SENS), slope, 0.0), SENS, 1)
     for k in range(SENS):
         cell = cell_ref[k]
-        found = depth_ref[(cell >> 7) & 1, pl.ds((cell >> 8) & (ROWS - 1), MEMBERS, stride=ROWS)]
+        found = depth_ref[(cell >> 7) & 1, pl.ds((cell >> 8) & (ROWS - 1), MEMBERS, stride=PITCH)]
         sampled = jnp.where(lane == k, pltpu.roll(found, (k - cell) & (LANES - 1), 1), sampled)
     for i in range(2):
         own_ref[i, SAMPLED:ACROSS] = sampled
@@ -276,11 +277,11 @@
     keep = lambda condition, row: each(lambda v: jnp.where(condition, v, 0.0), row)
 
     def line(ref, row):
-        return [ref[h, pl.ds(row, MEMBERS, stride=ROWS)] for h in range(2)]
+        return [ref[h, pl.ds(row, MEMBERS, stride=PITCH)] for h in range(2)]
 
     def set_line(ref, row, values):
         for h in range(2):
-            ref[h, pl.ds(row, MEMBERS, stride=ROWS)] = values[h]
+            ref[h, pl.ds(row, MEMBERS, stride=PITCH)] = values[h]
 
     back = keep(has_before, get(before_ref, 0))
     start = each(lambda d, q: d + advection * q, get(up_ref, 0), back)
@@ -329,19 +330,17 @@
 
     facts = beside(ACROSS, MESSAGE)
     place = facts[0:1]
-    hit = (lax.broadcasted_iota(jnp.int32, (COLS, LANES), 0).astype(f32) == facts[1:2]).astype(f32)
-
-    def sample(rows, pieces):
-        marks = [jnp.where((place == wanted) & (group == of), hit, 0.0) for _, wanted, of in rows]
-        return exact_product([jnp.concatenate(values, axis=1) for values, _, _ in rows], marks, pieces)
+    hit = (lax.broadcasted_iota(jnp.int32, (COLS, LANES), 0).astype(f32) == facts[1:2]).astype(f32).astype(bf16)
 
     far = each(lambda a, b: jnp.where(strip > 1.5, jnp.where(odd, a, b), 0.0), get(arrived_ref, 0), get(far_ref, 0))
-    added = sample([
-        (each(lambda i, d: advection * i * d, keep(has_before, get(before_ref, 2)), start), ROWS - 1.0, 1),
-        (depth_0, 0.0, 0), (more_1, 1.0, 0), (more_31, ROWS - 1.0, 0),
-        (depth_32, 0.0, 2),
-    ], 3)
-    beyond = sample([(far, 1.0, 1), (last, 1.0, 2)], 1)
+    beyond_31 = each(lambda i, d: advection * i * d, keep(has_before, get(before_ref, 2)), start)
+    wanted = [
+        (beyond_31, 3, ROWS - 1.0, 1), (depth_0, 3, 0.0, 0), (more_1, 3, 1.0, 0), (more_31, 3, ROWS - 1.0, 0),
+        (depth_32, 3, 0.0, 2), (far, 1, 1.0, 1), (last, 1, 1.0, 2),
+    ]
+    found = pick([(values, pieces) for values, pieces, _, _ in wanted], hit)
+    found = [jnp.where((place == row) & (group == of), value, 0.0) for value, (_, _, row, of) in zip(found, wanted)]
+    added, beyond = sum(found[1:5], found[0]), found[5] + found[6]
     known = jnp.where((place == 0.0) & (group != 1), 0.0, beside(SAMPLED, ACROSS))
     found = known + added + beside(SAMPLED, ACROSS, SENS) * beyond
     real = group < 3
@@ -368,7 +367,7 @@
             sums = [jnp.zeros((8, LANES), f32) for _ in range(4)]
             for p in range(MEMBERS):
                 factor = jnp.exp(weights[p] - best)
-                at = pl.ds(p * ROWS + 8 * i, 8)
+                at = pl.ds(p * PITCH + 8 * i, 8)
                 sums[0] = sums[0] + factor
                 sums[1] = sums[1] + factor * depth_ref[half, at]
                 sums[2] = sums[2] + factor * flow_ref[half, at]
@@ -435,7 +434,7 @@
     stay = lambda values: pltpu.with_memory_space_constraint(values, pltpu.HBM)
     as_row = lambda values: stay(values.reshape(1, SENS))
     fields = [stay(f) for f in (surface, discharge, storage, exchange, depth_perturbation, flow_perturbation)]
-    grid = ((2, MEMBERS * ROWS, LANES), f32)
+    grid = ((2, MEMBERS * PITCH, LANES), f32)
     message = (MESSAGE, LANES)
     edges = lambda count: ((2 * count * MEMBERS, LANES), f32)
     row_of = lambda dtype: pltpu.VMEM((1, SENS), dtype)

time: 52.2 us -> 51.8 us (level)
  no operation moved by 1% of the time
where the time goes in v7:
time: 51.8 us; the launch traced here: 51.6 us
  blocking collectives  34.5 us (67%)
  Pallas kernels  6.9 us (13%)
  starting transfers between devices  6.47 us (12%)
  waiting for transfers between devices  3.02 us (6%)
  between operations  0.68 us (1%)
    all_to_all x1, blocking collectives, local(): lax.all_to_all(parts.reshape(groups, 8, LANES), 'dom', 0, 0, tiled=True)  20.6 us
    all_to_all x1, blocking collectives, local(): lax.all_to_all(rows.reshape(groups, 8, LANES), 'dom', 0, 0, tiled=True)  13.9 us
    pallas_call x1, Pallas kernels, local(): call(forecast_kernel, 'forecast', [HBM] * 11, [((2,) + message, f32), (me...  3.79 us
    ppermute x1, starting transfers between devices, local(): far = lax.ppermute(far, 'strip', onward)  3.6 us
    ppermute x1, starting transfers between devices, local(): joined = lax.ppermute(joined, 'strip', swapped)  2.85 us
    pallas_call x1, Pallas kernels, local(): call(finish_kernel, 'finish', [VMEM] * 9, [((groups * 8, LANES), f32), gr...  1.91 us
    ppermute x1, waiting for transfers between devices, local(): far = lax.ppermute(far, 'strip', onward)  1.52 us
  transfers between devices with their start and end apart: 3, of which 3 were waited for; matrix products, arithmetic and copies ran while one was open for 0% of the time, Pallas kernels for 1%

profile of v7, /device:TPU:192, one launch (start us, length us, event | category | flops | bytes accessed | tf_op | source)
XLA Modules:
  0.0 51.6 jit_solution(7523698804684622869)
XLA Ops:
  0.6 3.8 %forecast.1 = (f32[2,176,128]{2,1,0:T(8,128)S(1)}, f32[176,128]{1,0:T(8,128)S(1)}, f32[2,176,128]{2,1,0:T(8,128)S(1)}, f32[48,128]{1,0:T(8,128)S(1)}, f32[336,12...) custom-call(s32[32]{0:T(128)} %cell_hbm.1, ...), custom_call_target="tpu_custom_call" | custom-call | tf_op jit(solution)/shard_map/forecast/pallas_call | solution.py:441
  4.4 0.0 collective-permute-start
  4.5 3.6 %collective-permute-start.1 = (f32[48,128]{1,0:T(8,128)S(1)}, f32[48,128]{1,0:T(8,128)S(1)}, u32[]{:S(2)}, u32[]{:S(2)}) collective-permute-start(f32[48,128]{1,0:T(8,128)S(1)} %get-tuple-element.15), channel_id=1, source_target_pairs={{0,2},{2,4},{4,6},{6,8},{8,10},{10,12},{12,14},{14,15},{15,13},{13... | collective-permute-start | bytes 73736 | tf_op jit(solution)/shard_map/ppermute | solution.py:452
  8.1 1.5 %collective-permute-done.1.far_ref = f32[48,128]{1,0:T(8,128)S(1)} collective-permute-done((f32[48,128]{1,0:T(8,128)S(1)}, f32[48,128]{1,0:T(8,128)S(1)}, u32[]{:S(2)}, u32[]{:S(2)}) %collective-permute-start.1) | collective-permute-done | bytes 24608 | tf_op jit(solution)/shard_map/ppermute | solution.py:452
  9.6 1.0 %collective-permute-done.arrived_ref = f32[176,128]{1,0:T(8,128)S(1)} collective-permute-done((f32[176,128]{1,0:T(8,128)S(1)}, f32[176,128]{1,0:T(8,128)S(1)}, u32[]{:S(2)}, u32[]{:S(2)}) %collective-permute-start) | collective-permute-done | bytes 90144 | tf_op jit(solution)/shard_map/ppermute | solution.py:451
  10.5 2.8 %collective-permute-start.2 = (f32[2,176,128]{2,1,0:T(8,128)S(1)}, f32[2,176,128]{2,1,0:T(8,128)S(1)}, u32[]{:S(2)}, u32[]{:S(2)}) collective-permute-start(f32[2,176,128]{2,1,0:T(8,128)S(1)} %join.1), channel_id=1, source_target_pairs={{0,1},{1,0},{2,3},{3,2},{4,5},{5,4},{6,7},{7,6},{8,9},{9,8},{10,11... | collective-permute-start | bytes 540680 | tf_op jit(solution)/shard_map/ppermute | solution.py:454
  13.4 0.5 taper.1.tapers_ref
  13.9 0.5 %collective-permute-done.2.joined_ref = f32[2,176,128]{2,1,0:T(8,128)S(1)} collective-permute-done((f32[2,176,128]{2,1,0:T(8,128)S(1)}, f32[2,176,128]{2,1,0:T(8,128)S(1)}, u32[]{:S(2)}, u32[]{:S(2)}) %collective-permute-start.2) | collective-permute-done | bytes 180256 | tf_op jit(solution)/shard_map/ppermute | solution.py:454
  14.4 1.9 %finish.1 = (f32[256,128]{1,0:T(8,128)S(1)}, f32[2,960,128]{2,1,0:T(8,128)S(1)}, f32[2,960,128]{2,1,0:T(8,128)S(1)}, f32[2,960,128]{2,1,0:T(8,128)S(1)}) custom-call(f32[2,176,128]{2,1,0:T(8,128)S(1)} %get-tuple-element.12.own_ref, bf16[32,64,256]{2,1,0:T(8,128)(2,1)S(1)} %taper.1.tapers_ref, ...), custom_call_target="tpu_custom_call", output_to_operand_aliasing={{1}: (6, {}), {2}: (7, {}), {3}: (8, {})} | custom-call | tf_op jit(solution)/shard_map/finish/pallas_call | solution.py:458
  16.4 20.6 %all_to_all.10 = f32[32,8,128]{2,1,0:T(8,128)S(1)} all-to-all(f32[32,8,128]{2,1,0:T(8,128)S(1)} %bitcast.11), channel_id=1, replica_groups=mesh['dom'=32,'strip'=16] {'dom'}, dimensions={0} | all-to-all | bytes 262144 | tf_op jit(solution)/shard_map/all_to_all | solution.py:466
  36.9 0.1 combine.1
  37.0 13.9 %all_to_all.11 = f32[32,8,128]{2,1,0:T(8,128)S(1)} all-to-all(f32[32,8,128]{2,1,0:T(8,128)S(1)} %bitcast.10), channel_id=1, replica_groups=mesh['dom'=32,'strip'=16] {'dom'}, dimensions={0} | all-to-all | bytes 262144 | tf_op jit(solution)/shard_map/all_to_all | solution.py:470
  50.9 0.7 %spread.1 = (f32[32,256]{1,0:T(8,128)}, f32[32,256]{1,0:T(8,128)}, f32[32,256]{1,0:T(8,128)}) custom-call(f32[256,128]{1,0:T(8,128)S(1)} %bitcast.8), custom_call_target="tpu_custom_call" | custom-call | tf_op jit(solution)/shard_map/spread/pallas_call | solution.py:472
  (1 shorter events, 0.0 us)
Async XLA Ops:
  4.4 6.1 %collective-permute-start = (f32[176,128]{1,0:T(8,128)S(1)}, f32[176,128]{1,0:T(8,128)S(1)}, u32[]{:S(2)}, u32[]{:S(2)}) collective-permute-start(f32[176,128]{1,0:T(8,128)S(1)} %get-tuple-element.14), channel_id=1, source_target_pairs={{2,0},{4,2},{6,4},{8,6},{10,8},{12,10},{14,12},{15,14},{13,15},{11... | collective-permute-start | bytes 270344 | tf_op jit(solution)/shard_map/ppermute | solution.py:451
  4.5 5.1 %collective-permute-start.1 = (f32[48,128]{1,0:T(8,128)S(1)}, f32[48,128]{1,0:T(8,128)S(1)}, u32[]{:S(2)}, u32[]{:S(2)}) collective-permute-start(f32[48,128]{1,0:T(8,128)S(1)} %get-tuple-element.15), channel_id=1, source_target_pairs={{0,2},{2,4},{4,6},{6,8},{8,10},{10,12},{12,14},{14,15},{15,13},{13... | collective-permute-start | bytes 73736 | tf_op jit(solution)/shard_map/ppermute | solution.py:452
  10.5 3.9 %collective-permute-start.2 = (f32[2,176,128]{2,1,0:T(8,128)S(1)}, f32[2,176,128]{2,1,0:T(8,128)S(1)}, u32[]{:S(2)}, u32[]{:S(2)}) collective-permute-start(f32[2,176,128]{2,1,0:T(8,128)S(1)} %join.1), channel_id=1, source_target_pairs={{0,1},{1,0},{2,3},{3,2},{4,5},{5,4},{6,7},{7,6},{8,9},{9,8},{10,11... | collective-permute-start | bytes 540680 | tf_op jit(solution)/shard_map/ppermute | solution.py:454

commit v8 on v7

--- a/solution.py
+++ b/solution.py
@@ -463,11 +463,14 @@
         ],
         aliases={6: 1, 7: 2, 8: 3},
     )(own, tapers, extra, arrived, far, joined, depth, flow, stored)
-    shared = lax.all_to_all(parts.reshape(groups, 8, LANES), "dom", 0, 0, tiled=True)
+    turned = [(20 + i) % groups for i in range(groups)]
+    shared = lax.all_to_all(parts.reshape(groups, 8, LANES), "dom", 0, 0, tiled=True, axis_index_groups=[turned])
     (rows,) = call(
         lambda *refs: combine_kernel(groups, *refs), "combine", [VMEM], [((groups * 8, LANES), f32)],
     )(shared.reshape(groups * 8, LANES))
-    whole = lax.all_to_all(rows.reshape(groups, 8, LANES), "dom", 0, 0, tiled=True)
+    whole = lax.all_to_all(
+        rows.reshape(groups, 8, LANES), "dom", 0, 0, tiled=True, axis_index_groups=[turned]
+    )
     return tuple(
         call(spread_kernel, "spread", [VMEM], [((ROWS, COLS), f32)] * 3)(whole.reshape(groups * 8, LANES))
     )

time: 51.8 us -> 47.6 us (0.919)
  the two profiles are of different devices: /device:TPU:192 before, /device:TPU:8 now
where the time goes in v8:
time: 47.6 us; the launch traced here: 47.4 us
  blocking collectives  32.1 us (67%)
  Pallas kernels  6.9 us (14%)
  starting transfers between devices  4.68 us (10%)
  waiting for transfers between devices  3.02 us (6%)
  between operations  0.68 us (1%)
    all_to_all x1, blocking collectives, local(): lax.all_to_all(parts.reshape(groups, 8, LANES), 'dom', 0, 0, tiled=True,...  18.4 us
    all_to_all x1, blocking collectives, local(): lax.all_to_all(rows.reshape(groups, 8, LANES), 'dom', 0, 0, tiled=True, a...  13.7 us
    pallas_call x1, Pallas kernels, local(): call(forecast_kernel, 'forecast', [HBM] * 11, [((2,) + message, f32), (me...  3.79 us
    ppermute x1, starting transfers between devices, local(): far = lax.ppermute(far, 'strip', onward)  2.39 us
    ppermute x1, starting transfers between devices, local(): joined = lax.ppermute(joined, 'strip', swapped)  2.27 us
    pallas_call x1, Pallas kernels, local(): call(finish_kernel, 'finish', [VMEM] * 9, [((groups * 8, LANES), f32), gr...  1.91 us
    ppermute x1, waiting for transfers between devices, local(): far = lax.ppermute(far, 'strip', onward)  1.52 us
    ppermute x1, waiting for transfers between devices, local(): arrived = lax.ppermute(along, 'strip', backward)  0.96 us
  transfers between devices with their start and end apart: 3, of which 3 were waited for; matrix products, arithmetic and copies ran while one was open for 0% of the time, Pallas kernels for 1%

profile of v8, /device:TPU:8, one launch (start us, length us, event | category | flops | bytes accessed | tf_op | source)
XLA Modules:
  0.0 47.4 jit_solution(2542310617577744881)
XLA Ops:
  0.6 3.8 %forecast.1 = (f32[2,176,128]{2,1,0:T(8,128)S(1)}, f32[176,128]{1,0:T(8,128)S(1)}, f32[2,176,128]{2,1,0:T(8,128)S(1)}, f32[48,128]{1,0:T(8,128)S(1)}, f32[336,12...) custom-call(s32[32]{0:T(128)} %cell_hbm.1, ...), custom_call_target="tpu_custom_call" | custom-call | tf_op jit(solution)/shard_map/forecast/pallas_call | solution.py:441
  4.4 0.0 collective-permute-start
  4.5 2.4 %collective-permute-start.1 = (f32[48,128]{1,0:T(8,128)S(1)}, f32[48,128]{1,0:T(8,128)S(1)}, u32[]{:S(2)}, u32[]{:S(2)}) collective-permute-start(f32[48,128]{1,0:T(8,128)S(1)} %get-tuple-element.15), channel_id=1, source_target_pairs={{0,2},{2,4},{4,6},{6,8},{8,10},{10,12},{12,14},{14,15},{15,13},{13... | collective-permute-start | bytes 73736 | tf_op jit(solution)/shard_map/ppermute | solution.py:452
  6.9 1.5 %collective-permute-done.1.far_ref = f32[48,128]{1,0:T(8,128)S(1)} collective-permute-done((f32[48,128]{1,0:T(8,128)S(1)}, f32[48,128]{1,0:T(8,128)S(1)}, u32[]{:S(2)}, u32[]{:S(2)}) %collective-permute-start.1) | collective-permute-done | bytes 24608 | tf_op jit(solution)/shard_map/ppermute | solution.py:452
  8.4 1.0 %collective-permute-done.arrived_ref = f32[176,128]{1,0:T(8,128)S(1)} collective-permute-done((f32[176,128]{1,0:T(8,128)S(1)}, f32[176,128]{1,0:T(8,128)S(1)}, u32[]{:S(2)}, u32[]{:S(2)}) %collective-permute-start) | collective-permute-done | bytes 90144 | tf_op jit(solution)/shard_map/ppermute | solution.py:451
  9.3 2.3 %collective-permute-start.2 = (f32[2,176,128]{2,1,0:T(8,128)S(1)}, f32[2,176,128]{2,1,0:T(8,128)S(1)}, u32[]{:S(2)}, u32[]{:S(2)}) collective-permute-start(f32[2,176,128]{2,1,0:T(8,128)S(1)} %join.1), channel_id=1, source_target_pairs={{0,1},{1,0},{2,3},{3,2},{4,5},{5,4},{6,7},{7,6},{8,9},{9,8},{10,11... | collective-permute-start | bytes 540680 | tf_op jit(solution)/shard_map/ppermute | solution.py:454
  11.6 0.5 %taper.1.tapers_ref = bf16[32,64,256]{2,1,0:T(8,128)(2,1)S(1)} custom-call(f32[2,176,128]{2,1,0:T(8,128)S(1)} %get-tuple-element.12.own_ref), custom_call_target="tpu_custom_call" | custom-call | tf_op jit(solution)/shard_map/taper/pallas_call | solution.py:455
  12.1 0.5 %collective-permute-done.2.joined_ref = f32[2,176,128]{2,1,0:T(8,128)S(1)} collective-permute-done((f32[2,176,128]{2,1,0:T(8,128)S(1)}, f32[2,176,128]{2,1,0:T(8,128)S(1)}, u32[]{:S(2)}, u32[]{:S(2)}) %collective-permute-start.2) | collective-permute-done | bytes 180256 | tf_op jit(solution)/shard_map/ppermute | solution.py:454
  12.6 1.9 %finish.1 = (f32[256,128]{1,0:T(8,128)S(1)}, f32[2,960,128]{2,1,0:T(8,128)S(1)}, f32[2,960,128]{2,1,0:T(8,128)S(1)}, f32[2,960,128]{2,1,0:T(8,128)S(1)}) custom-call(f32[2,176,128]{2,1,0:T(8,128)S(1)} %get-tuple-element.12.own_ref, bf16[32,64,256]{2,1,0:T(8,128)(2,1)S(1)} %taper.1.tapers_ref, ...), custom_call_target="tpu_custom_call", output_to_operand_aliasing={{1}: (6, {}), {2}: (7, {}), {3}: (8, {})} | custom-call | tf_op jit(solution)/shard_map/finish/pallas_call | solution.py:458
  14.6 18.4 %all_to_all.10 = f32[32,8,128]{2,1,0:T(8,128)S(1)} all-to-all(f32[32,8,128]{2,1,0:T(8,128)S(1)} %bitcast.11), channel_id=1, replica_groups={{320,336,352,368,384,400,416,432,448,464,480,496,0,16,32,48,64,80,96,11..., dimensions={0} | all-to-all | bytes 262144 | tf_op jit(solution)/shard_map/all_to_all | solution.py:467
  32.9 0.1 combine.1
  33.0 13.7 %all_to_all.11 = f32[32,8,128]{2,1,0:T(8,128)S(1)} all-to-all(f32[32,8,128]{2,1,0:T(8,128)S(1)} %bitcast.10), channel_id=1, replica_groups={{320,336,352,368,384,400,416,432,448,464,480,496,0,16,32,48,64,80,96,11..., dimensions={0} | all-to-all | bytes 262144 | tf_op jit(solution)/shard_map/all_to_all | solution.py:471
  46.7 0.7 %spread.1 = (f32[32,256]{1,0:T(8,128)}, f32[32,256]{1,0:T(8,128)}, f32[32,256]{1,0:T(8,128)}) custom-call(f32[256,128]{1,0:T(8,128)S(1)} %bitcast.8), custom_call_target="tpu_custom_call" | custom-call | tf_op jit(solution)/shard_map/spread/pallas_call | solution.py:475
  (1 shorter events, 0.0 us)
Async XLA Ops:
  4.4 4.9 %collective-permute-start = (f32[176,128]{1,0:T(8,128)S(1)}, f32[176,128]{1,0:T(8,128)S(1)}, u32[]{:S(2)}, u32[]{:S(2)}) collective-permute-start(f32[176,128]{1,0:T(8,128)S(1)} %get-tuple-element.14), channel_id=1, source_target_pairs={{2,0},{4,2},{6,4},{8,6},{10,8},{12,10},{14,12},{15,14},{13,15},{11... | collective-permute-start | bytes 270344 | tf_op jit(solution)/shard_map/ppermute | solution.py:451
  4.5 3.9 %collective-permute-start.1 = (f32[48,128]{1,0:T(8,128)S(1)}, f32[48,128]{1,0:T(8,128)S(1)}, u32[]{:S(2)}, u32[]{:S(2)}) collective-permute-start(f32[48,128]{1,0:T(8,128)S(1)} %get-tuple-element.15), channel_id=1, source_target_pairs={{0,2},{2,4},{4,6},{6,8},{8,10},{10,12},{12,14},{14,15},{15,13},{13... | collective-permute-start | bytes 73736 | tf_op jit(solution)/shard_map/ppermute | solution.py:452
  9.3 3.3 %collective-permute-start.2 = (f32[2,176,128]{2,1,0:T(8,128)S(1)}, f32[2,176,128]{2,1,0:T(8,128)S(1)}, u32[]{:S(2)}, u32[]{:S(2)}) collective-permute-start(f32[2,176,128]{2,1,0:T(8,128)S(1)} %join.1), channel_id=1, source_target_pairs={{0,1},{1,0},{2,3},{3,2},{4,5},{5,4},{6,7},{7,6},{8,9},{9,8},{10,11... | collective-permute-start | bytes 540680 | tf_op jit(solution)/shard_map/ppermute | solution.py:454

commit v9 on v8

--- a/solution.py
+++ b/solution.py
@@ -76,6 +76,11 @@
         found.append(sum(parts[1:], parts[0]))
         at += pieces * MEMBERS
     return found
+
+
+def next_flow(flow, depth, noise, row):
+    depth_above = jnp.where(row == ROWS - 1, 0.0, pltpu.roll(depth, ROWS - 1, 0))
+    return (flow - gravity * (depth_above - depth) + noise) * (1.0 / (1.0 + friction * jnp.abs(flow)))
 
 
 def forecast_kernel(
@@ -92,8 +97,8 @@
             (ref.at[some], to.at[some])
             for ref, to in ((surface_hbm, surface_ref), (discharge_hbm, discharge_ref), (storage_hbm, storage_ref))
         ] + [
-            (ref.at[:, some], to.at[:, some])
-            for ref, to in ((depth_noise_hbm, depth_noise_ref), (flow_noise_hbm, flow_noise_ref))
+            (depth_noise_hbm.at[:, some], depth_noise_ref.at[:, some]),
+            (flow_noise_hbm.at[0, some], flow_noise_ref.at[some]),
         ]
         if c == 0:
             pairs.append((exchange_hbm, exchange_ref))
@@ -126,25 +131,21 @@
         keep(1, flow)
         keep(2, stored)
         for step in range(2):
-            depth_noise, flow_noise = [halves(ref[step, p].astype(f32)) for ref in (depth_noise_ref, flow_noise_ref)]
+            depth_noise = halves(depth_noise_ref[step, p].astype(f32))
             keep(3 + 2 * step, depth_noise)
-            keep(4 + 2 * step, flow_noise)
             beside = sides(*depth)
             for h in range(2):
                 flow_below = jnp.where(row == 0, 0.0, pltpu.roll(flow[h], 1, 0))
                 inflow = rate[h] * (depth[h] - stored[h])
-                depth_next = (
+                depth[h] = (
                     (1.0 - 2.0 * diffusion) * depth[h] + diffusion * beside[h]
                     - advection * (flow[h] - flow_below) - inflow + depth_noise[h]
                 )
                 stored[h] = (1.0 - drainage) * stored[h] + inflow
-                depth_above = jnp.where(row == ROWS - 1, 0.0, pltpu.roll(depth_next, ROWS - 1, 0))
-                flow[h] = (flow[h] - gravity * (depth_above - depth_next) + flow_noise[h]) * (
-                    1.0 / (1.0 + friction * jnp.abs(flow[h]))
-                )
-                depth[h] = depth_next
             if step == 0:
-                keep(7, flow)
+                flow_noise = halves(flow_noise_ref[p].astype(f32))
+                keep(4, flow_noise)
+                flow = each(lambda q, d, n: next_flow(q, d, n, row), flow, depth, flow_noise)
         at = pl.ds(pl.multiple_of(p * PITCH, 8), ROWS)
         for ref, value in ((depth_ref, depth), (flow_ref, flow), (stored_ref, stored)):
             for h in range(2):
@@ -194,12 +195,7 @@
     put(far_ref, 0, flow_31)
     put(extra_ref, 0, each(lambda i: gravity * i, inverse_0))
     put(extra_ref, 1, each(lambda q, i, d: q + gravity * i * d, flow_part, inverse_0, depth_0))
-    put(extra_ref, 2, row_of(first_ref, 6, 0))
-    put(extra_ref, 3, row_of(last_ref, 6, 7))
-    put(extra_ref, 6, each(lambda e, z: e + z, rate_0, nothing))
-    put(extra_ref, 4, each(lambda q: 1.0 / (1.0 + friction * jnp.abs(q)), row_of(first_ref, 7, 1)))
-    put(extra_ref, 5, each(lambda q: 1.0 / (1.0 + friction * jnp.abs(q)), row_of(last_ref, 7, 6)))
-
+    put(extra_ref, 2, each(lambda e, z: e + z, rate_0, nothing))
     for copy in copies[-1]:
         copy.wait()
     cells = cells_ref[...]
@@ -225,8 +221,44 @@
     across_ref[0] = own_ref[1 - odd]
 
 
-def join_kernel(across_ref, arrived_ref, far_ref, joined_ref):
-    del across_ref, far_ref
+def line(ref, row):
+    return [ref[h, pl.ds(row, MEMBERS, stride=PITCH)] for h in range(2)]
+
+
+def set_line(ref, row, values):
+    for h in range(2):
+        ref[h, pl.ds(row, MEMBERS, stride=PITCH)] = values[h]
+
+
+def flow_kernel(flow_noise_hbm, depth_ref, flow_in, flow_ref, late_ref, flow_noise_ref, first_ref, last_ref, sems):
+    del flow_in
+    copies = []
+    for c in range(MEMBERS // CHUNK):
+        some = pl.ds(c * CHUNK, CHUNK)
+        copies.append(pltpu.make_async_copy(flow_noise_hbm.at[1, some], flow_noise_ref.at[some], sems.at[c]))
+        copies[c].start()
+    for slot, row in ((2, 1), (3, ROWS - 2)):
+        put(late_ref, slot, each(lambda q: 1.0 / (1.0 + friction * jnp.abs(q)), line(flow_ref, row)))
+    row = lax.broadcasted_iota(jnp.int32, (ROWS, LANES), 0)
+
+    def member(p, carry):
+        at, edge = pl.ds(pl.multiple_of(p * PITCH, 8), ROWS), pl.ds(pl.multiple_of(p * 8, 8), 8)
+        noise = halves(flow_noise_ref[p].astype(f32))
+        for h in range(2):
+            first_ref[h, edge] = noise[h][:8]
+            last_ref[h, edge] = noise[h][ROWS - 8 :]
+            flow_ref[h, at] = next_flow(flow_ref[h, at], depth_ref[h, at], noise[h], row)
+        return carry
+
+    for c in range(MEMBERS // CHUNK):
+        copies[c].wait()
+        lax.fori_loop(c * CHUNK, (c + 1) * CHUNK, member, 0, unroll=4)
+    put(late_ref, 0, [first_ref[h, pl.ds(0, MEMBERS, stride=8)] for h in range(2)])
+    put(late_ref, 1, [last_ref[h, pl.ds(7, MEMBERS, stride=8)] for h in range(2)])
+
+
+def join_kernel(across_ref, arrived_ref, far_ref, late_ref, joined_ref):
+    del across_ref, far_ref, late_ref
     joined_ref[1] = arrived_ref[...]
 
 
@@ -262,7 +294,7 @@
 
 
 def finish_kernel(
-    own_ref, tapers_ref, extra_ref, arrived_ref, far_ref, joined_ref, depth_in, flow_in, stored_in,
+    own_ref, tapers_ref, extra_ref, late_ref, arrived_ref, far_ref, joined_ref, depth_in, flow_in, stored_in,
     out_ref, depth_ref, flow_ref, stored_ref,
     before_ref, after_ref, near_ref, taper_ref, weight_ref,
 ):
@@ -276,13 +308,6 @@
     has_after = after_ref[ACROSS + 3 : ACROSS + 4, 0:1] == strip + 1.0
     keep = lambda condition, row: each(lambda v: jnp.where(condition, v, 0.0), row)
 
-    def line(ref, row):
-        return [ref[h, pl.ds(row, MEMBERS, stride=PITCH)] for h in range(2)]
-
-    def set_line(ref, row, values):
-        for h in range(2):
-            ref[h, pl.ds(row, MEMBERS, stride=PITCH)] = values[h]
-
     back = keep(has_before, get(before_ref, 0))
     start = each(lambda d, q: d + advection * q, get(up_ref, 0), back)
     back_next = keep(has_before, each(lambda f, i, d: f - i * d, get(before_ref, 1), get(before_ref, 2), start))
@@ -298,10 +323,10 @@
     set_line(depth_ref, 1, depth_1)
     set_line(flow_ref, 0, each(
         lambda f, a, d, n: (f - gravity * (a - d) + n) * (1.0 / (1.0 + friction * jnp.abs(f))),
-        flow_0, depth_1, depth_0, get(extra_ref, 2),
+        flow_0, depth_1, depth_0, get(late_ref, 0),
     ))
-    set_line(flow_ref, 1, each(lambda f, i, m: f + gravity * i * m, line(flow_ref, 1), get(extra_ref, 4), more_1))
-    set_line(stored_ref, 0, each(lambda t, e, q: t + advection * e * q, line(stored_ref, 0), get(extra_ref, 6), back))
+    set_line(flow_ref, 1, each(lambda f, i, m: f + gravity * i * m, line(flow_ref, 1), get(late_ref, 2), more_1))
+    set_line(stored_ref, 0, each(lambda t, e, q: t + advection * e * q, line(stored_ref, 0), get(extra_ref, 2), back))
     last = get(down_ref, 0)
     end = keep(has_after, each(lambda d, q: d + advection * q, get(after_ref, 0), last))
     flow_31 = each(lambda f, i, d: f - i * d, get(down_ref, 1), get(down_ref, 2), end)
@@ -314,10 +339,10 @@
     set_line(depth_ref, ROWS - 1, depth_31)
     set_line(flow_ref, ROWS - 1, each(
         lambda f, a, d, n: (f - gravity * (a - d) + n) * (1.0 / (1.0 + friction * jnp.abs(f))),
-        flow_31, depth_32, depth_31, get(extra_ref, 3),
+        flow_31, depth_32, depth_31, get(late_ref, 1),
     ))
     set_line(flow_ref, ROWS - 2, each(
-        lambda f, i, m: f - gravity * i * m, line(flow_ref, ROWS - 2), get(extra_ref, 5), more_31
+        lambda f, i, m: f - gravity * i * m, line(flow_ref, ROWS - 2), get(late_ref, 3), more_31
     ))
 
     lane = lax.broadcasted_iota(jnp.int32, (1, LANES), 1)
@@ -440,29 +465,38 @@
     row_of = lambda dtype: pltpu.VMEM((1, SENS), dtype)
     own, along, across, far, extra, depth, flow, stored = call(
         forecast_kernel, "forecast", [HBM] * 11,
-        [((2,) + message, f32), (message, f32), ((2,) + message, f32), edges(1), edges(7), grid, grid, grid],
-        [pltpu.VMEM(field.shape, field.dtype) for field in fields]
+        [((2,) + message, f32), (message, f32), ((2,) + message, f32), edges(1), edges(3), grid, grid, grid],
+        [pltpu.VMEM(field.shape, field.dtype) for field in fields[:-1]]
         + [
+            pltpu.VMEM(fields[0].shape, bf16),
             pltpu.VMEM((8, 2, MEMBERS * 8, LANES), f32), pltpu.VMEM((8, 2, MEMBERS * 8, LANES), f32),
             pltpu.SMEM((SENS,), jnp.int32), row_of(jnp.int32), row_of(jnp.int32), row_of(f32), row_of(f32),
             pltpu.SemaphoreType.DMA((21,)),
         ],
     )(stay(sensor_cell), as_row(sensor_cell), as_row(sensor_radius), as_row(observed), as_row(sensor_sigma), *fields)
+    strip_edges = pltpu.VMEM((2, MEMBERS * 8, LANES), f32)
+    flow, late = call(
+        flow_kernel, "flow", [HBM] + [VMEM] * 2, [grid, edges(4)],
+        [
+            pltpu.VMEM(fields[0].shape, bf16), strip_edges, strip_edges, pltpu.SemaphoreType.DMA((MEMBERS // CHUNK,)),
+        ],
+        aliases={2: 0},
+    )(fields[-1], depth, flow)
     arrived = lax.ppermute(along, "strip", backward)
     far = lax.ppermute(far, "strip", onward)
-    (joined,) = call(join_kernel, "join", [VMEM] * 3, [((2,) + message, f32)], aliases={0: 0})(across, arrived, far)
+    (joined,) = call(join_kernel, "join", [VMEM] * 4, [((2,) + message, f32)], aliases={0: 0})(across, arrived, far, late)
     joined = lax.ppermute(joined, "strip", swapped)
     (tapers,) = call(
         taper_kernel, "taper", [VMEM], [((ROWS, 2 * SENS, COLS), bf16)], [pltpu.VMEM((1, SENS, COLS), f32)],
     )(own)
     parts, depth, flow, stored = call(
-        finish_kernel, "finish", [VMEM] * 9, [((groups * 8, LANES), f32), grid, grid, grid],
+        finish_kernel, "finish", [VMEM] * 10, [((groups * 8, LANES), f32), grid, grid, grid],
         [
             pltpu.VMEM(message, f32), pltpu.VMEM(message, f32), pltpu.VMEM((2, SENS, COLS), f32),
             pltpu.VMEM((ROWS, 4 * SENS, COLS), bf16), pltpu.VMEM((2, ROWS * MEMBERS, LANES), f32),
         ],
-        aliases={6: 1, 7: 2, 8: 3},
-    )(own, tapers, extra, arrived, far, joined, depth, flow, stored)
+        aliases={7: 1, 8: 2, 9: 3},
+    )(own, tapers, extra, late, arrived, far, joined, depth, flow, stored)
     turned = [(20 + i) % groups for i in range(groups)]
     shared = lax.all_to_all(parts.reshape(groups, 8, LANES), "dom", 0, 0, tiled=True, axis_index_groups=[turned])
     (rows,) = call(

time: 47.6 us -> 47.2 us (level)
  waiting for transfers between devices: 3.02 us -> 1.72 us
  Pallas kernels: 6.9 us -> 7.79 us
    pallas_call x2 -> x3, Pallas kernels: 1.92 us -> 3.23 us  [the longest x1 1.93 us: local(): call(finish_kernel, 'finish', [VMEM] * 10, [((groups * 8, LANES), f32), g...]
    ppermute x1, waiting for transfers between devices: 1.52 us -> 0.22 us  [local(): far = lax.ppermute(far, 'strip', onward)]
  transfers between devices with their start and end apart: 3 -> 3, of which waited for: 3 -> 3; matrix products, arithmetic and copies ran while one was open for 0% -> 0% of each run, Pallas kernels for 1% -> 4%
where the time goes in v9:
time: 47.2 us; the launch traced here: 47 us
  blocking collectives  32.1 us (68%)
  Pallas kernels  7.79 us (17%)
  starting transfers between devices  4.68 us (10%)
  waiting for transfers between devices  1.72 us (4%)
  between operations  0.69 us (1%)
    all_to_all x1, blocking collectives, local(): lax.all_to_all(parts.reshape(groups, 8, LANES), 'dom', 0, 0, tiled=True,...  18.4 us
    all_to_all x1, blocking collectives, local(): lax.all_to_all(rows.reshape(groups, 8, LANES), 'dom', 0, 0, tiled=True, a...  13.7 us
    pallas_call x1, Pallas kernels, local(): call(forecast_kernel, 'forecast', [HBM] * 11, [((2,) + message, f32), (me...  3.37 us
    ppermute x1, starting transfers between devices, local(): far = lax.ppermute(far, 'strip', onward)  2.39 us
    ppermute x1, starting transfers between devices, local(): joined = lax.ppermute(joined, 'strip', swapped)  2.27 us
    pallas_call x1, Pallas kernels, local(): call(finish_kernel, 'finish', [VMEM] * 10, [((groups * 8, LANES), f32), g...  1.93 us
    pallas_call x1, Pallas kernels, local(): call(flow_kernel, 'flow', [HBM] + [VMEM] * 2, [grid, edges(4)], [pltpu.VM...  1.3 us
    ppermute x1, waiting for transfers between devices, local(): arrived = lax.ppermute(along, 'strip', backward)  0.96 us
  transfers between devices with their start and end apart: 3, of which 3 were waited for; matrix products, arithmetic and copies ran while one was open for 0% of the time, Pallas kernels for 4%

profile of v9, /device:TPU:8, one launch (start us, length us, event | category | flops | bytes accessed | tf_op | source)
XLA Modules:
  0.0 47.0 jit_solution(17441696061649154427)
XLA Ops:
  0.6 3.4 %forecast.1 = (f32[2,176,128]{2,1,0:T(8,128)S(1)}, f32[176,128]{1,0:T(8,128)S(1)}, f32[2,176,128]{2,1,0:T(8,128)S(1)}, f32[48,128]{1,0:T(8,128)S(1)}, f32[144,12...) custom-call(s32[32]{0:T(128)} %cell_hbm.1, ...), custom_call_target="tpu_custom_call" | custom-call | tf_op jit(solution)/shard_map/forecast/pallas_call | solution.py:466
  4.0 0.0 collective-permute-start
  4.0 2.4 %collective-permute-start.1 = (f32[48,128]{1,0:T(8,128)S(1)}, f32[48,128]{1,0:T(8,128)S(1)}, u32[]{:S(2)}, u32[]{:S(2)}) collective-permute-start(f32[48,128]{1,0:T(8,128)S(1)} %get-tuple-element.20), channel_id=1, source_target_pairs={{0,2},{2,4},{4,6},{6,8},{8,10},{10,12},{12,14},{14,15},{15,13},{13... | collective-permute-start | bytes 73736 | tf_op jit(solution)/shard_map/ppermute | solution.py:486
  6.4 1.3 %flow.1 = (f32[2,960,128]{2,1,0:T(8,128)S(1)}, f32[192,128]{1,0:T(8,128)S(1)}) custom-call(bf16[2,24,32,256]{3,2,1,0:T(8,128)(2,1)} %flow_noise_hbm.3, f32[2,960,128]{2,1,0:T(8,128)S(1)} %get-tuple-element.16.depth_ref.depth_in, f32[2,960,128]{2,1,0:T(8,128)S(1)} %get-tuple-element.17.flow_in), custom_call_target="tpu_custom_call", output_to_operand_aliasing={{0}: (2, {})} | custom-call | tf_op jit(solution)/shard_map/flow/pallas_call | solution.py:478
  7.7 0.2 collective-permute-done.1.far_ref
  8.0 1.0 %collective-permute-done.arrived_ref = f32[176,128]{1,0:T(8,128)S(1)} collective-permute-done((f32[176,128]{1,0:T(8,128)S(1)}, f32[176,128]{1,0:T(8,128)S(1)}, u32[]{:S(2)}, u32[]{:S(2)}) %collective-permute-start) | collective-permute-done | bytes 90144 | tf_op jit(solution)/shard_map/ppermute | solution.py:485
  8.9 2.3 %collective-permute-start.2 = (f32[2,176,128]{2,1,0:T(8,128)S(1)}, f32[2,176,128]{2,1,0:T(8,128)S(1)}, u32[]{:S(2)}, u32[]{:S(2)}) collective-permute-start(f32[2,176,128]{2,1,0:T(8,128)S(1)} %join.1), channel_id=1, source_target_pairs={{0,1},{1,0},{2,3},{3,2},{4,5},{5,4},{6,7},{7,6},{8,9},{9,8},{10,11... | collective-permute-start | bytes 540680 | tf_op jit(solution)/shard_map/ppermute | solution.py:488
  11.2 0.5 %taper.1.tapers_ref = bf16[32,64,256]{2,1,0:T(8,128)(2,1)S(1)} custom-call(f32[2,176,128]{2,1,0:T(8,128)S(1)} %get-tuple-element.14.own_ref), custom_call_target="tpu_custom_call" | custom-call | tf_op jit(solution)/shard_map/taper/pallas_call | solution.py:489
  11.7 0.5 %collective-permute-done.2.joined_ref = f32[2,176,128]{2,1,0:T(8,128)S(1)} collective-permute-done((f32[2,176,128]{2,1,0:T(8,128)S(1)}, f32[2,176,128]{2,1,0:T(8,128)S(1)}, u32[]{:S(2)}, u32[]{:S(2)}) %collective-permute-start.2) | collective-permute-done | bytes 180256 | tf_op jit(solution)/shard_map/ppermute | solution.py:488
  12.2 1.9 %finish.1 = (f32[256,128]{1,0:T(8,128)S(1)}, f32[2,960,128]{2,1,0:T(8,128)S(1)}, f32[2,960,128]{2,1,0:T(8,128)S(1)}, f32[2,960,128]{2,1,0:T(8,128)S(1)}) custom-call(f32[2,176,128]{2,1,0:T(8,128)S(1)} %get-tuple-element.14.own_ref, bf16[32,64,256]{2,1,0:T(8,128)(2,1)S(1)} %taper.1.tapers_ref, ...), custom_call_target="tpu_custom_call", output_to_operand_aliasing={{1}: (7, {}), {2}: (8, {}), {3}: (9, {})} | custom-call | tf_op jit(solution)/shard_map/finish/pallas_call | solution.py:492
  14.2 18.4 %all_to_all.10 = f32[32,8,128]{2,1,0:T(8,128)S(1)} all-to-all(f32[32,8,128]{2,1,0:T(8,128)S(1)} %bitcast.11), channel_id=1, replica_groups={{320,336,352,368,384,400,416,432,448,464,480,496,0,16,32,48,64,80,96,11..., dimensions={0} | all-to-all | bytes 262144 | tf_op jit(solution)/shard_map/all_to_all | solution.py:501
  32.5 0.1 combine.1
  32.6 13.7 %all_to_all.11 = f32[32,8,128]{2,1,0:T(8,128)S(1)} all-to-all(f32[32,8,128]{2,1,0:T(8,128)S(1)} %bitcast.10), channel_id=1, replica_groups={{320,336,352,368,384,400,416,432,448,464,480,496,0,16,32,48,64,80,96,11..., dimensions={0} | all-to-all | bytes 262144 | tf_op jit(solution)/shard_map/all_to_all | solution.py:505
  46.3 0.7 %spread.1 = (f32[32,256]{1,0:T(8,128)}, f32[32,256]{1,0:T(8,128)}, f32[32,256]{1,0:T(8,128)}) custom-call(f32[256,128]{1,0:T(8,128)S(1)} %bitcast.8), custom_call_target="tpu_custom_call" | custom-call | tf_op jit(solution)/shard_map/spread/pallas_call | solution.py:509
  (1 shorter events, 0.0 us)
Async XLA Ops:
  4.0 4.9 %collective-permute-start = (f32[176,128]{1,0:T(8,128)S(1)}, f32[176,128]{1,0:T(8,128)S(1)}, u32[]{:S(2)}, u32[]{:S(2)}) collective-permute-start(f32[176,128]{1,0:T(8,128)S(1)} %get-tuple-element.19), channel_id=1, source_target_pairs={{2,0},{4,2},{6,4},{8,6},{10,8},{12,10},{14,12},{15,14},{13,15},{11... | collective-permute-start | bytes 270344 | tf_op jit(solution)/shard_map/ppermute | solution.py:485
  4.0 3.9 %collective-permute-start.1 = (f32[48,128]{1,0:T(8,128)S(1)}, f32[48,128]{1,0:T(8,128)S(1)}, u32[]{:S(2)}, u32[]{:S(2)}) collective-permute-start(f32[48,128]{1,0:T(8,128)S(1)} %get-tuple-element.20), channel_id=1, source_target_pairs={{0,2},{2,4},{4,6},{6,8},{8,10},{10,12},{12,14},{14,15},{15,13},{13... | collective-permute-start | bytes 73736 | tf_op jit(solution)/shard_map/ppermute | solution.py:486
  8.9 3.3 %collective-permute-start.2 = (f32[2,176,128]{2,1,0:T(8,128)S(1)}, f32[2,176,128]{2,1,0:T(8,128)S(1)}, u32[]{:S(2)}, u32[]{:S(2)}) collective-permute-start(f32[2,176,128]{2,1,0:T(8,128)S(1)} %join.1), channel_id=1, source_target_pairs={{0,1},{1,0},{2,3},{3,2},{4,5},{5,4},{6,7},{7,6},{8,9},{9,8},{10,11... | collective-permute-start | bytes 540680 | tf_op jit(solution)/shard_map/ppermute | solution.py:488

commit v10 on v9

--- a/solution.py
+++ b/solution.py
@@ -86,7 +86,7 @@
 def forecast_kernel(
     cell_hbm, cells_hbm, radius_hbm, observed_hbm, sigma_hbm,
     surface_hbm, discharge_hbm, storage_hbm, exchange_hbm, depth_noise_hbm, flow_noise_hbm,
-    own_ref, along_ref, across_ref, far_ref, extra_ref, depth_ref, flow_ref, stored_ref,
+    own_ref, along_ref, far_ref, extra_ref, depth_ref, flow_ref, stored_ref,
     surface_ref, discharge_ref, storage_ref, exchange_ref, depth_noise_ref, flow_noise_ref,
     first_ref, last_ref, cell_ref, cells_ref, radius_ref, observed_ref, sigma_ref, sems,
 ):
@@ -216,9 +216,7 @@
     for i in range(2):
         own_ref[i, SAMPLED:ACROSS] = sampled
         own_ref[i, ACROSS:MESSAGE] = facts
-    odd = (cell_ref[0] >> 13) & 1
-    along_ref[...] = own_ref[odd]
-    across_ref[0] = own_ref[1 - odd]
+    along_ref[...] = own_ref[(cell_ref[0] >> 13) & 1]
 
 
 def line(ref, row):
@@ -230,13 +228,20 @@
         ref[h, pl.ds(row, MEMBERS, stride=PITCH)] = values[h]
 
 
-def flow_kernel(flow_noise_hbm, depth_ref, flow_in, flow_ref, late_ref, flow_noise_ref, first_ref, last_ref, sems):
+def is_odd(strip):
+    return strip - 2.0 * jnp.floor(0.5 * strip) > 0.5
+
+
+def flow_kernel(
+    flow_noise_hbm, own_ref, depth_ref, flow_in, flow_ref, late_ref, across_ref, flow_noise_ref, first_ref, last_ref, sems
+):
     del flow_in
     copies = []
     for c in range(MEMBERS // CHUNK):
         some = pl.ds(c * CHUNK, CHUNK)
         copies.append(pltpu.make_async_copy(flow_noise_hbm.at[1, some], flow_noise_ref.at[some], sems.at[c]))
         copies[c].start()
+    across_ref[0] = jnp.where(is_odd(own_ref[0, ACROSS + 3 : ACROSS + 4, 0:1]), own_ref[0], own_ref[1])
     for slot, row in ((2, 1), (3, ROWS - 2)):
         put(late_ref, slot, each(lambda q: 1.0 / (1.0 + friction * jnp.abs(q)), line(flow_ref, row)))
     row = lax.broadcasted_iota(jnp.int32, (ROWS, LANES), 0)
@@ -257,51 +262,45 @@
     put(late_ref, 1, [last_ref[h, pl.ds(7, MEMBERS, stride=8)] for h in range(2)])
 
 
-def join_kernel(across_ref, arrived_ref, far_ref, late_ref, joined_ref):
-    del across_ref, far_ref, late_ref
+def join_kernel(across_ref, arrived_ref, far_ref, joined_ref):
+    del across_ref, far_ref
     joined_ref[1] = arrived_ref[...]
 
 
-def taper_rows(facts, at, offsets, strip, near_ref, taper_ref):
-    count = len(offsets)
-    entries = jnp.transpose(facts)
-    column_at = lax.broadcasted_iota(jnp.int32, (SENS, COLS), 1).astype(f32)
-    lines = []
-    for part, offset in enumerate(offsets):
-        entry = entries[at + part * SENS : at + (part + 1) * SENS]
-        gap = column_at - entry[:, 1:2]
-        squared = jnp.where(entry[:, 3:4] == strip + offset, entry[:, 2:3], 0.0)
-        near_ref[part] = squared - gap * gap
-        lines.append(jnp.broadcast_to(entry[:, 0:1] + offset * ROWS, (SENS, LANES)))
-
-    def at_row(r, carry):
-        here = r.astype(f32)
-        for part in range(count):
-            gap = here - lines[part]
-            gap = gap * gap
-            value = jnp.maximum(near_ref[part] - jnp.concatenate([gap, gap], axis=1), 0.0)
-            coarse = value.astype(bf16)
-            taper_ref[r, part * SENS : (part + 1) * SENS] = coarse
-            taper_ref[r, (count + part) * SENS : (count + part + 1) * SENS] = (value - coarse.astype(f32)).astype(bf16)
-        return carry
-
-    lax.fori_loop(0, ROWS, at_row, 0, unroll=4 // count)
+def taper_terms(entry, offset, strip):
+    gap = lax.broadcasted_iota(jnp.int32, (SENS, COLS), 1).astype(f32) - entry[:, 1:2]
+    squared = jnp.where(entry[:, 3:4] == strip + offset, entry[:, 2:3], 0.0)
+    return squared - gap * gap, jnp.broadcast_to(entry[:, 0:1] + offset * ROWS, (SENS, LANES))
+
+
+def taper_pieces(near, lines, here):
+    gap = here - lines
+    gap = gap * gap
+    value = jnp.maximum(near - jnp.concatenate([gap, gap], axis=1), 0.0)
+    coarse = value.astype(bf16)
+    return coarse, (value - coarse.astype(f32)).astype(bf16)
 
 
 def taper_kernel(own_ref, tapers_ref, near_ref):
     facts = own_ref[0, ACROSS:MESSAGE]
-    taper_rows(facts, 0, [0.0], facts[3:4, 0:1], near_ref, tapers_ref)
+    near_ref[...], lines = taper_terms(jnp.transpose(facts)[:SENS], 0.0, facts[3:4, 0:1])
+
+    def at_row(r, carry):
+        tapers_ref[r, :SENS], tapers_ref[r, SENS:] = taper_pieces(near_ref[...], lines, r.astype(f32))
+        return carry
+
+    lax.fori_loop(0, ROWS, at_row, 0, unroll=4)
 
 
 def finish_kernel(
     own_ref, tapers_ref, extra_ref, late_ref, arrived_ref, far_ref, joined_ref, depth_in, flow_in, stored_in,
     out_ref, depth_ref, flow_ref, stored_ref,
-    before_ref, after_ref, near_ref, taper_ref, weight_ref,
+    before_ref, after_ref, near_ref, weight_ref,
 ):
     del depth_in, flow_in, stored_in
     up_ref, down_ref = own_ref.at[0], own_ref.at[1]
     strip = own_ref[0, ACROSS + 3 : ACROSS + 4, 0:1]
-    odd = strip - 2.0 * jnp.floor(0.5 * strip) > 0.5
+    odd = is_odd(strip)
     before_ref[...] = jnp.where(odd, joined_ref[0], joined_ref[1])
     after_ref[...] = jnp.where(odd, joined_ref[1], joined_ref[0])
     has_before = before_ref[ACROSS + 3 : ACROSS + 4, 0:1] == strip - 1.0
@@ -376,10 +375,15 @@
         [jnp.where(group == 0, pieces, pltpu.roll(pieces, SENS, 1)), pltpu.roll(pieces, LANES - SENS, 1)], axis=1
     )[:, : 6 * SENS].astype(bf16)
 
-    taper_rows(facts, SENS, [-1.0, 1.0], strip, near_ref, taper_ref)
+    entries = jnp.transpose(facts)
+    lines = []
+    for part, offset in enumerate((-1.0, 1.0)):
+        near_ref[part], rows = taper_terms(entries[(part + 1) * SENS : (part + 2) * SENS], offset, strip)
+        lines.append(rows)
     for i in range(ROWS // 8):
         for r in range(8 * i, 8 * i + 8):
-            tapers = jnp.concatenate([tapers_ref[r], taper_ref[r]], axis=0)
+            fringe = [taper_pieces(near_ref[part], lines[part], float(r)) for part in range(2)]
+            tapers = jnp.concatenate([tapers_ref[r]] + [piece for pieced in zip(*fringe) for piece in pieced], axis=0)
             part = jnp.dot(pieces, tapers, preferred_element_type=f32)
             weight = part[:MEMBERS] + part[MEMBERS : 2 * MEMBERS] + part[2 * MEMBERS :]
             for half in range(2):
@@ -463,9 +467,9 @@
     message = (MESSAGE, LANES)
     edges = lambda count: ((2 * count * MEMBERS, LANES), f32)
     row_of = lambda dtype: pltpu.VMEM((1, SENS), dtype)
-    own, along, across, far, extra, depth, flow, stored = call(
+    own, along, far, extra, depth, flow, stored = call(
         forecast_kernel, "forecast", [HBM] * 11,
-        [((2,) + message, f32), (message, f32), ((2,) + message, f32), edges(1), edges(3), grid, grid, grid],
+        [((2,) + message, f32), (message, f32), edges(1), edges(3), grid, grid, grid],
         [pltpu.VMEM(field.shape, field.dtype) for field in fields[:-1]]
         + [
             pltpu.VMEM(fields[0].shape, bf16),
@@ -475,25 +479,25 @@
         ],
     )(stay(sensor_cell), as_row(sensor_cell), as_row(sensor_radius), as_row(observed), as_row(sensor_sigma), *fields)
     strip_edges = pltpu.VMEM((2, MEMBERS * 8, LANES), f32)
-    flow, late = call(
-        flow_kernel, "flow", [HBM] + [VMEM] * 2, [grid, edges(4)],
+    flow, late, across = call(
+        flow_kernel, "flow", [HBM] + [VMEM] * 3, [grid, edges(4), ((2,) + message, f32)],
         [
             pltpu.VMEM(fields[0].shape, bf16), strip_edges, strip_edges, pltpu.SemaphoreType.DMA((MEMBERS // CHUNK,)),
         ],
-        aliases={2: 0},
-    )(fields[-1], depth, flow)
+        aliases={3: 0},
+    )(fields[-1], own, depth, flow)
     arrived = lax.ppermute(along, "strip", backward)
     far = lax.ppermute(far, "strip", onward)
-    (joined,) = call(join_kernel, "join", [VMEM] * 4, [((2,) + message, f32)], aliases={0: 0})(across, arrived, far, late)
+    (joined,) = call(join_kernel, "join", [VMEM] * 3, [((2,) + message, f32)], aliases={0: 0})(across, arrived, far)
     joined = lax.ppermute(joined, "strip", swapped)
     (tapers,) = call(
-        taper_kernel, "taper", [VMEM], [((ROWS, 2 * SENS, COLS), bf16)], [pltpu.VMEM((1, SENS, COLS), f32)],
+        taper_kernel, "taper", [VMEM], [((ROWS, 2 * SENS, COLS), bf16)], [pltpu.VMEM((SENS, COLS), f32)],
     )(own)
     parts, depth, flow, stored = call(
         finish_kernel, "finish", [VMEM] * 10, [((groups * 8, LANES), f32), grid, grid, grid],
         [
             pltpu.VMEM(message, f32), pltpu.VMEM(message, f32), pltpu.VMEM((2, SENS, COLS), f32),
-            pltpu.VMEM((ROWS, 4 * SENS, COLS), bf16), pltpu.VMEM((2, ROWS * MEMBERS, LANES), f32),
+ pltpu.VMEM((2, ROWS * MEMBERS, LANES), f32),
         ],
         aliases={7: 1, 8: 2, 9: 3},
     )(own, tapers, extra, late, arrived, far, joined, depth, flow, stored)

time: 47.2 us -> 46.8 us (level)
  no operation moved by 1% of the time
where the time goes in v10:
time: 46.8 us; the launch traced here: 46.6 us
  blocking collectives  32.1 us (69%)
  Pallas kernels  7.39 us (16%)
  starting transfers between devices  4.68 us (10%)
  waiting for transfers between devices  1.72 us (4%)
  between operations  0.69 us (1%)
    all_to_all x1, blocking collectives, local(): lax.all_to_all(parts.reshape(groups, 8, LANES), 'dom', 0, 0, tiled=True,...  18.4 us
    all_to_all x1, blocking collectives, local(): lax.all_to_all(rows.reshape(groups, 8, LANES), 'dom', 0, 0, tiled=True, a...  13.7 us
    pallas_call x1, Pallas kernels, local(): call(forecast_kernel, 'forecast', [HBM] * 11, [((2,) + message, f32), (me...  3.37 us
    ppermute x1, starting transfers between devices, local(): far = lax.ppermute(far, 'strip', onward)  2.39 us
    ppermute x1, starting transfers between devices, local(): joined = lax.ppermute(joined, 'strip', swapped)  2.27 us
    pallas_call x1, Pallas kernels, local(): call(finish_kernel, 'finish', [VMEM] * 10, [((groups * 8, LANES), f32), g...  1.53 us
    pallas_call x1, Pallas kernels, local(): call(flow_kernel, 'flow', [HBM] + [VMEM] * 3, [grid, edges(4), ((2,) + me...  1.3 us
    ppermute x1, waiting for transfers between devices, local(): arrived = lax.ppermute(along, 'strip', backward)  0.96 us
  transfers between devices with their start and end apart: 3, of which 3 were waited for; matrix products, arithmetic and copies ran while one was open for 0% of the time, Pallas kernels for 4%

profile of v10, /device:TPU:8, one launch (start us, length us, event | category | flops | bytes accessed | tf_op | source)
XLA Modules:
  0.0 46.6 jit_solution(4864452924595617953)
XLA Ops:
  0.6 3.4 %forecast.1 = (f32[2,176,128]{2,1,0:T(8,128)S(1)}, f32[176,128]{1,0:T(8,128)S(1)}, f32[48,128]{1,0:T(8,128)S(1)}, f32[144,128]{1,0:T(8,128)S(1)}, f32[2,960,128]...) custom-call(s32[32]{0:T(128)} %cell_hbm.1, s32[1,32]{1,0:T(1,128)} %bitcast.12, ...), custom_call_target="tpu_custom_call" | custom-call | tf_op jit(solution)/shard_map/forecast/pallas_call | solution.py:470
  4.0 0.0 collective-permute-start
  4.0 2.4 %collective-permute-start.1 = (f32[48,128]{1,0:T(8,128)S(1)}, f32[48,128]{1,0:T(8,128)S(1)}, u32[]{:S(2)}, u32[]{:S(2)}) collective-permute-start(f32[48,128]{1,0:T(8,128)S(1)} %get-tuple-element.20), channel_id=1, source_target_pairs={{0,2},{2,4},{4,6},{6,8},{8,10},{10,12},{12,14},{14,15},{15,13},{13... | collective-permute-start | bytes 73736 | tf_op jit(solution)/shard_map/ppermute | solution.py:490
  6.4 1.3 %flow.1 = (f32[2,960,128]{2,1,0:T(8,128)S(1)}, f32[192,128]{1,0:T(8,128)S(1)}, f32[2,176,128]{2,1,0:T(8,128)S(1)}) custom-call(bf16[2,24,32,256]{3,2,1,0:T(8,128)(2,1)} %flow_noise_hbm.3, f32[2,176,128]{2,1,0:T(8,128)S(1)} %get-tuple-element.14.own_ref, f32[2,960,128]{2,1,0:T(8,128)S(1)} %get-tuple-element.16.depth_ref.depth_in, ...), custom_call_target="tpu_custom_call", output_to_operand_aliasing={{0}: (3, {})} | custom-call | tf_op jit(solution)/shard_map/flow/pallas_call | solution.py:482
  7.7 0.2 collective-permute-done.1.far_ref
  7.9 1.0 %collective-permute-done.arrived_ref = f32[176,128]{1,0:T(8,128)S(1)} collective-permute-done((f32[176,128]{1,0:T(8,128)S(1)}, f32[176,128]{1,0:T(8,128)S(1)}, u32[]{:S(2)}, u32[]{:S(2)}) %collective-permute-start) | collective-permute-done | bytes 90144 | tf_op jit(solution)/shard_map/ppermute | solution.py:489
  8.9 2.3 %collective-permute-start.2 = (f32[2,176,128]{2,1,0:T(8,128)S(1)}, f32[2,176,128]{2,1,0:T(8,128)S(1)}, u32[]{:S(2)}, u32[]{:S(2)}) collective-permute-start(f32[2,176,128]{2,1,0:T(8,128)S(1)} %join.1), channel_id=1, source_target_pairs={{0,1},{1,0},{2,3},{3,2},{4,5},{5,4},{6,7},{7,6},{8,9},{9,8},{10,11... | collective-permute-start | bytes 540680 | tf_op jit(solution)/shard_map/ppermute | solution.py:492
  11.2 0.5 %taper.1.tapers_ref = bf16[32,64,256]{2,1,0:T(8,128)(2,1)S(1)} custom-call(f32[2,176,128]{2,1,0:T(8,128)S(1)} %get-tuple-element.14.own_ref), custom_call_target="tpu_custom_call" | custom-call | tf_op jit(solution)/shard_map/taper/pallas_call | solution.py:493
  11.7 0.5 %collective-permute-done.2.joined_ref = f32[2,176,128]{2,1,0:T(8,128)S(1)} collective-permute-done((f32[2,176,128]{2,1,0:T(8,128)S(1)}, f32[2,176,128]{2,1,0:T(8,128)S(1)}, u32[]{:S(2)}, u32[]{:S(2)}) %collective-permute-start.2) | collective-permute-done | bytes 180256 | tf_op jit(solution)/shard_map/ppermute | solution.py:492
  12.2 1.5 %finish.1 = (f32[256,128]{1,0:T(8,128)S(1)}, f32[2,960,128]{2,1,0:T(8,128)S(1)}, f32[2,960,128]{2,1,0:T(8,128)S(1)}, f32[2,960,128]{2,1,0:T(8,128)S(1)}) custom-call(f32[2,176,128]{2,1,0:T(8,128)S(1)} %get-tuple-element.14.own_ref, bf16[32,64,256]{2,1,0:T(8,128)(2,1)S(1)} %taper.1.tapers_ref, ...), custom_call_target="tpu_custom_call", output_to_operand_aliasing={{1}: (7, {}), {2}: (8, {}), {3}: (9, {})} | custom-call | tf_op jit(solution)/shard_map/finish/pallas_call | solution.py:496
  13.8 18.4 %all_to_all.10 = f32[32,8,128]{2,1,0:T(8,128)S(1)} all-to-all(f32[32,8,128]{2,1,0:T(8,128)S(1)} %bitcast.11), channel_id=1, replica_groups={{320,336,352,368,384,400,416,432,448,464,480,496,0,16,32,48,64,80,96,11..., dimensions={0} | all-to-all | bytes 262144 | tf_op jit(solution)/shard_map/all_to_all | solution.py:505
  32.1 0.1 combine.1
  32.2 13.7 %all_to_all.11 = f32[32,8,128]{2,1,0:T(8,128)S(1)} all-to-all(f32[32,8,128]{2,1,0:T(8,128)S(1)} %bitcast.10), channel_id=1, replica_groups={{320,336,352,368,384,400,416,432,448,464,480,496,0,16,32,48,64,80,96,11..., dimensions={0} | all-to-all | bytes 262144 | tf_op jit(solution)/shard_map/all_to_all | solution.py:509
  45.9 0.7 %spread.1 = (f32[32,256]{1,0:T(8,128)}, f32[32,256]{1,0:T(8,128)}, f32[32,256]{1,0:T(8,128)}) custom-call(f32[256,128]{1,0:T(8,128)S(1)} %bitcast.8), custom_call_target="tpu_custom_call" | custom-call | tf_op jit(solution)/shard_map/spread/pallas_call | solution.py:513
  (1 shorter events, 0.0 us)
Async XLA Ops:
  4.0 4.9 %collective-permute-start = (f32[176,128]{1,0:T(8,128)S(1)}, f32[176,128]{1,0:T(8,128)S(1)}, u32[]{:S(2)}, u32[]{:S(2)}) collective-permute-start(f32[176,128]{1,0:T(8,128)S(1)} %get-tuple-element.19), channel_id=1, source_target_pairs={{2,0},{4,2},{6,4},{8,6},{10,8},{12,10},{14,12},{15,14},{13,15},{11... | collective-permute-start | bytes 270344 | tf_op jit(solution)/shard_map/ppermute | solution.py:489
  4.0 3.9 %collective-permute-start.1 = (f32[48,128]{1,0:T(8,128)S(1)}, f32[48,128]{1,0:T(8,128)S(1)}, u32[]{:S(2)}, u32[]{:S(2)}) collective-permute-start(f32[48,128]{1,0:T(8,128)S(1)} %get-tuple-element.20), channel_id=1, source_target_pairs={{0,2},{2,4},{4,6},{6,8},{8,10},{10,12},{12,14},{14,15},{15,13},{13... | collective-permute-start | bytes 73736 | tf_op jit(solution)/shard_map/ppermute | solution.py:490
  8.9 3.3 %collective-permute-start.2 = (f32[2,176,128]{2,1,0:T(8,128)S(1)}, f32[2,176,128]{2,1,0:T(8,128)S(1)}, u32[]{:S(2)}, u32[]{:S(2)}) collective-permute-start(f32[2,176,128]{2,1,0:T(8,128)S(1)} %join.1), channel_id=1, source_target_pairs={{0,1},{1,0},{2,3},{3,2},{4,5},{5,4},{6,7},{7,6},{8,9},{9,8},{10,11... | collective-permute-start | bytes 540680 | tf_op jit(solution)/shard_map/ppermute | solution.py:492

commit v11 on v10

--- a/solution.py
+++ b/solution.py
@@ -463,7 +463,7 @@
     stay = lambda values: pltpu.with_memory_space_constraint(values, pltpu.HBM)
     as_row = lambda values: stay(values.reshape(1, SENS))
     fields = [stay(f) for f in (surface, discharge, storage, exchange, depth_perturbation, flow_perturbation)]
-    grid = ((2, MEMBERS * PITCH, LANES), f32)
+    grid = ((2, MEMBERS * PITCH + ROWS, LANES), f32)
     message = (MESSAGE, LANES)
     edges = lambda count: ((2 * count * MEMBERS, LANES), f32)
     row_of = lambda dtype: pltpu.VMEM((1, SENS), dtype)

time: 46.8 us -> 46.8 us (level)
  no operation moved by 1% of the time
where the time goes in v11:
time: 46.8 us; the launch traced here: 46.6 us
  blocking collectives  32.1 us (69%)
  Pallas kernels  7.39 us (16%)
  starting transfers between devices  4.68 us (10%)
  waiting for transfers between devices  1.72 us (4%)
  between operations  0.69 us (1%)
    all_to_all x1, blocking collectives, local(): lax.all_to_all(parts.reshape(groups, 8, LANES), 'dom', 0, 0, tiled=True,...  18.4 us
    all_to_all x1, blocking collectives, local(): lax.all_to_all(rows.reshape(groups, 8, LANES), 'dom', 0, 0, tiled=True, a...  13.7 us
    pallas_call x1, Pallas kernels, local(): call(forecast_kernel, 'forecast', [HBM] * 11, [((2,) + message, f32), (me...  3.37 us
    ppermute x1, starting transfers between devices, local(): far = lax.ppermute(far, 'strip', onward)  2.39 us
    ppermute x1, starting transfers between devices, local(): joined = lax.ppermute(joined, 'strip', swapped)  2.27 us
    pallas_call x1, Pallas kernels, local(): call(finish_kernel, 'finish', [VMEM] * 10, [((groups * 8, LANES), f32), g...  1.53 us
    pallas_call x1, Pallas kernels, local(): call(flow_kernel, 'flow', [HBM] + [VMEM] * 3, [grid, edges(4), ((2,) + me...  1.3 us
    ppermute x1, waiting for transfers between devices, local(): arrived = lax.ppermute(along, 'strip', backward)  0.96 us
  transfers between devices with their start and end apart: 3, of which 3 were waited for; matrix products, arithmetic and copies ran while one was open for 0% of the time, Pallas kernels for 4%

profile of v11, /device:TPU:8, one launch (start us, length us, event | category | flops | bytes accessed | tf_op | source)
XLA Modules:
  0.0 46.6 jit_solution(11477719149342142628)
XLA Ops:
  0.6 3.4 %forecast.1 = (f32[2,176,128]{2,1,0:T(8,128)S(1)}, f32[176,128]{1,0:T(8,128)S(1)}, f32[48,128]{1,0:T(8,128)S(1)}, f32[144,128]{1,0:T(8,128)S(1)}, f32[2,992,128]...) custom-call(s32[32]{0:T(128)} %cell_hbm.1, s32[1,32]{1,0:T(1,128)} %bitcast.12, ...), custom_call_target="tpu_custom_call" | custom-call | tf_op jit(solution)/shard_map/forecast/pallas_call | solution.py:470
  4.0 0.0 collective-permute-start
  4.0 2.4 %collective-permute-start.1 = (f32[48,128]{1,0:T(8,128)S(1)}, f32[48,128]{1,0:T(8,128)S(1)}, u32[]{:S(2)}, u32[]{:S(2)}) collective-permute-start(f32[48,128]{1,0:T(8,128)S(1)} %get-tuple-element.20), channel_id=1, source_target_pairs={{0,2},{2,4},{4,6},{6,8},{8,10},{10,12},{12,14},{14,15},{15,13},{13... | collective-permute-start | bytes 73736 | tf_op jit(solution)/shard_map/ppermute | solution.py:490
  6.4 1.3 %flow.1 = (f32[2,992,128]{2,1,0:T(8,128)S(1)}, f32[192,128]{1,0:T(8,128)S(1)}, f32[2,176,128]{2,1,0:T(8,128)S(1)}) custom-call(bf16[2,24,32,256]{3,2,1,0:T(8,128)(2,1)} %flow_noise_hbm.3, f32[2,176,128]{2,1,0:T(8,128)S(1)} %get-tuple-element.14.own_ref, f32[2,992,128]{2,1,0:T(8,128)S(1)} %get-tuple-element.16.depth_ref.depth_in, ...), custom_call_target="tpu_custom_call", output_to_operand_aliasing={{0}: (3, {})} | custom-call | tf_op jit(solution)/shard_map/flow/pallas_call | solution.py:482
  7.7 0.2 collective-permute-done.1.far_ref
  7.9 1.0 %collective-permute-done.arrived_ref = f32[176,128]{1,0:T(8,128)S(1)} collective-permute-done((f32[176,128]{1,0:T(8,128)S(1)}, f32[176,128]{1,0:T(8,128)S(1)}, u32[]{:S(2)}, u32[]{:S(2)}) %collective-permute-start) | collective-permute-done | bytes 90144 | tf_op jit(solution)/shard_map/ppermute | solution.py:489
  8.9 2.3 %collective-permute-start.2 = (f32[2,176,128]{2,1,0:T(8,128)S(1)}, f32[2,176,128]{2,1,0:T(8,128)S(1)}, u32[]{:S(2)}, u32[]{:S(2)}) collective-permute-start(f32[2,176,128]{2,1,0:T(8,128)S(1)} %join.1), channel_id=1, source_target_pairs={{0,1},{1,0},{2,3},{3,2},{4,5},{5,4},{6,7},{7,6},{8,9},{9,8},{10,11... | collective-permute-start | bytes 540680 | tf_op jit(solution)/shard_map/ppermute | solution.py:492
  11.2 0.5 %taper.1.tapers_ref = bf16[32,64,256]{2,1,0:T(8,128)(2,1)S(1)} custom-call(f32[2,176,128]{2,1,0:T(8,128)S(1)} %get-tuple-element.14.own_ref), custom_call_target="tpu_custom_call" | custom-call | tf_op jit(solution)/shard_map/taper/pallas_call | solution.py:493
  11.7 0.5 %collective-permute-done.2.joined_ref = f32[2,176,128]{2,1,0:T(8,128)S(1)} collective-permute-done((f32[2,176,128]{2,1,0:T(8,128)S(1)}, f32[2,176,128]{2,1,0:T(8,128)S(1)}, u32[]{:S(2)}, u32[]{:S(2)}) %collective-permute-start.2) | collective-permute-done | bytes 180256 | tf_op jit(solution)/shard_map/ppermute | solution.py:492
  12.2 1.5 %finish.1 = (f32[256,128]{1,0:T(8,128)S(1)}, f32[2,992,128]{2,1,0:T(8,128)S(1)}, f32[2,992,128]{2,1,0:T(8,128)S(1)}, f32[2,992,128]{2,1,0:T(8,128)S(1)}) custom-call(f32[2,176,128]{2,1,0:T(8,128)S(1)} %get-tuple-element.14.own_ref, bf16[32,64,256]{2,1,0:T(8,128)(2,1)S(1)} %taper.1.tapers_ref, ...), custom_call_target="tpu_custom_call", output_to_operand_aliasing={{1}: (7, {}), {2}: (8, {}), {3}: (9, {})} | custom-call | tf_op jit(solution)/shard_map/finish/pallas_call | solution.py:496
  13.8 18.4 %all_to_all.10 = f32[32,8,128]{2,1,0:T(8,128)S(1)} all-to-all(f32[32,8,128]{2,1,0:T(8,128)S(1)} %bitcast.11), channel_id=1, replica_groups={{320,336,352,368,384,400,416,432,448,464,480,496,0,16,32,48,64,80,96,11..., dimensions={0} | all-to-all | bytes 262144 | tf_op jit(solution)/shard_map/all_to_all | solution.py:505
  32.1 0.1 combine.1
  32.2 13.7 %all_to_all.11 = f32[32,8,128]{2,1,0:T(8,128)S(1)} all-to-all(f32[32,8,128]{2,1,0:T(8,128)S(1)} %bitcast.10), channel_id=1, replica_groups={{320,336,352,368,384,400,416,432,448,464,480,496,0,16,32,48,64,80,96,11..., dimensions={0} | all-to-all | bytes 262144 | tf_op jit(solution)/shard_map/all_to_all | solution.py:509
  45.9 0.7 %spread.1 = (f32[32,256]{1,0:T(8,128)}, f32[32,256]{1,0:T(8,128)}, f32[32,256]{1,0:T(8,128)}) custom-call(f32[256,128]{1,0:T(8,128)S(1)} %bitcast.8), custom_call_target="tpu_custom_call" | custom-call | tf_op jit(solution)/shard_map/spread/pallas_call | solution.py:513
  (1 shorter events, 0.0 us)
Async XLA Ops:
  4.0 4.9 %collective-permute-start = (f32[176,128]{1,0:T(8,128)S(1)}, f32[176,128]{1,0:T(8,128)S(1)}, u32[]{:S(2)}, u32[]{:S(2)}) collective-permute-start(f32[176,128]{1,0:T(8,128)S(1)} %get-tuple-element.19), channel_id=1, source_target_pairs={{2,0},{4,2},{6,4},{8,6},{10,8},{12,10},{14,12},{15,14},{13,15},{11... | collective-permute-start | bytes 270344 | tf_op jit(solution)/shard_map/ppermute | solution.py:489
  4.0 3.9 %collective-permute-start.1 = (f32[48,128]{1,0:T(8,128)S(1)}, f32[48,128]{1,0:T(8,128)S(1)}, u32[]{:S(2)}, u32[]{:S(2)}) collective-permute-start(f32[48,128]{1,0:T(8,128)S(1)} %get-tuple-element.20), channel_id=1, source_target_pairs={{0,2},{2,4},{4,6},{6,8},{8,10},{10,12},{12,14},{14,15},{15,13},{13... | collective-permute-start | bytes 73736 | tf_op jit(solution)/shard_map/ppermute | solution.py:490
  8.9 3.3 %collective-permute-start.2 = (f32[2,176,128]{2,1,0:T(8,128)S(1)}, f32[2,176,128]{2,1,0:T(8,128)S(1)}, u32[]{:S(2)}, u32[]{:S(2)}) collective-permute-start(f32[2,176,128]{2,1,0:T(8,128)S(1)} %join.1), channel_id=1, source_target_pairs={{0,1},{1,0},{2,3},{3,2},{4,5},{5,4},{6,7},{7,6},{8,9},{9,8},{10,11... | collective-permute-start | bytes 540680 | tf_op jit(solution)/shard_map/ppermute | solution.py:492

commit v12 on v11

--- a/solution.py
+++ b/solution.py
@@ -295,14 +295,14 @@
 def finish_kernel(
     own_ref, tapers_ref, extra_ref, late_ref, arrived_ref, far_ref, joined_ref, depth_in, flow_in, stored_in,
     out_ref, depth_ref, flow_ref, stored_ref,
-    before_ref, after_ref, near_ref, weight_ref,
+    near_ref, weight_ref,
 ):
     del depth_in, flow_in, stored_in
     up_ref, down_ref = own_ref.at[0], own_ref.at[1]
     strip = own_ref[0, ACROSS + 3 : ACROSS + 4, 0:1]
     odd = is_odd(strip)
-    before_ref[...] = jnp.where(odd, joined_ref[0], joined_ref[1])
-    after_ref[...] = jnp.where(odd, joined_ref[1], joined_ref[0])
+    parity = lax.axis_index("strip") & 1
+    before_ref, after_ref = joined_ref.at[1 - parity], joined_ref.at[parity]
     has_before = before_ref[ACROSS + 3 : ACROSS + 4, 0:1] == strip - 1.0
     has_after = after_ref[ACROSS + 3 : ACROSS + 4, 0:1] == strip + 1.0
     keep = lambda condition, row: each(lambda v: jnp.where(condition, v, 0.0), row)
@@ -496,12 +496,14 @@
     parts, depth, flow, stored = call(
         finish_kernel, "finish", [VMEM] * 10, [((groups * 8, LANES), f32), grid, grid, grid],
         [
-            pltpu.VMEM(message, f32), pltpu.VMEM(message, f32), pltpu.VMEM((2, SENS, COLS), f32),
+            pltpu.VMEM((2, SENS, COLS), f32),
  pltpu.VMEM((2, ROWS * MEMBERS, LANES), f32),
         ],
         aliases={7: 1, 8: 2, 9: 3},
     )(own, tapers, extra, late, arrived, far, joined, depth, flow, stored)
-    turned = [(20 + i) % groups for i in range(groups)]
+    winding = [8 * x + (7 - y if x % 2 else y) for x in range(groups // 8) for y in range(8)]
+    start = winding.index(20)
+    turned = winding[start:] + winding[:start]
     shared = lax.all_to_all(parts.reshape(groups, 8, LANES), "dom", 0, 0, tiled=True, axis_index_groups=[turned])
     (rows,) = call(
         lambda *refs: combine_kernel(groups, *refs), "combine", [VMEM], [((groups * 8, LANES), f32)],

time: 46.8 us -> 46.8 us (level)
  the two profiles are of different devices: /device:TPU:8 before, /device:TPU:2 now
where the time goes in v12:
time: 46.8 us; the launch traced here: 46.5 us
  blocking collectives  32.1 us (69%)
  Pallas kernels  7.37 us (16%)
  starting transfers between devices  4.68 us (10%)
  waiting for transfers between devices  1.72 us (4%)
  between operations  0.69 us (1%)
    all_to_all x1, blocking collectives, local(): lax.all_to_all(parts.reshape(groups, 8, LANES), 'dom', 0, 0, tiled=True,...  18.4 us
    all_to_all x1, blocking collectives, local(): lax.all_to_all(rows.reshape(groups, 8, LANES), 'dom', 0, 0, tiled=True, a...  13.7 us
    pallas_call x1, Pallas kernels, local(): call(forecast_kernel, 'forecast', [HBM] * 11, [((2,) + message, f32), (me...  3.37 us
    ppermute x1, starting transfers between devices, local(): far = lax.ppermute(far, 'strip', onward)  2.39 us
    ppermute x1, starting transfers between devices, local(): joined = lax.ppermute(joined, 'strip', swapped)  2.27 us
    pallas_call x1, Pallas kernels, local(): call(finish_kernel, 'finish', [VMEM] * 10, [((groups * 8, LANES), f32), g...  1.51 us
    pallas_call x1, Pallas kernels, local(): call(flow_kernel, 'flow', [HBM] + [VMEM] * 3, [grid, edges(4), ((2,) + me...  1.3 us
    ppermute x1, waiting for transfers between devices, local(): arrived = lax.ppermute(along, 'strip', backward)  0.96 us
  transfers between devices with their start and end apart: 3, of which 3 were waited for; matrix products, arithmetic and copies ran while one was open for 0% of the time, Pallas kernels for 4%

profile of v12, /device:TPU:2, one launch (start us, length us, event | category | flops | bytes accessed | tf_op | source)
XLA Modules:
  0.0 46.5 jit_solution(8503944459117135800)
XLA Ops:
  0.6 3.4 %forecast.1 = (f32[2,176,128]{2,1,0:T(8,128)S(1)}, f32[176,128]{1,0:T(8,128)S(1)}, f32[48,128]{1,0:T(8,128)S(1)}, f32[144,128]{1,0:T(8,128)S(1)}, f32[2,992,128]...) custom-call(s32[32]{0:T(128)} %cell_hbm.1, s32[1,32]{1,0:T(1,128)} %bitcast.12, ...), custom_call_target="tpu_custom_call" | custom-call | tf_op jit(solution)/shard_map/forecast/pallas_call | solution.py:470
  4.0 0.0 collective-permute-start
  4.0 2.4 %collective-permute-start.1 = (f32[48,128]{1,0:T(8,128)S(1)}, f32[48,128]{1,0:T(8,128)S(1)}, u32[]{:S(2)}, u32[]{:S(2)}) collective-permute-start(f32[48,128]{1,0:T(8,128)S(1)} %get-tuple-element.20), channel_id=1, source_target_pairs={{0,2},{2,4},{4,6},{6,8},{8,10},{10,12},{12,14},{14,15},{15,13},{13... | collective-permute-start | bytes 73736 | tf_op jit(solution)/shard_map/ppermute | solution.py:490
  6.4 1.3 %flow.1 = (f32[2,992,128]{2,1,0:T(8,128)S(1)}, f32[192,128]{1,0:T(8,128)S(1)}, f32[2,176,128]{2,1,0:T(8,128)S(1)}) custom-call(bf16[2,24,32,256]{3,2,1,0:T(8,128)(2,1)} %flow_noise_hbm.3, f32[2,176,128]{2,1,0:T(8,128)S(1)} %get-tuple-element.14.own_ref, f32[2,992,128]{2,1,0:T(8,128)S(1)} %get-tuple-element.16.depth_ref.depth_in, ...), custom_call_target="tpu_custom_call", output_to_operand_aliasing={{0}: (3, {})} | custom-call | tf_op jit(solution)/shard_map/flow/pallas_call | solution.py:482
  7.7 0.2 collective-permute-done.1.far_ref
  7.9 1.0 %collective-permute-done.arrived_ref = f32[176,128]{1,0:T(8,128)S(1)} collective-permute-done((f32[176,128]{1,0:T(8,128)S(1)}, f32[176,128]{1,0:T(8,128)S(1)}, u32[]{:S(2)}, u32[]{:S(2)}) %collective-permute-start) | collective-permute-done | bytes 90144 | tf_op jit(solution)/shard_map/ppermute | solution.py:489
  8.9 2.3 %collective-permute-start.2 = (f32[2,176,128]{2,1,0:T(8,128)S(1)}, f32[2,176,128]{2,1,0:T(8,128)S(1)}, u32[]{:S(2)}, u32[]{:S(2)}) collective-permute-start(f32[2,176,128]{2,1,0:T(8,128)S(1)} %join.1), channel_id=1, source_target_pairs={{0,1},{1,0},{2,3},{3,2},{4,5},{5,4},{6,7},{7,6},{8,9},{9,8},{10,11... | collective-permute-start | bytes 540680 | tf_op jit(solution)/shard_map/ppermute | solution.py:492
  11.2 0.5 %taper.1.tapers_ref = bf16[32,64,256]{2,1,0:T(8,128)(2,1)S(1)} custom-call(f32[2,176,128]{2,1,0:T(8,128)S(1)} %get-tuple-element.14.own_ref), custom_call_target="tpu_custom_call" | custom-call | tf_op jit(solution)/shard_map/taper/pallas_call | solution.py:493
  11.7 0.5 %collective-permute-done.2.joined_ref = f32[2,176,128]{2,1,0:T(8,128)S(1)} collective-permute-done((f32[2,176,128]{2,1,0:T(8,128)S(1)}, f32[2,176,128]{2,1,0:T(8,128)S(1)}, u32[]{:S(2)}, u32[]{:S(2)}) %collective-permute-start.2) | collective-permute-done | bytes 180256 | tf_op jit(solution)/shard_map/ppermute | solution.py:492
  12.2 1.5 %finish.1 = (f32[256,128]{1,0:T(8,128)S(1)}, f32[2,992,128]{2,1,0:T(8,128)S(1)}, f32[2,992,128]{2,1,0:T(8,128)S(1)}, f32[2,992,128]{2,1,0:T(8,128)S(1)}) custom-call(f32[2,176,128]{2,1,0:T(8,128)S(1)} %get-tuple-element.14.own_ref, bf16[32,64,256]{2,1,0:T(8,128)(2,1)S(1)} %taper.1.tapers_ref, ...), custom_call_target="tpu_custom_call", output_to_operand_aliasing={{1}: (7, {}), {2}: (8, {}), {3}: (9, {})} | custom-call | tf_op jit(solution)/shard_map/finish/pallas_call | solution.py:496
  13.7 18.4 %all_to_all.10 = f32[32,8,128]{2,1,0:T(8,128)S(1)} all-to-all(f32[32,8,128]{2,1,0:T(8,128)S(1)} %bitcast.11), channel_id=1, replica_groups={{320,336,352,368,496,480,464,448,432,416,400,384,0,16,32,48,64,80,96,11..., dimensions={0} | all-to-all | bytes 262144 | tf_op jit(solution)/shard_map/all_to_all | solution.py:507
  32.2 0.1 combine.1
  32.2 13.7 %all_to_all.11 = f32[32,8,128]{2,1,0:T(8,128)S(1)} all-to-all(f32[32,8,128]{2,1,0:T(8,128)S(1)} %bitcast.10), channel_id=1, replica_groups={{320,336,352,368,496,480,464,448,432,416,400,384,0,16,32,48,64,80,96,11..., dimensions={0} | all-to-all | bytes 262144 | tf_op jit(solution)/shard_map/all_to_all | solution.py:511
  45.9 0.7 %spread.1 = (f32[32,256]{1,0:T(8,128)}, f32[32,256]{1,0:T(8,128)}, f32[32,256]{1,0:T(8,128)}) custom-call(f32[256,128]{1,0:T(8,128)S(1)} %bitcast.8), custom_call_target="tpu_custom_call" | custom-call | tf_op jit(solution)/shard_map/spread/pallas_call | solution.py:515
  (1 shorter events, 0.0 us)
Async XLA Ops:
  4.0 4.9 %collective-permute-start = (f32[176,128]{1,0:T(8,128)S(1)}, f32[176,128]{1,0:T(8,128)S(1)}, u32[]{:S(2)}, u32[]{:S(2)}) collective-permute-start(f32[176,128]{1,0:T(8,128)S(1)} %get-tuple-element.19), channel_id=1, source_target_pairs={{2,0},{4,2},{6,4},{8,6},{10,8},{12,10},{14,12},{15,14},{13,15},{11... | collective-permute-start | bytes 270344 | tf_op jit(solution)/shard_map/ppermute | solution.py:489
  4.0 3.9 %collective-permute-start.1 = (f32[48,128]{1,0:T(8,128)S(1)}, f32[48,128]{1,0:T(8,128)S(1)}, u32[]{:S(2)}, u32[]{:S(2)}) collective-permute-start(f32[48,128]{1,0:T(8,128)S(1)} %get-tuple-element.20), channel_id=1, source_target_pairs={{0,2},{2,4},{4,6},{6,8},{8,10},{10,12},{12,14},{14,15},{15,13},{13... | collective-permute-start | bytes 73736 | tf_op jit(solution)/shard_map/ppermute | solution.py:490
  8.9 3.3 %collective-permute-start.2 = (f32[2,176,128]{2,1,0:T(8,128)S(1)}, f32[2,176,128]{2,1,0:T(8,128)S(1)}, u32[]{:S(2)}, u32[]{:S(2)}) collective-permute-start(f32[2,176,128]{2,1,0:T(8,128)S(1)} %join.1), channel_id=1, source_target_pairs={{0,1},{1,0},{2,3},{3,2},{4,5},{5,4},{6,7},{7,6},{8,9},{9,8},{10,11... | collective-permute-start | bytes 540680 | tf_op jit(solution)/shard_map/ppermute | solution.py:492
